TPU v7x, 256 devices: a whole 4x4x8 slice. The times are simulated.
256 devices in a mesh: line: 16 (over z_hi, x, core), shot: 16 (over z_lo, y).
Axes of the slice: x: 4, y: 4, z: 8 (z_hi: 2, z_lo: 4; z = z_hi * 4 + z_lo), core: 2. Of those that a mesh axis runs over, the one named last changes fastest.
Arguments:
- velocity: float32 [256, 256, 128], P('line', 'shot'), may hold values from 1.5 to 4.5
- density: float32 [256, 256, 128], P('line', 'shot'), may hold values from 1 to 3
- start_pressure: float32 [512, 512, 128], P('line', 'shot'), may hold values from -6 to 6
- observed: float32 [512, 512, 128], P('line', 'shot'), may hold values from -6 to 6
- corners: int32 [16, 16, 2], P('line', 'shot'), may hold values from 0 to 224, as said below
Outputs:
- grad_velocity: float32 [256, 256, 128], P('line', 'shot')
- grad_density: float32 [256, 256, 128], P('line', 'shot')
Inputs may be any that keep to these rules, and one draw needn't show every extreme that they name: corners[a, b, 0] = min(max(a * 16 - 16 + r, 0), 224) and corners[a, b, 1] = min(max(b * 16 - 16 + t, 0), 224) for whole numbers r and t of 0 to 16.
All inputs are finite; a program needn't handle non-finite values.
Results may differ from a plain program's by a relative error of at most 0.0003.
Values sent between devices are 32-bit elements; how exact they have to be, the bound alone decides.
No kernel may reach another device: no remote copies, remote signals or barrier semaphores. Data moves between devices by JAX's collectives and lax.ppermute only.
A program may use at most 64 MiB of HBM per device.

v0:
```python
import jax
import jax.numpy as jnp
from jax import lax
from jax.sharding import PartitionSpec as P

coeffs = (1225.0 / 1024.0, -245.0 / 3072.0, 49.0 / 5120.0, -5.0 / 7168.0)
time_ratio = 0.1
wavelet = (20.0, -12.0)


def passed_along(block, axis, distance):
    devices = range(lax.axis_size(axis))
    route = [(i - distance, i) for i in devices if i - distance in devices]
    return lax.ppermute(block, axis, route)


def extended_2(cells, sides, width):
    for axis, dim in sides:
        count = lax.axis_size(axis)
        ends = count - 1
        head = lax.slice_in_dim(cells, 0, width, axis=dim)
        tail = lax.slice_in_dim(cells, cells.shape[dim] - width, cells.shape[dim], axis=dim)
        cells = jnp.concatenate(
            [
                lax.ppermute(tail, axis, [(i, (i + 1) % count) for i in range(ends)]),
                cells,
                lax.ppermute(head, axis, [((i + 1) % count, i) for i in range(ends)]),
            ],
            axis=dim,
        )
    return cells


def deriv_plus(field, axis):
    widths = [(0, 0)] * 3
    widths[axis] = (4, 4)
    padded = jnp.pad(field, widths)
    count = field.shape[axis]
    total = jnp.zeros_like(field)
    for m in range(1, 5):
        upper = lax.slice_in_dim(padded, 4 + m, 4 + m + count, axis=axis)
        lower = lax.slice_in_dim(padded, 5 - m, 5 - m + count, axis=axis)
        total = total + coeffs[m - 1] * (upper - lower)
    return total


def deriv_minus(field, axis):
    widths = [(0, 0)] * 3
    widths[axis] = (4, 4)
    padded = jnp.pad(field, widths)
    count = field.shape[axis]
    total = jnp.zeros_like(field)
    for m in range(1, 5):
        upper = lax.slice_in_dim(padded, 3 + m, 3 + m + count, axis=axis)
        lower = lax.slice_in_dim(padded, 4 - m, 4 - m + count, axis=axis)
        total = total + coeffs[m - 1] * (upper - lower)
    return total


def shot_misfit(model, pressure, observed):
    speed = model[0]
    dense = model[1]
    vel_x = jnp.zeros_like(pressure)
    vel_y = jnp.zeros_like(pressure)
    vel_z = jnp.zeros_like(pressure)
    centre = (pressure.shape[0] // 2, pressure.shape[1] // 2, pressure.shape[2] // 2)
    for level in range(2):
        vel_x = vel_x - time_ratio * deriv_plus(pressure, 0) / dense
        vel_y = vel_y - time_ratio * deriv_plus(pressure, 1) / dense
        vel_z = vel_z - time_ratio * deriv_plus(pressure, 2) / dense
        spread = deriv_minus(vel_x, 0) + deriv_minus(vel_y, 1) + deriv_minus(vel_z, 2)
        pressure = pressure - time_ratio * dense * speed * speed * spread
        pressure = pressure.at[centre].add(wavelet[level])
    misfit_term = pressure - observed
    return 0.5 * jnp.sum(misfit_term * misfit_term)


def return_line(terms, block):
    below = lax.slice_in_dim(terms, 0, block, axis=1)
    middle = lax.slice_in_dim(terms, block, 2 * block, axis=1)
    above = lax.slice_in_dim(terms, 2 * block, 3 * block, axis=1)
    from_prev = passed_along(above, "line", 1)
    from_next = passed_along(below, "line", -1)
    return middle + from_prev + from_next


def return_shot(terms, block):
    below = lax.slice_in_dim(terms, 0, block, axis=2)
    middle = lax.slice_in_dim(terms, block, 2 * block, axis=2)
    above = lax.slice_in_dim(terms, 2 * block, 3 * block, axis=2)
    from_prev = passed_along(above, "shot", 1)
    from_next = passed_along(below, "shot", -1)
    return middle + from_prev + from_next


def body(velocity, density, start_pressure, observed, corners):
    block = velocity.shape[0]
    depth = velocity.shape[2]
    width = start_pressure.shape[0]
    model = jnp.stack([velocity, density])
    extended = extended_2(model, (("line", 1), ("shot", 2)), block)
    line_index = lax.axis_index("line")
    shot_index = lax.axis_index("shot")
    corner = corners[0, 0]
    offset_x = corner[0] - (line_index - 1) * block
    offset_y = corner[1] - (shot_index - 1) * block
    zero_int = jnp.zeros((), jnp.int32)
    place = (zero_int, offset_x, offset_y, zero_int)
    aperture = lax.dynamic_slice(extended, place, (2, width, width, depth))
    local = jax.grad(shot_misfit)(aperture, start_pressure, observed)
    terms = lax.dynamic_update_slice(
        jnp.zeros((2, 3 * block, 3 * block, depth), jnp.float32), local, place
    )
    owned = return_shot(return_line(terms, block), block)
    return (owned[0], owned[1])


def solution(mesh):
    placed = (
        P("line", "shot", None),
        P("line", "shot", None),
        P("line", "shot", None),
        P("line", "shot", None),
        P("line", "shot", None),
    )
    return jax.shard_map(
        body,
        mesh=mesh,
        in_specs=placed,
        out_specs=(P("line", "shot", None), P("line", "shot", None)),
        check_vma=False,
    )
```

profile of v0, /device:TPU:95, one launch (start us, length us, event | category | flops | bytes accessed | tf_op | source)
XLA Modules:
  0.0 120.0 jit_solution(15456487612573108916)
XLA Ops:
  0.6 1.0 pad_maximum_fusion.1
  1.6 7.6 %collective-permute-start = (f32[2,16,16,128]{3,2,1,0:T(8,128)S(1)}, f32[2,16,16,128]{3,2,1,0:T(8,128)S(1)}, u32[]{:S(2)}, u32[]{:S(2)}) collective-permute-start(f32[2,16,16,128]{3,2,1,0:T(8,128)S(1)} %pad_maximum_fusion.1), channel_id=1, source_target_pairs={{0,16},{16,32},{32,48},{48,64},{64,80},{80,96},{96,112},{112,128},... | collective-permute-start | bytes 786440 | tf_op jit(solution)/shard_map/ppermute | solution.py:25
  9.3 1.9 %collective-permute-start.1 = (f32[2,16,16,128]{3,2,1,0:T(8,128)S(1)}, f32[2,16,16,128]{3,2,1,0:T(8,128)S(1)}, u32[]{:S(2)}, u32[]{:S(2)}) collective-permute-start(f32[2,16,16,128]{3,2,1,0:T(8,128)S(1)} %pad_maximum_fusion.1), channel_id=1, source_target_pairs={{16,0},{32,16},{48,32},{64,48},{80,64},{96,80},{112,96},{128,112},... | collective-permute-start | bytes 786440 | tf_op jit(solution)/shard_map/ppermute | solution.py:27
  11.2 4.2 %collective-permute-done = f32[2,16,16,128]{3,2,1,0:T(8,128)S(1)} collective-permute-done((f32[2,16,16,128]{3,2,1,0:T(8,128)S(1)}, f32[2,16,16,128]{3,2,1,0:T(8,128)S(1)}, u32[]{:S(2)}, u32[]{:S(2)}) %collective-permute-start) | collective-permute-done | bytes 262176 | tf_op jit(solution)/shard_map/ppermute | solution.py:25
  15.4 12.2 %collective-permute-done.1 = f32[2,16,16,128]{3,2,1,0:T(8,128)S(1)} collective-permute-done((f32[2,16,16,128]{3,2,1,0:T(8,128)S(1)}, f32[2,16,16,128]{3,2,1,0:T(8,128)S(1)}, u32[]{:S(2)}, u32[]{:S(2)}) %collective-permute-start.1) | collective-permute-done | bytes 262176 | tf_op jit(solution)/shard_map/ppermute | solution.py:27
  27.5 1.0 pad_maximum_fusion
  28.6 1.9 %collective-permute-start.2 = (f32[2,48,16,128]{3,2,1,0:T(8,128)S(1)}, f32[2,48,16,128]{3,2,1,0:T(8,128)S(1)}, u32[]{:S(2)}, u32[]{:S(2)}) collective-permute-start(f32[2,48,16,128]{3,2,1,0:T(8,128)S(1)} %pad_maximum_fusion), channel_id=1, source_target_pairs={{0,1},{1,2},{2,3},{3,4},{4,5},{5,6},{6,7},{7,8},{8,9},{9,10},{10,1... | collective-permute-start | bytes 2359304 | tf_op jit(solution)/shard_map/ppermute | solution.py:25
  30.5 3.4 %collective-permute-start.3 = (f32[2,48,16,128]{3,2,1,0:T(8,128)S(1)}, f32[2,48,16,128]{3,2,1,0:T(8,128)}, u32[]{:S(2)}, u32[]{:S(2)}) collective-permute-start(f32[2,48,16,128]{3,2,1,0:T(8,128)S(1)} %pad_maximum_fusion), channel_id=1, source_target_pairs={{1,0},{2,1},{3,2},{4,3},{5,4},{6,5},{7,6},{8,7},{9,8},{10,9},{11,1... | collective-permute-start | bytes 2359304 | tf_op jit(solution)/shard_map/ppermute | solution.py:27
  33.9 1.3 %fusion.271 = (s32[1,1,1]{2,1,0:T(1,128)}, s32[1,1,1]{2,1,0:T(1,128)}) fusion(s32[1,1,2]{2,1,0:T(1,128)} %param.13), kind=kLoop, calls=%fused_computation.411 | loop fusion | bytes 16 | tf_op jit(solution)/shard_map/slice | solution.py:106
  36.5 4.8 %collective-permute-done.2 = f32[2,48,16,128]{3,2,1,0:T(8,128)S(1)} collective-permute-done((f32[2,48,16,128]{3,2,1,0:T(8,128)S(1)}, f32[2,48,16,128]{3,2,1,0:T(8,128)S(1)}, u32[]{:S(2)}, u32[]{:S(2)}) %collective-permute-start.2) | collective-permute-done | bytes 786464 | tf_op jit(solution)/shard_map/ppermute | solution.py:25
  41.3 4.1 %collective-permute-done.3 = f32[2,48,16,128]{3,2,1,0:T(8,128)} collective-permute-done((f32[2,48,16,128]{3,2,1,0:T(8,128)S(1)}, f32[2,48,16,128]{3,2,1,0:T(8,128)}, u32[]{:S(2)}, u32[]{:S(2)}) %collective-permute-start.3) | collective-permute-done | bytes 786464 | tf_op jit(solution)/shard_map/ppermute | solution.py:27
  45.5 1.8 %fusion.1 = f32[2,32,32,128]{3,2,1,0:T(8,128)S(1)} fusion(s32[]{:T(128)S(6)} %select_n.8, s32[]{:T(128)S(6)} %select_n.9, f32[2,48,16,128]{3,2,1,0:T(8,128)S(1)} %collective-permute-done.2, f32[2,16,16,128]{3,2,1,0:T(8,128)S(1)} %collective-permute-done, f32[1,16,16,128]{3,2,1,0:T(8,128)} %bitcast.56, f32[1,16,16,128]{3,2,1,0:T(8,128)} %bitcast.53, ...), kind=kLoop, calls=%fused_computation.35 | loop fusion | flops 1310720 | bytes 3407880 | tf_op jit(solution)/shard_map/concatenate | solution.py:23
  47.3 2.3 %divide_subtract_fusion.5 = (f32[32,32,128]{2,1,0:T(8,128)S(1)}, f32[32,32,128]{2,1,0:T(8,128)}, f32[32,32,128]{2,1,0:T(8,128)S(1)}, f32[32,32,128]{2,1,0:T(8,12...) fusion(f32[2,32,32,128]{3,2,1,0:T(8,128)S(1)} %fusion.1, f32[32,32,128]{2,1,0:T(8,128)S(1)} %copy-done.3), kind=kLoop, calls=%fused_computation.356 | loop fusion | flops 5505024 | bytes 4194304 | tf_op jit(solution)/shard_map/jvp()/sub | solution.py:68
  49.5 1.1 multiply_subtract_fusion.1
  50.6 0.6 slice.462
  51.8 0.1 scatter-add.6
  52.0 3.4 %divide_subtract_fusion.2 = (f32[32,32,128]{2,1,0:T(8,128)S(1)}, f32[32,32,128]{2,1,0:T(8,128)}, f32[32,32,128]{2,1,0:T(8,128)S(1)}, f32[32,32,128]{2,1,0:T(8,12...) fusion(f32[32,32,128]{2,1,0:T(8,128)S(1)} %get-tuple-element.56, f32[2,32,32,128]{3,2,1,0:T(8,128)S(1)} %fusion.1, ...), kind=kLoop, calls=%fused_computation.352 | loop fusion | flops 5505024 | bytes 5767168 | tf_op jit(solution)/shard_map/jvp()/sub | solution.py:68
  55.4 1.1 multiply_subtract_fusion
  56.5 0.8 copy-done.2
  57.3 0.6 slice.463
  58.5 1.5 %scatter-add.9 = f32[32,32,128]{2,1,0:T(8,128)} dynamic-update-slice(f32[32,32,128]{2,1,0:T(8,128)} %copy-done.2, f32[1,1,1]{2,1,0:T(1,128)S(6)} %add.372, s32[]{:T(128)} %constant.103.clone.1, s32[]{:T(128)} %constant.103.clone.1, s32[]{:T(128)} %constant.111.clone.1) | dynamic-update-slice | bytes 12 | tf_op jit(solution)/shard_map/jvp()/scatter-add | solution.py:73
  60.0 1.4 %broadcast_multiply_fusion.18 = (f32[32,32,128]{2,1,0:T(8,128)S(1)}, f32[32,32,128]{2,1,0:T(8,128)S(1)}, f32[32,32,128]{2,1,0:T(8,128)S(1)}) fusion(f32[32,32,128]{2,1,0:T(8,128)S(1)} %get-tuple-element.51, f32[32,32,128]{2,1,0:T(8,128)} %scatter-add.9, f32[32,32,128]{2,1,0:T(8,128)} %param.12), kind=kLoop, calls=%fused_computation.385 | loop fusion | flops 786432 | bytes 3145728 | tf_op jit(solution)/shard_map/transpose(jvp())/mul | solution.py:56
  61.4 0.5 fusion.243
  61.9 1.2 fusion.247
  63.0 0.5 fusion.249
  63.6 0.5 fusion.246
  64.0 0.9 fusion.244
  65.0 1.6 %broadcast_multiply_fusion.19 = (f32[32,32,128]{2,1,0:T(8,128)S(1)}, f32[32,32,128]{2,1,0:T(8,128)S(1)}, f32[32,32,128]{2,1,0:T(8,128)S(1)}) fusion(f32[32,32,128]{2,1,0:T(8,128)S(1)} %get-tuple-element.51, f32[32,32,128]{2,1,0:T(8,128)S(1)} %get-tuple-element.97, f32[32,32,128]{2,1,0:T(8,128)S(1)} %get-tuple-element.96, ...), kind=kLoop, calls=%fused_computation.386 | loop fusion | flops 3538944 | bytes 15204352 | tf_op jit(solution)/shard_map/transpose(jvp())/mul | solution.py:56
  66.6 0.5 fusion.237
  67.2 0.4 add_bitcast_fusion
  67.6 0.6 copy-done.5
  68.2 0.2 copy-done.6
  68.3 0.2 copy-done.7
  68.5 0.2 copy-done.8
  68.7 0.2 copy-done.9
  68.8 0.2 copy-done.10
  69.0 2.5 %fusion.51 = f32[1,32,32,128]{3,2,1,0:T(8,128)S(1)} fusion(f32[32,32,128]{2,1,0:T(8,128)S(1)} %copy-done.6, f32[32,32,128]{2,1,0:T(8,128)S(1)} %get-tuple-element.60, f32[32,32,128]{2,1,0:T(8,128)S(1)} %get-tuple-element.75, f32[32,32,128]{2,1,0:T(8,128)S(1)} %get-tuple-element.79, f32[32,32,128]{2,1,0:T(8,128)S(1)} %copy-done.5, ...), kind=kLoop, calls=%fused_computation.162 | loop fusion | flops 8650752 | bytes 12582912 | tf_op jit(solution)/shard_map/transpose(jvp())/broadcast_in_dim | solution.py:62
  71.6 0.2 broadcast_in_dim.13
  71.7 2.6 %dynamic_update_slice.3 = f32[2,48,48,128]{3,2,1,0:T(8,128)S(1)} dynamic-update-slice(f32[2,48,48,128]{3,2,1,0:T(8,128)S(1)} %broadcast_in_dim.13, f32[2,32,32,128]{3,2,1,0:T(8,128)S(1)} %pad_add_fusion, s32[]{:T(128)} %constant.99.clone.1, s32[]{:T(128)S(6)} %select_n.8, s32[]{:T(128)S(6)} %select_n.9, s32[]{:T(128)} %constant.99.clone.1) | dynamic-update-slice | bytes 2097156 | tf_op jit(solution)/shard_map/dynamic_update_slice | solution.py:111
  74.4 2.9 %collective-permute-start.4 = (f32[2,16,48,128]{3,2,1,0:T(8,128)S(1)}, f32[2,16,48,128]{3,2,1,0:T(8,128)S(1)}, u32[]{:S(2)}, u32[]{:S(2)}) collective-permute-start(f32[2,16,48,128]{3,2,1,0:T(8,128)S(1)} %get-tuple-element.61), channel_id=1, source_target_pairs={{0,16},{16,32},{32,48},{48,64},{64,80},{80,96},{96,112},{112,128},... | collective-permute-start | bytes 2359304 | tf_op jit(solution)/shard_map/ppermute | solution.py:14
  77.3 1.9 %collective-permute-start.5 = (f32[2,16,48,128]{3,2,1,0:T(8,128)S(1)}, f32[2,16,48,128]{3,2,1,0:T(8,128)S(1)}, u32[]{:S(2)}, u32[]{:S(2)}) collective-permute-start(f32[2,16,48,128]{3,2,1,0:T(8,128)S(1)} %get-tuple-element.62), channel_id=1, source_target_pairs={{16,0},{32,16},{48,32},{64,48},{80,64},{96,80},{112,96},{128,112},... | collective-permute-start | bytes 2359304 | tf_op jit(solution)/shard_map/ppermute | solution.py:14
  79.3 18.2 %collective-permute-done.4 = f32[2,16,48,128]{3,2,1,0:T(8,128)S(1)} collective-permute-done((f32[2,16,48,128]{3,2,1,0:T(8,128)S(1)}, f32[2,16,48,128]{3,2,1,0:T(8,128)S(1)}, u32[]{:S(2)}, u32[]{:S(2)}) %collective-permute-start.4) | collective-permute-done | bytes 786464 | tf_op jit(solution)/shard_map/ppermute | solution.py:14
  97.5 10.4 %collective-permute-done.5 = f32[2,16,48,128]{3,2,1,0:T(8,128)S(1)} collective-permute-done((f32[2,16,48,128]{3,2,1,0:T(8,128)S(1)}, f32[2,16,48,128]{3,2,1,0:T(8,128)S(1)}, u32[]{:S(2)}, u32[]{:S(2)}) %collective-permute-start.5) | collective-permute-done | bytes 786464 | tf_op jit(solution)/shard_map/ppermute | solution.py:14
  108.1 1.9 %collective-permute-start.6 = (f32[2,16,16,128]{3,2,1,0:T(8,128)S(1)}, f32[2,16,16,128]{3,2,1,0:T(8,128)S(1)}, u32[]{:S(2)}, u32[]{:S(2)}) collective-permute-start(f32[2,16,16,128]{3,2,1,0:T(8,128)S(1)} %get-tuple-element.71), channel_id=1, source_target_pairs={{0,1},{1,2},{2,3},{3,4},{4,5},{5,6},{6,7},{7,8},{8,9},{9,10},{10,1... | collective-permute-start | bytes 786440 | tf_op jit(solution)/shard_map/ppermute | solution.py:14
  110.0 3.4 %collective-permute-start.7 = (f32[2,16,16,128]{3,2,1,0:T(8,128)S(1)}, f32[2,16,16,128]{3,2,1,0:T(8,128)S(1)}, u32[]{:S(2)}, u32[]{:S(2)}) collective-permute-start(f32[2,16,16,128]{3,2,1,0:T(8,128)S(1)} %get-tuple-element.72), channel_id=1, source_target_pairs={{1,0},{2,1},{3,2},{4,3},{5,4},{6,5},{7,6},{8,7},{9,8},{10,9},{11,1... | collective-permute-start | bytes 786440 | tf_op jit(solution)/shard_map/ppermute | solution.py:14
  113.4 1.8 %collective-permute-done.6 = f32[2,16,16,128]{3,2,1,0:T(8,128)S(1)} collective-permute-done((f32[2,16,16,128]{3,2,1,0:T(8,128)S(1)}, f32[2,16,16,128]{3,2,1,0:T(8,128)S(1)}, u32[]{:S(2)}, u32[]{:S(2)}) %collective-permute-start.6) | collective-permute-done | bytes 262176 | tf_op jit(solution)/shard_map/ppermute | solution.py:14
  115.2 4.0 %collective-permute-done.7 = f32[2,16,16,128]{3,2,1,0:T(8,128)S(1)} collective-permute-done((f32[2,16,16,128]{3,2,1,0:T(8,128)S(1)}, f32[2,16,16,128]{3,2,1,0:T(8,128)S(1)}, u32[]{:S(2)}, u32[]{:S(2)}) %collective-permute-start.7) | collective-permute-done | bytes 262176 | tf_op jit(solution)/shard_map/ppermute | solution.py:14
  119.3 0.7 slice_bitcast_fusion.2
  (20 shorter events, 0.5 us)
Async XLA Ops:
  1.6 45.6 %copy-start.3 = (f32[32,32,128]{2,1,0:T(8,128)S(1)}, f32[32,32,128]{2,1,0:T(8,128)}, u32[]{:S(2)}) copy-start(f32[32,32,128]{2,1,0:T(8,128)} %param.11) | copy-start | bytes 1572868
  1.6 13.7 %collective-permute-start = (f32[2,16,16,128]{3,2,1,0:T(8,128)S(1)}, f32[2,16,16,128]{3,2,1,0:T(8,128)S(1)}, u32[]{:S(2)}, u32[]{:S(2)}) collective-permute-start(f32[2,16,16,128]{3,2,1,0:T(8,128)S(1)} %pad_maximum_fusion.1), channel_id=1, source_target_pairs={{0,16},{16,32},{32,48},{48,64},{64,80},{80,96},{96,112},{112,128},... | collective-permute-start | bytes 786440 | tf_op jit(solution)/shard_map/ppermute | solution.py:25
  9.3 18.3 %collective-permute-start.1 = (f32[2,16,16,128]{3,2,1,0:T(8,128)S(1)}, f32[2,16,16,128]{3,2,1,0:T(8,128)S(1)}, u32[]{:S(2)}, u32[]{:S(2)}) collective-permute-start(f32[2,16,16,128]{3,2,1,0:T(8,128)S(1)} %pad_maximum_fusion.1), channel_id=1, source_target_pairs={{16,0},{32,16},{48,32},{64,48},{80,64},{96,80},{112,96},{128,112},... | collective-permute-start | bytes 786440 | tf_op jit(solution)/shard_map/ppermute | solution.py:27
  28.6 12.7 %collective-permute-start.2 = (f32[2,48,16,128]{3,2,1,0:T(8,128)S(1)}, f32[2,48,16,128]{3,2,1,0:T(8,128)S(1)}, u32[]{:S(2)}, u32[]{:S(2)}) collective-permute-start(f32[2,48,16,128]{3,2,1,0:T(8,128)S(1)} %pad_maximum_fusion), channel_id=1, source_target_pairs={{0,1},{1,2},{2,3},{3,4},{4,5},{5,6},{6,7},{7,8},{8,9},{9,10},{10,1... | collective-permute-start | bytes 2359304 | tf_op jit(solution)/shard_map/ppermute | solution.py:25
  30.5 14.9 %collective-permute-start.3 = (f32[2,48,16,128]{3,2,1,0:T(8,128)S(1)}, f32[2,48,16,128]{3,2,1,0:T(8,128)}, u32[]{:S(2)}, u32[]{:S(2)}) collective-permute-start(f32[2,48,16,128]{3,2,1,0:T(8,128)S(1)} %pad_maximum_fusion), channel_id=1, source_target_pairs={{1,0},{2,1},{3,2},{4,3},{5,4},{6,5},{7,6},{8,7},{9,8},{10,9},{11,1... | collective-permute-start | bytes 2359304 | tf_op jit(solution)/shard_map/ppermute | solution.py:27
  47.2 2.3 %copy-start.4 = (f32[32,32,128]{2,1,0:T(8,128)S(1)}, f32[32,32,128]{2,1,0:T(8,128)}, u32[]{:S(2)}) copy-start(f32[32,32,128]{2,1,0:T(8,128)} %param.11) | copy-start | bytes 1572868
  49.5 1.1 copy-start
  49.5 1.1 copy-start.1
  56.5 0.8 copy-start.2
  67.1 1.0 copy-start.5
  67.1 1.2 copy-start.6
  67.1 1.3 %copy-start.7 = (f32[32,32,128]{2,1,0:T(8,128)S(1)}, f32[32,32,128]{2,1,0:T(8,128)}, u32[]{:S(2)}) copy-start(f32[32,32,128]{2,1,0:T(8,128)} %get-tuple-element.70) | copy-start | bytes 1572868
  67.2 1.5 %copy-start.8 = (f32[32,32,128]{2,1,0:T(8,128)S(1)}, f32[32,32,128]{2,1,0:T(8,128)}, u32[]{:S(2)}) copy-start(f32[32,32,128]{2,1,0:T(8,128)} %get-tuple-element.48) | copy-start | bytes 1572868
  67.2 1.6 %copy-start.9 = (f32[32,32,128]{2,1,0:T(8,128)S(1)}, f32[32,32,128]{2,1,0:T(8,128)}, u32[]{:S(2)}) copy-start(f32[32,32,128]{2,1,0:T(8,128)} %get-tuple-element.64) | copy-start | bytes 1572868
  67.2 1.8 %copy-start.10 = (f32[32,32,128]{2,1,0:T(8,128)S(1)}, f32[32,32,128]{2,1,0:T(8,128)}, u32[]{:S(2)}) copy-start(f32[32,32,128]{2,1,0:T(8,128)} %get-tuple-element.66) | copy-start | bytes 1572868
  74.4 23.0 %collective-permute-start.4 = (f32[2,16,48,128]{3,2,1,0:T(8,128)S(1)}, f32[2,16,48,128]{3,2,1,0:T(8,128)S(1)}, u32[]{:S(2)}, u32[]{:S(2)}) collective-permute-start(f32[2,16,48,128]{3,2,1,0:T(8,128)S(1)} %get-tuple-element.61), channel_id=1, source_target_pairs={{0,16},{16,32},{32,48},{48,64},{64,80},{80,96},{96,112},{112,128},... | collective-permute-start | bytes 2359304 | tf_op jit(solution)/shard_map/ppermute | solution.py:14
  77.3 30.6 %collective-permute-start.5 = (f32[2,16,48,128]{3,2,1,0:T(8,128)S(1)}, f32[2,16,48,128]{3,2,1,0:T(8,128)S(1)}, u32[]{:S(2)}, u32[]{:S(2)}) collective-permute-start(f32[2,16,48,128]{3,2,1,0:T(8,128)S(1)} %get-tuple-element.62), channel_id=1, source_target_pairs={{16,0},{32,16},{48,32},{64,48},{80,64},{96,80},{112,96},{128,112},... | collective-permute-start | bytes 2359304 | tf_op jit(solution)/shard_map/ppermute | solution.py:14
  108.1 7.1 %collective-permute-start.6 = (f32[2,16,16,128]{3,2,1,0:T(8,128)S(1)}, f32[2,16,16,128]{3,2,1,0:T(8,128)S(1)}, u32[]{:S(2)}, u32[]{:S(2)}) collective-permute-start(f32[2,16,16,128]{3,2,1,0:T(8,128)S(1)} %get-tuple-element.71), channel_id=1, source_target_pairs={{0,1},{1,2},{2,3},{3,4},{4,5},{5,6},{6,7},{7,8},{8,9},{9,10},{10,1... | collective-permute-start | bytes 786440 | tf_op jit(solution)/shard_map/ppermute | solution.py:14
  110.0 9.2 %collective-permute-start.7 = (f32[2,16,16,128]{3,2,1,0:T(8,128)S(1)}, f32[2,16,16,128]{3,2,1,0:T(8,128)S(1)}, u32[]{:S(2)}, u32[]{:S(2)}) collective-permute-start(f32[2,16,16,128]{3,2,1,0:T(8,128)S(1)} %get-tuple-element.72), channel_id=1, source_target_pairs={{1,0},{2,1},{3,2},{4,3},{5,4},{6,5},{7,6},{8,7},{9,8},{10,9},{11,1... | collective-permute-start | bytes 786440 | tf_op jit(solution)/shard_map/ppermute | solution.py:14
where the time goes:
time: 121 us; the launch traced here: 120 us
  waiting for transfers between devices  59.8 us (49%)
  starting transfers between devices  24.9 us (21%)
  other arithmetic  21.8 us (18%)
  local copies, waits for them, and re-layouts  9.91 us (8%)
  between operations  3.56 us (3%)
    ppermute x4, waiting for transfers between devices, passed_along(): return lax.ppermute(block, axis, route)  34.5 us
    ppermute x2, waiting for transfers between devices, extended_2(): lax.ppermute(head, axis, [((i + 1) % count, i) for i in range(ends)])  16.3 us
    ppermute x4, starting transfers between devices, passed_along(): return lax.ppermute(block, axis, route)  10.1 us
    ppermute x2, starting transfers between devices, extended_2(): lax.ppermute(tail, axis, [(i, (i + 1) % count) for i in range(ends)])  9.55 us
    ppermute x2, waiting for transfers between devices, extended_2(): lax.ppermute(tail, axis, [(i, (i + 1) % count) for i in range(ends)])  8.98 us
    sub x2, other arithmetic, shot_misfit(): vel_x = vel_x - time_ratio * deriv_plus(pressure, 0) / dense  5.7 us
    ppermute x2, starting transfers between devices, extended_2(): lax.ppermute(head, axis, [((i + 1) % count, i) for i in range(ends)])  5.28 us
    neg x4, other arithmetic, deriv_plus(): total = total + coeffs[m - 1] * (upper - lower)  3.07 us
  transfers between devices with their start and end apart: 8, of which 8 were waited for; matrix products, arithmetic and copies ran while one was open for 1% of the time, Pallas kernels for 0%

commit v1 on v0

v1 whole, which is shorter than its diff:
```python
import jax
import jax.numpy as jnp
from jax import lax
from jax.experimental import pallas as pl
from jax.experimental.pallas import tpu as pltpu
from jax.sharding import PartitionSpec as P

coeffs = (1225.0 / 1024.0, -245.0 / 3072.0, 49.0 / 5120.0, -5.0 / 7168.0)
DEPTH_UNIT = coeffs[0] / 105.0
wavelet = (20.0, -12.0)

BLOCK = 16
APER = 32
NZ = 128
ROWS = 4
F32 = jnp.float32


def swap_pairs(odd):
    pairs = []
    for i in range(1 if odd else 0, 15, 2):
        pairs += [(i, i + 1), (i + 1, i)]
    return pairs


def swap(block, axis, odd):
    return lax.ppermute(block, axis, swap_pairs(odd))


def vmem(count):
    return [pl.BlockSpec(memory_space=pltpu.VMEM)] * count


def offset_in_frame(corner_ref, dim, axis):
    return corner_ref[0, 0, dim] - (lax.axis_index(axis) - 1) * BLOCK


def pack_kernel(corner_ref, vel_ref, rho_ref, out_ref):
    out_ref[0:BLOCK] = vel_ref[...]
    out_ref[BLOCK : 2 * BLOCK] = rho_ref[...]
    shift = offset_in_frame(corner_ref, 0, "line").astype(F32)
    out_ref[2 * BLOCK] = jnp.full((BLOCK, NZ), shift, F32)


def pack(corners, velocity, density):
    return pl.pallas_call(
        pack_kernel,
        out_shape=jax.ShapeDtypeStruct((2 * BLOCK + 1, BLOCK, NZ), F32),
        in_specs=[pl.BlockSpec(memory_space=pltpu.SMEM)] + vmem(2),
        out_specs=pl.BlockSpec(memory_space=pltpu.VMEM),
        name="pack",
    )(corners, velocity, density)


def relay_kernel(c_ref, x_ref, ye_ref, yo_ref, oute_ref, outo_ref):
    even = lax.rem(lax.axis_index("line"), 2) == 0
    sign = jnp.where(even, 1.0, -1.0).astype(F32)
    for y_ref, out_ref in ((ye_ref, oute_ref), (yo_ref, outo_ref)):
        shift = y_ref[2 * BLOCK]
        for j in range(BLOCK):
            from_core = (shift - (j + 0.5)) * sign > 0.0
            for f in range(2):
                out_ref[f * BLOCK + j] = jnp.where(from_core, c_ref[f * BLOCK + j], x_ref[f * BLOCK + j])


def relay(c, x, ye, yo):
    shape = jax.ShapeDtypeStruct((2 * BLOCK, BLOCK, NZ), F32)
    return pl.pallas_call(
        relay_kernel,
        out_shape=(shape, shape),
        in_specs=vmem(4),
        out_specs=tuple(vmem(2)),
        name="relay",
    )(c, x, ye, yo)


def stencil(window, rows):
    total = None
    for m in range(1, 5):
        part = coeffs[m - 1] * (window(3 + m) - window(4 - m))
        total = part if total is None else total + part
    return total


def depth_matrix(first):
    source = lax.broadcasted_iota(jnp.int32, (NZ, NZ), 0)
    target = lax.broadcasted_iota(jnp.int32, (NZ, NZ), 1)
    away = source - target + first
    total = jnp.zeros((NZ, NZ), F32)
    for m in range(1, 5):
        value = coeffs[m - 1] / DEPTH_UNIT
        total = jnp.where(away == m, value, total)
        total = jnp.where(away == 1 - m, -value, total)
    half = total.astype(jnp.bfloat16)
    return jnp.concatenate([half, half], axis=0)


def along_depth(values, matrix):
    flat = values.reshape(-1, NZ)
    upper = flat.astype(jnp.bfloat16)
    lower = (flat - upper.astype(F32)).astype(jnp.bfloat16)
    both = jnp.concatenate([upper, lower], axis=1)
    out = jnp.dot(both, matrix, preferred_element_type=F32)
    return (out * DEPTH_UNIT).reshape(values.shape)


def wave_kernel(
    corner_ref, p0_ref, obs_ref, own_ref, c_ref, x_ref, ye_ref, yo_ref, ye2_ref, yo2_ref,
    eh_ref, oh_ref, ew_ref, ow_ref, mh_ref, mw_ref,
    model, terms, field, bx, by, bz, g1, gs, a1, a2, lam, kap, buoy, quad, dens, dplus_mat, dminus_mat,
):
    ox = offset_in_frame(corner_ref, 0, "line")
    oy = offset_in_frame(corner_ref, 1, "shot")
    even_a = lax.rem(lax.axis_index("line"), 2) == 0
    even_b = lax.rem(lax.axis_index("shot"), 2) == 0
    col_e = pl.multiple_of(jnp.where(even_b, 2 * BLOCK, 0), BLOCK)
    col_o = pl.multiple_of(jnp.where(even_b, 0, 2 * BLOCK), BLOCK)

    dplus_mat[...] = depth_matrix(0)
    dminus_mat[...] = depth_matrix(1)

    for f in range(2):
        rows = slice(f * BLOCK, (f + 1) * BLOCK)
        model[f, BLOCK:, BLOCK : 2 * BLOCK] = own_ref[rows]
        model[f, BLOCK:, pl.ds(col_e, BLOCK)] = ye_ref[rows]
        model[f, BLOCK:, pl.ds(col_o, BLOCK)] = yo_ref[rows]
        model[f, :BLOCK, pl.ds(col_e, BLOCK)] = ye2_ref[rows]
        model[f, :BLOCK, pl.ds(col_o, BLOCK)] = yo2_ref[rows]
        for j in range(BLOCK):
            from_core = (j < ox) == even_a

            @pl.when(from_core)
            def _():
                model[f, j, BLOCK : 2 * BLOCK] = c_ref[f * BLOCK + j]

            @pl.when(jnp.logical_not(from_core))
            def _():
                model[f, j, BLOCK : 2 * BLOCK] = x_ref[f * BLOCK + j]

    field[0:4] = jnp.zeros((4, 48, NZ), F32)
    field[36:40] = jnp.zeros((4, 48, NZ), F32)
    bx[0:4] = jnp.zeros((4, APER, NZ), F32)
    bx[36:40] = jnp.zeros((4, APER, NZ), F32)

    def prepare(i, carry):
        slot = lax.rem(ox + i, APER)
        speed = model[0, slot, pl.ds(oy, APER)]
        dense = model[1, slot, pl.ds(oy, APER)]
        dens[i] = dense
        kap[i] = 0.1 * dense * speed * speed
        buoy[i] = 0.1 / dense
        field[4 + i, 0:8] = jnp.zeros((8, NZ), F32)
        field[4 + i, 40:48] = jnp.zeros((8, NZ), F32)
        by[i, 0:8] = jnp.zeros((8, NZ), F32)
        by[i, 40:48] = jnp.zeros((8, NZ), F32)
        field[4 + i, 8:40] = p0_ref[i]
        for f in range(2):
            terms[f, i] = jnp.zeros((48, NZ), F32)
        return carry

    lax.fori_loop(0, APER, prepare, 0, unroll=2)

    def plus(i0, visit):
        rows = pl.ds(i0, ROWS)
        inner = pl.ds(4 + i0, ROWS)
        gz_all = along_depth(field[inner, 8:40], dplus_mat[...])
        for c in range(4):
            window = field[pl.ds(i0 + 1, ROWS + 7), 8 + 8 * c : 16 + 8 * c]
            gx = stencil(lambda k: window[k : k + ROWS], ROWS)
            gy = stencil(lambda k: field[inner, 5 + 8 * c + k : 13 + 8 * c + k], ROWS)
            visit(rows, c, (gx, gy, gz_all[:, 8 * c : 8 * c + 8]))

    def minus(i0, visit):
        rows = pl.ds(i0, ROWS)
        sz_all = along_depth(bz[rows], dminus_mat[...])
        for c in range(4):
            window = bx[pl.ds(i0, ROWS + 7), 8 * c : 8 * c + 8]
            sx = stencil(lambda k: window[k : k + ROWS], ROWS)
            sy = stencil(lambda k: by[rows, 4 + 8 * c + k : 12 + 8 * c + k], ROWS)
            visit(i0, rows, c, sx + sy + sz_all[:, 8 * c : 8 * c + 8])

    def scaled(rows, c, i0, values):
        cols = slice(8 * c, 8 * c + 8)
        light = buoy[rows, cols]
        bx[pl.ds(4 + i0, ROWS), cols] = light * values[0]
        by[rows, 8 + 8 * c : 16 + 8 * c] = light * values[1]
        bz[rows, cols] = light * values[2]

    def spike(i0, c, weight):
        if c != 2:
            return None
        row = lax.broadcasted_iota(jnp.int32, (ROWS, 8, NZ), 0) + i0
        col = lax.broadcasted_iota(jnp.int32, (ROWS, 8, NZ), 1)
        lane = lax.broadcasted_iota(jnp.int32, (ROWS, 8, NZ), 2)
        return jnp.where((row == 16) & (col == 0) & (lane == 64), weight, 0.0)

    def loop(body):
        lax.fori_loop(0, APER // ROWS, lambda k, carry: (body(k * ROWS), carry)[1], 0)

    def first_plus(i0):
        def visit(rows, c, g):
            cols = slice(8 * c, 8 * c + 8)
            for k in range(3):
                g1[k, rows, cols] = g[k]
            scaled(rows, c, i0, g)

        plus(i0, visit)

    loop(first_plus)

    def first_minus(i0):
        def visit(i0, rows, c, spread):
            cols = slice(8 * c, 8 * c + 8)
            a1[rows, cols] = spread
            place = (pl.ds(4 + i0, ROWS), slice(8 + 8 * c, 16 + 8 * c))
            value = field[place] + kap[rows, cols] * spread
            hit = spike(i0, c, wavelet[0])
            field[place] = value if hit is None else value + hit

        minus(i0, visit)

    loop(first_minus)

    def second_plus(i0):
        def visit(rows, c, g):
            cols = slice(8 * c, 8 * c + 8)
            both = [g1[k, rows, cols] + g[k] for k in range(3)]
            for k in range(3):
                gs[k, rows, cols] = both[k]
            scaled(rows, c, i0, both)

        plus(i0, visit)

    loop(second_plus)

    def second_minus(i0):
        def visit(i0, rows, c, spread):
            cols = slice(8 * c, 8 * c + 8)
            a2[rows, cols] = spread
            place = (pl.ds(4 + i0, ROWS), slice(8 + 8 * c, 16 + 8 * c))
            stiff = kap[rows, cols]
            value = field[place] + stiff * spread
            hit = spike(i0, c, wavelet[1])
            value = value if hit is None else value + hit
            value = value - obs_ref[rows, cols]
            lam[rows, cols] = value
            field[place] = stiff * value

        minus(i0, visit)

    loop(second_minus)

    def third_plus(i0):
        def visit(rows, c, h):
            cols = slice(8 * c, 8 * c + 8)
            quad[rows, cols] = h[0] * gs[0, rows, cols] + h[1] * gs[1, rows, cols] + h[2] * gs[2, rows, cols]
            scaled(rows, c, i0, h)

        plus(i0, visit)

    loop(third_plus)

    def third_minus(i0):
        def visit(i0, rows, c, spread):
            cols = slice(8 * c, 8 * c + 8)
            late = lam[rows, cols]
            early = late + spread
            place = (pl.ds(4 + i0, ROWS), slice(8 + 8 * c, 16 + 8 * c))
            field[place] = kap[rows, cols] * early
            lam[rows, cols] = late * a2[rows, cols] + early * a1[rows, cols]

        minus(i0, visit)

    loop(third_minus)

    def last_plus(i0):
        def visit(rows, c, h):
            cols = slice(8 * c, 8 * c + 8)
            quad[rows, cols] += h[0] * g1[0, rows, cols] + h[1] * g1[1, rows, cols] + h[2] * g1[2, rows, cols]

        plus(i0, visit)

    loop(last_plus)

    def finish(i, carry):
        slot = lax.rem(ox + i, APER)
        speed = model[0, slot, pl.ds(oy, APER)]
        dense = dens[i]
        light = buoy[i]
        stiff = lam[i]
        terms[0, slot, pl.ds(oy, APER)] = 0.2 * dense * speed * stiff
        terms[1, slot, pl.ds(oy, APER)] = 0.1 * speed * speed * stiff + 10.0 * light * light * quad[i]
        return carry

    lax.fori_loop(0, APER, finish, 0, unroll=2)

    for f in range(2):
        rows = slice(f * BLOCK, (f + 1) * BLOCK)
        eh_ref[rows] = terms[f, :BLOCK, pl.ds(col_e, BLOCK)]
        oh_ref[rows] = terms[f, :BLOCK, pl.ds(col_o, BLOCK)]
        ew_ref[rows] = terms[f, BLOCK:, pl.ds(col_e, BLOCK)]
        ow_ref[rows] = terms[f, BLOCK:, pl.ds(col_o, BLOCK)]
        mh_ref[rows] = terms[f, :BLOCK, BLOCK : 2 * BLOCK]
        mw_ref[rows] = terms[f, BLOCK:, BLOCK : 2 * BLOCK]


def wave(corners, p0, obs, own, c, x, ye, yo, ye2, yo2):
    part = jax.ShapeDtypeStruct((2 * BLOCK, BLOCK, NZ), F32)
    cube = pltpu.VMEM((APER, APER, NZ), F32)
    return pl.pallas_call(
        wave_kernel,
        out_shape=(part,) * 6,
        in_specs=[pl.BlockSpec(memory_space=pltpu.SMEM)] + vmem(9),
        out_specs=tuple(vmem(6)),
        scratch_shapes=[
            pltpu.VMEM((2, APER, 48, NZ), F32),
            pltpu.VMEM((2, APER, 48, NZ), F32),
            pltpu.VMEM((APER + 8, 48, NZ), F32),
            pltpu.VMEM((APER + 8, APER, NZ), F32),
            pltpu.VMEM((APER, 48, NZ), F32),
            cube,
            pltpu.VMEM((3, APER, APER, NZ), F32),
            pltpu.VMEM((3, APER, APER, NZ), F32),
            cube, cube, cube, cube, cube, cube, cube,
            pltpu.VMEM((2 * NZ, NZ), jnp.bfloat16),
            pltpu.VMEM((2 * NZ, NZ), jnp.bfloat16),
        ],
        compiler_params=pltpu.CompilerParams(vmem_limit_bytes=32 << 20),
        name="wave",
    )(corners, p0, obs, own, c, x, ye, yo, ye2, yo2)


def combine_kernel(corner_ref, own_ref, e_ref, o_ref, ye_ref, yo_ref, c_ref, x_ref):
    ox = offset_in_frame(corner_ref, 0, "line").astype(F32)
    even = lax.rem(lax.axis_index("line"), 2) == 0
    sign = jnp.where(even, 1.0, -1.0).astype(F32)
    shifts = (jnp.full((BLOCK, NZ), ox, F32), ye_ref[0], yo_ref[0])
    for j in range(BLOCK):
        to_core = [(shift - (j + 0.5)) * sign > 0.0 for shift in shifts]
        for f in range(2):
            r = f * BLOCK + j
            values = (own_ref[r], e_ref[r], o_ref[r])
            near = [jnp.where(m, v, 0.0) for m, v in zip(to_core, values)]
            far = [jnp.where(m, 0.0, v) for m, v in zip(to_core, values)]
            c_ref[r] = near[0] + near[1] + near[2]
            x_ref[r] = far[0] + far[1] + far[2]


def combine(corners, own, e, o, ye, yo):
    part = jax.ShapeDtypeStruct((2 * BLOCK, BLOCK, NZ), F32)
    whole = pl.BlockSpec((2 * BLOCK, BLOCK, NZ), lambda i: (0, 0, 0))
    last = pl.BlockSpec((1, BLOCK, NZ), lambda i: (2 * BLOCK, 0, 0))
    return pl.pallas_call(
        combine_kernel,
        grid=(1,),
        out_shape=(part, part),
        in_specs=[pl.BlockSpec(memory_space=pltpu.SMEM), whole, whole, whole, last, last],
        out_specs=(whole, whole),
        name="combine",
    )(corners, own, e, o, ye, yo)


def total_kernel(own_ref, e_ref, o_ref, c_ref, x_ref, vel_ref, rho_ref):
    for f, out_ref in ((0, vel_ref), (1, rho_ref)):
        rows = slice(f * BLOCK, (f + 1) * BLOCK)
        out_ref[...] = ((own_ref[rows] + e_ref[rows]) + (o_ref[rows] + c_ref[rows])) + x_ref[rows]


def total(*parts):
    block = jax.ShapeDtypeStruct((BLOCK, BLOCK, NZ), F32)
    return pl.pallas_call(
        total_kernel,
        out_shape=(block, block),
        in_specs=vmem(5),
        out_specs=tuple(vmem(2)),
        name="total",
    )(*parts)


def body(velocity, density, start_pressure, observed, corners):
    own = pack(corners, velocity, density)
    x = swap(own, "line", True)
    ye = swap(own, "shot", False)
    yo = swap(own, "shot", True)
    c = swap(own, "line", False)
    ye2, yo2 = relay(c, x, ye, yo)
    ye2 = swap(ye2, "shot", False)
    yo2 = swap(yo2, "shot", True)
    eh, oh, ew, ow, mh, mw = wave(corners, start_pressure, observed, own, c, x, ye, yo, ye2, yo2)
    eh = swap(eh, "shot", False)
    oh = swap(oh, "shot", True)
    ew = swap(ew, "shot", False)
    ow = swap(ow, "shot", True)
    to_core, to_chip = combine(corners, mh, eh, oh, ye, yo)
    chip = swap(to_chip, "line", True)
    core = swap(to_core, "line", False)
    return total(mw, ew, ow, core, chip)


def solution(mesh):
    placed = (P("line", "shot", None),) * 5
    return jax.shard_map(
        body,
        mesh=mesh,
        in_specs=placed,
        out_specs=(P("line", "shot", None),) * 2,
        check_vma=False,
    )
```

time: 121 us -> 88.3 us (0.73)
  the two profiles are of different devices: /device:TPU:95 before, /device:TPU:160 now
where the time goes in v1:
time: 88.3 us; the launch traced here: 87.8 us
  waiting for transfers between devices  37 us (42%)
  starting transfers between devices  23.3 us (26%)
  Pallas kernels  18.7 us (21%)
  local copies, waits for them, and re-layouts  8.01 us (9%)
    ppermute x12, waiting for transfers between devices, swap(): return lax.ppermute(block, axis, swap_pairs(odd))  37 us
    ppermute x12, starting transfers between devices, swap(): return lax.ppermute(block, axis, swap_pairs(odd))  23.3 us
    pallas_call x1, Pallas kernels, wave(): pl.pallas_call(wave_kernel, out_shape=(part,) * 6, in_specs=[pl.BlockSpec...  10.8 us
    unnamed x40, local copies, waits for them, and re-layouts  8.01 us
    pallas_call x1, Pallas kernels, combine(): pl.pallas_call(combine_kernel, grid=(1,), out_shape=(part, part), in_spec...  2.09 us
    pallas_call x1, Pallas kernels, relay(): pl.pallas_call(relay_kernel, out_shape=(shape, shape), in_specs=vmem(4),...  2.05 us
    pallas_call x1, Pallas kernels, total(): pl.pallas_call(total_kernel, out_shape=(block, block), in_specs=vmem(5),...  2 us
  transfers between devices with their start and end apart: 12, of which 7 were waited for; matrix products, arithmetic and copies ran while one was open for 0% of the time, Pallas kernels for 2%

profile of v1, /device:TPU:160, one launch (start us, length us, event | category | flops | bytes accessed | tf_op | source)
XLA Modules:
  0.0 87.8 jit_solution(7058901844274246936)
XLA Ops:
  0.6 0.0 copy-start.10
  0.6 1.7 %pack.1.own_ref = f32[33,16,128]{2,1,0:T(8,128)} custom-call(s32[1,1,2]{2,1,0:T(1,128)} %corner_ref.5, f32[16,16,128]{2,1,0:T(8,128)} %vel_ref.1, f32[16,16,128]{2,1,0:T(8,128)} %rho_ref.1), custom_call_target="tpu_custom_call" | custom-call | tf_op jit(solution)/shard_map/pack/pallas_call | solution.py:46
  2.4 5.5 %collective-permute-start.3 = (f32[33,16,128]{2,1,0:T(8,128)}, f32[33,16,128]{2,1,0:T(8,128)S(1)}, u32[]{:S(2)}, u32[]{:S(2)}) collective-permute-start(f32[33,16,128]{2,1,0:T(8,128)} %pack.1.own_ref), channel_id=1, source_target_pairs={{1,2},{2,1},{3,4},{4,3},{5,6},{6,5},{7,8},{8,7},{9,10},{10,9},{11,... | collective-permute-start | bytes 811016 | tf_op jit(solution)/shard_map/ppermute | solution.py:27
  7.9 0.1 collective-permute-start.2
  8.0 2.3 %collective-permute-start.1 = (f32[33,16,128]{2,1,0:T(8,128)}, f32[33,16,128]{2,1,0:T(8,128)S(1)}, u32[]{:S(2)}, u32[]{:S(2)}) collective-permute-start(f32[33,16,128]{2,1,0:T(8,128)} %pack.1.own_ref), channel_id=1, source_target_pairs={{16,32},{32,16},{48,64},{64,48},{80,96},{96,80},{112,128},{128,112... | collective-permute-start | bytes 811016 | tf_op jit(solution)/shard_map/ppermute | solution.py:27
  10.3 1.3 %collective-permute-start = (f32[33,16,128]{2,1,0:T(8,128)}, f32[33,16,128]{2,1,0:T(8,128)S(1)}, u32[]{:S(2)}, u32[]{:S(2)}) collective-permute-start(f32[33,16,128]{2,1,0:T(8,128)} %pack.1.own_ref), channel_id=1, source_target_pairs={{0,16},{16,0},{32,48},{48,32},{64,80},{80,64},{96,112},{112,96},{1... | collective-permute-start | bytes 811016 | tf_op jit(solution)/shard_map/ppermute | solution.py:27
  11.6 3.4 %collective-permute-done.3.yo_ref = f32[33,16,128]{2,1,0:T(8,128)S(1)} collective-permute-done((f32[33,16,128]{2,1,0:T(8,128)}, f32[33,16,128]{2,1,0:T(8,128)S(1)}, u32[]{:S(2)}, u32[]{:S(2)}) %collective-permute-start.3) | collective-permute-done | bytes 270368 | tf_op jit(solution)/shard_map/ppermute | solution.py:27
  14.9 1.2 %collective-permute-done.2.ye_ref = f32[33,16,128]{2,1,0:T(8,128)S(1)} collective-permute-done((f32[33,16,128]{2,1,0:T(8,128)}, f32[33,16,128]{2,1,0:T(8,128)S(1)}, u32[]{:S(2)}, u32[]{:S(2)}) %collective-permute-start.2) | collective-permute-done | bytes 270368 | tf_op jit(solution)/shard_map/ppermute | solution.py:27
  16.1 8.8 %collective-permute-done.1.x_ref = f32[33,16,128]{2,1,0:T(8,128)S(1)} collective-permute-done((f32[33,16,128]{2,1,0:T(8,128)}, f32[33,16,128]{2,1,0:T(8,128)S(1)}, u32[]{:S(2)}, u32[]{:S(2)}) %collective-permute-start.1) | collective-permute-done | bytes 270368 | tf_op jit(solution)/shard_map/ppermute | solution.py:27
  24.9 0.0 collective-permute-done.c_ref
  24.9 0.0 copy-done
  24.9 0.0 copy-done.2
  24.9 0.7 copy-done.5
  25.6 0.7 copy-done.7
  26.3 2.1 %relay.1 = (f32[32,16,128]{2,1,0:T(8,128)}, f32[32,16,128]{2,1,0:T(8,128)}) custom-call(f32[33,16,128]{2,1,0:T(8,128)} %copy-done.7, f32[33,16,128]{2,1,0:T(8,128)} %copy-done.5, f32[33,16,128]{2,1,0:T(8,128)} %copy-done.2, f32[33,16,128]{2,1,0:T(8,128)} %copy-done), custom_call_target="tpu_custom_call" | custom-call | tf_op jit(solution)/shard_map/relay/pallas_call | solution.py:68
  28.3 2.0 %collective-permute-start.4 = (f32[32,16,128]{2,1,0:T(8,128)}, f32[32,16,128]{2,1,0:T(8,128)S(1)}, u32[]{:S(2)}, u32[]{:S(2)}) collective-permute-start(f32[32,16,128]{2,1,0:T(8,128)} %get-tuple-element.12), channel_id=1, source_target_pairs={{0,1},{1,0},{2,3},{3,2},{4,5},{5,4},{6,7},{7,6},{8,9},{9,8},{10,11... | collective-permute-start | bytes 786440 | tf_op jit(solution)/shard_map/ppermute | solution.py:27
  30.3 1.9 %collective-permute-start.5 = (f32[32,16,128]{2,1,0:T(8,128)}, f32[32,16,128]{2,1,0:T(8,128)S(1)}, u32[]{:S(2)}, u32[]{:S(2)}) collective-permute-start(f32[32,16,128]{2,1,0:T(8,128)} %get-tuple-element.13), channel_id=1, source_target_pairs={{1,2},{2,1},{3,4},{4,3},{5,6},{6,5},{7,8},{8,7},{9,10},{10,9},{11,... | collective-permute-start | bytes 786440 | tf_op jit(solution)/shard_map/ppermute | solution.py:27
  32.3 2.7 %collective-permute-done.4.ye2_ref = f32[32,16,128]{2,1,0:T(8,128)S(1)} collective-permute-done((f32[32,16,128]{2,1,0:T(8,128)}, f32[32,16,128]{2,1,0:T(8,128)S(1)}, u32[]{:S(2)}, u32[]{:S(2)}) %collective-permute-start.4) | collective-permute-done | bytes 262176 | tf_op jit(solution)/shard_map/ppermute | solution.py:27
  34.9 6.0 %collective-permute-done.5.yo2_ref = f32[32,16,128]{2,1,0:T(8,128)S(1)} collective-permute-done((f32[32,16,128]{2,1,0:T(8,128)}, f32[32,16,128]{2,1,0:T(8,128)S(1)}, u32[]{:S(2)}, u32[]{:S(2)}) %collective-permute-start.5) | collective-permute-done | bytes 262176 | tf_op jit(solution)/shard_map/ppermute | solution.py:27
  40.9 0.0 copy-done.10
  40.9 0.0 copy-done.4
  40.9 0.9 %copy-done.1 = f32[33,16,128]{2,1,0:T(8,128)S(1)} copy-done((f32[33,16,128]{2,1,0:T(8,128)S(1)}, f32[33,16,128]{2,1,0:T(8,128)}, u32[]{:S(2)}) %copy-start.1) | copy-done | bytes 270360
  41.9 1.0 %copy-done.3 = f32[33,16,128]{2,1,0:T(8,128)S(1)} copy-done((f32[33,16,128]{2,1,0:T(8,128)S(1)}, f32[33,16,128]{2,1,0:T(8,128)}, u32[]{:S(2)}) %copy-start.3) | copy-done | bytes 270360
  42.8 1.0 %copy-done.6 = f32[33,16,128]{2,1,0:T(8,128)S(1)} copy-done((f32[33,16,128]{2,1,0:T(8,128)S(1)}, f32[33,16,128]{2,1,0:T(8,128)}, u32[]{:S(2)}) %copy-start.6) | copy-done | bytes 270360
  43.8 1.0 %copy-done.8 = f32[33,16,128]{2,1,0:T(8,128)S(1)} copy-done((f32[33,16,128]{2,1,0:T(8,128)S(1)}, f32[33,16,128]{2,1,0:T(8,128)}, u32[]{:S(2)}) %copy-start.8) | copy-done | bytes 270360
  44.7 10.8 %wave.1 = (f32[32,16,128]{2,1,0:T(8,128)S(1)}, f32[32,16,128]{2,1,0:T(8,128)S(1)}, f32[32,16,128]{2,1,0:T(8,128)S(1)}, f32[32,16,128]{2,1,0:T(8,128)S(1)}, f32[3...) custom-call(s32[1,1,2]{2,1,0:T(1,128)S(1)} %copy-done.13, f32[32,32,128]{2,1,0:T(8,128)S(1)} %copy-done.9, ...), custom_call_target="tpu_custom_call" | custom-call | tf_op jit(solution)/shard_map/wave/pallas_call | solution.py:310
  55.6 0.7 copy-done.11
  56.3 0.7 copy-done.12
  57.0 0.0 collective-permute-start.8
  57.0 1.9 %collective-permute-start.9 = (f32[32,16,128]{2,1,0:T(8,128)S(1)}, f32[32,16,128]{2,1,0:T(8,128)S(1)}, u32[]{:S(2)}, u32[]{:S(2)}) collective-permute-start(f32[32,16,128]{2,1,0:T(8,128)S(1)} %get-tuple-element.19), channel_id=1, source_target_pairs={{1,2},{2,1},{3,4},{4,3},{5,6},{6,5},{7,8},{8,7},{9,10},{10,9},{11,... | collective-permute-start | bytes 786440 | tf_op jit(solution)/shard_map/ppermute | solution.py:27
  58.9 2.1 %collective-permute-start.6 = (f32[32,16,128]{2,1,0:T(8,128)S(1)}, f32[32,16,128]{2,1,0:T(8,128)S(1)}, u32[]{:S(2)}, u32[]{:S(2)}) collective-permute-start(f32[32,16,128]{2,1,0:T(8,128)S(1)} %get-tuple-element.15), channel_id=1, source_target_pairs={{0,1},{1,0},{2,3},{3,2},{4,5},{5,4},{6,7},{7,6},{8,9},{9,8},{10,11... | collective-permute-start | bytes 786440 | tf_op jit(solution)/shard_map/ppermute | solution.py:27
  61.0 4.0 %collective-permute-start.7 = (f32[32,16,128]{2,1,0:T(8,128)S(1)}, f32[32,16,128]{2,1,0:T(8,128)S(1)}, u32[]{:S(2)}, u32[]{:S(2)}) collective-permute-start(f32[32,16,128]{2,1,0:T(8,128)S(1)} %get-tuple-element.16), channel_id=1, source_target_pairs={{1,2},{2,1},{3,4},{4,3},{5,6},{6,5},{7,8},{8,7},{9,10},{10,9},{11,... | collective-permute-start | bytes 786440 | tf_op jit(solution)/shard_map/ppermute | solution.py:27
  65.0 0.0 collective-permute-done.8.e_ref
  65.0 2.3 %collective-permute-done.9.o_ref = f32[32,16,128]{2,1,0:T(8,128)S(1)} collective-permute-done((f32[32,16,128]{2,1,0:T(8,128)S(1)}, f32[32,16,128]{2,1,0:T(8,128)S(1)}, u32[]{:S(2)}, u32[]{:S(2)}) %collective-permute-start.9) | collective-permute-done | bytes 262176 | tf_op jit(solution)/shard_map/ppermute | solution.py:27
  67.3 0.0 copy-done.17
  67.3 0.7 copy-done.19
  68.0 2.1 %combine.1 = (f32[32,16,128]{2,1,0:T(8,128)}, f32[32,16,128]{2,1,0:T(8,128)}) custom-call(s32[1,1,2]{2,1,0:T(1,128)} %corner_ref.5, f32[32,16,128]{2,1,0:T(8,128)} %copy-done.12, f32[32,16,128]{2,1,0:T(8,128)} %copy-done.17, f32[32,16,128]{2,1,0:T(8,128)} %copy-done.19, f32[33,16,128]{2,1,0:T(8,128)} %copy-done.2, f32[33,16,128]{2,1,0:T(8,128)} %copy-done), custom_call_target="tpu_custom_call" | custom-call | tf_op jit(solution)/shard_map/combine/pallas_call | solution.py:353
  70.1 0.0 collective-permute-start.10
  70.1 2.1 %collective-permute-start.11 = (f32[32,16,128]{2,1,0:T(8,128)}, f32[32,16,128]{2,1,0:T(8,128)S(1)}, u32[]{:S(2)}, u32[]{:S(2)}) collective-permute-start(f32[32,16,128]{2,1,0:T(8,128)} %get-tuple-element.21), channel_id=1, source_target_pairs={{16,32},{32,16},{48,64},{64,48},{80,96},{96,80},{112,128},{128,112... | collective-permute-start | bytes 786440 | tf_op jit(solution)/shard_map/ppermute | solution.py:27
  72.3 0.0 collective-permute-done.6.e_ref
  72.3 0.0 collective-permute-done.7.o_ref
  72.3 0.0 copy-start.15
  72.3 0.0 collective-permute-done.10.c_ref
  72.3 12.8 %collective-permute-done.11.x_ref = f32[32,16,128]{2,1,0:T(8,128)S(1)} collective-permute-done((f32[32,16,128]{2,1,0:T(8,128)}, f32[32,16,128]{2,1,0:T(8,128)S(1)}, u32[]{:S(2)}, u32[]{:S(2)}) %collective-permute-start.11) | collective-permute-done | bytes 262176 | tf_op jit(solution)/shard_map/ppermute | solution.py:27
  85.1 0.0 copy-done.14
  85.1 0.0 copy-done.16
  85.1 0.7 copy-done.18
  85.8 2.0 %total.1 = (f32[16,16,128]{2,1,0:T(8,128)}, f32[16,16,128]{2,1,0:T(8,128)}) custom-call(f32[32,16,128]{2,1,0:T(8,128)} %copy-done.11, f32[32,16,128]{2,1,0:T(8,128)} %copy-done.14, f32[32,16,128]{2,1,0:T(8,128)} %copy-done.15, f32[32,16,128]{2,1,0:T(8,128)} %copy-done.16, f32[32,16,128]{2,1,0:T(8,128)} %copy-done.18), custom_call_target="tpu_custom_call" | custom-call | tf_op jit(solution)/shard_map/total/pallas_call | solution.py:371
  (21 shorter events, 0.0 us)
Async XLA Ops:
  0.6 40.3 %copy-start.10 = (f32[32,32,128]{2,1,0:T(8,128)S(1)}, f32[32,32,128]{2,1,0:T(8,128)}, u32[]{:S(2)}) copy-start(f32[32,32,128]{2,1,0:T(8,128)} %obs_ref.1) | copy-start | bytes 1572868
  2.4 38.5 %copy-start.4 = (f32[33,16,128]{2,1,0:T(8,128)S(1)}, f32[33,16,128]{2,1,0:T(8,128)}, u32[]{:S(2)}) copy-start(f32[33,16,128]{2,1,0:T(8,128)} %pack.1.own_ref) | copy-start | bytes 811012
  2.4 38.5 %copy-start.9 = (f32[32,32,128]{2,1,0:T(8,128)S(1)}, f32[32,32,128]{2,1,0:T(8,128)}, u32[]{:S(2)}) copy-start(f32[32,32,128]{2,1,0:T(8,128)} %p0_ref.1) | copy-start | bytes 1572868
  2.4 12.6 %collective-permute-start.3 = (f32[33,16,128]{2,1,0:T(8,128)}, f32[33,16,128]{2,1,0:T(8,128)S(1)}, u32[]{:S(2)}, u32[]{:S(2)}) collective-permute-start(f32[33,16,128]{2,1,0:T(8,128)} %pack.1.own_ref), channel_id=1, source_target_pairs={{1,2},{2,1},{3,4},{4,3},{5,6},{6,5},{7,8},{8,7},{9,10},{10,9},{11,... | collective-permute-start | bytes 811016 | tf_op jit(solution)/shard_map/ppermute | solution.py:27
  7.9 8.2 %collective-permute-start.2 = (f32[33,16,128]{2,1,0:T(8,128)}, f32[33,16,128]{2,1,0:T(8,128)S(1)}, u32[]{:S(2)}, u32[]{:S(2)}) collective-permute-start(f32[33,16,128]{2,1,0:T(8,128)} %pack.1.own_ref), channel_id=1, source_target_pairs={{0,1},{1,0},{2,3},{3,2},{4,5},{5,4},{6,7},{7,6},{8,9},{9,8},{10,11... | collective-permute-start | bytes 811016 | tf_op jit(solution)/shard_map/ppermute | solution.py:27
  8.0 16.9 %collective-permute-start.1 = (f32[33,16,128]{2,1,0:T(8,128)}, f32[33,16,128]{2,1,0:T(8,128)S(1)}, u32[]{:S(2)}, u32[]{:S(2)}) collective-permute-start(f32[33,16,128]{2,1,0:T(8,128)} %pack.1.own_ref), channel_id=1, source_target_pairs={{16,32},{32,16},{48,64},{64,48},{80,96},{96,80},{112,128},{128,112... | collective-permute-start | bytes 811016 | tf_op jit(solution)/shard_map/ppermute | solution.py:27
  10.3 14.6 %collective-permute-start = (f32[33,16,128]{2,1,0:T(8,128)}, f32[33,16,128]{2,1,0:T(8,128)S(1)}, u32[]{:S(2)}, u32[]{:S(2)}) collective-permute-start(f32[33,16,128]{2,1,0:T(8,128)} %pack.1.own_ref), channel_id=1, source_target_pairs={{0,16},{16,0},{32,48},{48,32},{64,80},{80,64},{96,112},{112,96},{1... | collective-permute-start | bytes 811016 | tf_op jit(solution)/shard_map/ppermute | solution.py:27
  14.9 9.9 %copy-start = (f32[33,16,128]{2,1,0:T(8,128)}, f32[33,16,128]{2,1,0:T(8,128)S(1)}, u32[]{:S(2)}) copy-start(f32[33,16,128]{2,1,0:T(8,128)S(1)} %collective-permute-done.3.yo_ref) | copy-start | bytes 811012
  16.1 8.8 %copy-start.2 = (f32[33,16,128]{2,1,0:T(8,128)}, f32[33,16,128]{2,1,0:T(8,128)S(1)}, u32[]{:S(2)}) copy-start(f32[33,16,128]{2,1,0:T(8,128)S(1)} %collective-permute-done.2.ye_ref) | copy-start | bytes 811012
  24.9 0.7 copy-start.5
  25.6 0.7 copy-start.7
  28.3 12.6 %copy-start.13 = (s32[1,1,2]{2,1,0:T(1,128)S(1)}, s32[1,1,2]{2,1,0:T(1,128)}, u32[]{:S(2)}) copy-start(s32[1,1,2]{2,1,0:T(1,128)} %corner_ref.5) | copy-start | bytes 28
  28.3 6.6 %collective-permute-start.4 = (f32[32,16,128]{2,1,0:T(8,128)}, f32[32,16,128]{2,1,0:T(8,128)S(1)}, u32[]{:S(2)}, u32[]{:S(2)}) collective-permute-start(f32[32,16,128]{2,1,0:T(8,128)} %get-tuple-element.12), channel_id=1, source_target_pairs={{0,1},{1,0},{2,3},{3,2},{4,5},{5,4},{6,7},{7,6},{8,9},{9,8},{10,11... | collective-permute-start | bytes 786440 | tf_op jit(solution)/shard_map/ppermute | solution.py:27
  30.3 10.6 %collective-permute-start.5 = (f32[32,16,128]{2,1,0:T(8,128)}, f32[32,16,128]{2,1,0:T(8,128)S(1)}, u32[]{:S(2)}, u32[]{:S(2)}) collective-permute-start(f32[32,16,128]{2,1,0:T(8,128)} %get-tuple-element.13), channel_id=1, source_target_pairs={{1,2},{2,1},{3,4},{4,3},{5,6},{6,5},{7,8},{8,7},{9,10},{10,9},{11,... | collective-permute-start | bytes 786440 | tf_op jit(solution)/shard_map/ppermute | solution.py:27
  40.9 1.0 %copy-start.1 = (f32[33,16,128]{2,1,0:T(8,128)S(1)}, f32[33,16,128]{2,1,0:T(8,128)}, u32[]{:S(2)}) copy-start(f32[33,16,128]{2,1,0:T(8,128)} %copy-done) | copy-start | bytes 811012
  41.9 1.0 %copy-start.3 = (f32[33,16,128]{2,1,0:T(8,128)S(1)}, f32[33,16,128]{2,1,0:T(8,128)}, u32[]{:S(2)}) copy-start(f32[33,16,128]{2,1,0:T(8,128)} %copy-done.2) | copy-start | bytes 811012
  42.8 1.0 %copy-start.6 = (f32[33,16,128]{2,1,0:T(8,128)S(1)}, f32[33,16,128]{2,1,0:T(8,128)}, u32[]{:S(2)}) copy-start(f32[33,16,128]{2,1,0:T(8,128)} %copy-done.5) | copy-start | bytes 811012
  43.8 1.0 %copy-start.8 = (f32[33,16,128]{2,1,0:T(8,128)S(1)}, f32[33,16,128]{2,1,0:T(8,128)}, u32[]{:S(2)}) copy-start(f32[33,16,128]{2,1,0:T(8,128)} %copy-done.7) | copy-start | bytes 811012
  55.6 0.7 copy-start.11
  56.3 0.7 copy-start.12
  57.0 8.1 %collective-permute-start.8 = (f32[32,16,128]{2,1,0:T(8,128)S(1)}, f32[32,16,128]{2,1,0:T(8,128)S(1)}, u32[]{:S(2)}, u32[]{:S(2)}) collective-permute-start(f32[32,16,128]{2,1,0:T(8,128)S(1)} %get-tuple-element.18), channel_id=1, source_target_pairs={{0,1},{1,0},{2,3},{3,2},{4,5},{5,4},{6,7},{7,6},{8,9},{9,8},{10,11... | collective-permute-start | bytes 786440 | tf_op jit(solution)/shard_map/ppermute | solution.py:27
  57.0 10.4 %collective-permute-start.9 = (f32[32,16,128]{2,1,0:T(8,128)S(1)}, f32[32,16,128]{2,1,0:T(8,128)S(1)}, u32[]{:S(2)}, u32[]{:S(2)}) collective-permute-start(f32[32,16,128]{2,1,0:T(8,128)S(1)} %get-tuple-element.19), channel_id=1, source_target_pairs={{1,2},{2,1},{3,4},{4,3},{5,6},{6,5},{7,8},{8,7},{9,10},{10,9},{11,... | collective-permute-start | bytes 786440 | tf_op jit(solution)/shard_map/ppermute | solution.py:27
  58.9 13.4 %collective-permute-start.6 = (f32[32,16,128]{2,1,0:T(8,128)S(1)}, f32[32,16,128]{2,1,0:T(8,128)S(1)}, u32[]{:S(2)}, u32[]{:S(2)}) collective-permute-start(f32[32,16,128]{2,1,0:T(8,128)S(1)} %get-tuple-element.15), channel_id=1, source_target_pairs={{0,1},{1,0},{2,3},{3,2},{4,5},{5,4},{6,7},{7,6},{8,9},{9,8},{10,11... | collective-permute-start | bytes 786440 | tf_op jit(solution)/shard_map/ppermute | solution.py:27
  61.0 11.3 %collective-permute-start.7 = (f32[32,16,128]{2,1,0:T(8,128)S(1)}, f32[32,16,128]{2,1,0:T(8,128)S(1)}, u32[]{:S(2)}, u32[]{:S(2)}) collective-permute-start(f32[32,16,128]{2,1,0:T(8,128)S(1)} %get-tuple-element.16), channel_id=1, source_target_pairs={{1,2},{2,1},{3,4},{4,3},{5,6},{6,5},{7,8},{8,7},{9,10},{10,9},{11,... | collective-permute-start | bytes 786440 | tf_op jit(solution)/shard_map/ppermute | solution.py:27
  65.0 2.3 %copy-start.17 = (f32[32,16,128]{2,1,0:T(8,128)}, f32[32,16,128]{2,1,0:T(8,128)S(1)}, u32[]{:S(2)}) copy-start(f32[32,16,128]{2,1,0:T(8,128)S(1)} %collective-permute-done.8.e_ref) | copy-start | bytes 786436
  67.3 0.7 copy-start.19
  70.1 2.2 %collective-permute-start.10 = (f32[32,16,128]{2,1,0:T(8,128)}, f32[32,16,128]{2,1,0:T(8,128)S(1)}, u32[]{:S(2)}, u32[]{:S(2)}) collective-permute-start(f32[32,16,128]{2,1,0:T(8,128)} %get-tuple-element.20), channel_id=1, source_target_pairs={{0,16},{16,0},{32,48},{48,32},{64,80},{80,64},{96,112},{112,96},{1... | collective-permute-start | bytes 786440 | tf_op jit(solution)/shard_map/ppermute | solution.py:27
  70.1 14.9 %collective-permute-start.11 = (f32[32,16,128]{2,1,0:T(8,128)}, f32[32,16,128]{2,1,0:T(8,128)S(1)}, u32[]{:S(2)}, u32[]{:S(2)}) collective-permute-start(f32[32,16,128]{2,1,0:T(8,128)} %get-tuple-element.21), channel_id=1, source_target_pairs={{16,32},{32,16},{48,64},{64,48},{80,96},{96,80},{112,128},{128,112... | collective-permute-start | bytes 786440 | tf_op jit(solution)/shard_map/ppermute | solution.py:27
  72.3 12.8 %copy-start.14 = (f32[32,16,128]{2,1,0:T(8,128)}, f32[32,16,128]{2,1,0:T(8,128)S(1)}, u32[]{:S(2)}) copy-start(f32[32,16,128]{2,1,0:T(8,128)S(1)} %collective-permute-done.6.e_ref) | copy-start | bytes 786436
  72.3 12.8 %copy-start.15 = (f32[32,16,128]{2,1,0:T(8,128)}, f32[32,16,128]{2,1,0:T(8,128)S(1)}, u32[]{:S(2)}) copy-start(f32[32,16,128]{2,1,0:T(8,128)S(1)} %collective-permute-done.7.o_ref) | copy-start | bytes 786436
  72.3 12.8 %copy-start.16 = (f32[32,16,128]{2,1,0:T(8,128)}, f32[32,16,128]{2,1,0:T(8,128)S(1)}, u32[]{:S(2)}) copy-start(f32[32,16,128]{2,1,0:T(8,128)S(1)} %collective-permute-done.10.c_ref) | copy-start | bytes 786436
  85.1 0.7 copy-start.18

commit v2 on v0

v2 whole, which is shorter than its diff:
```python
import jax
import jax.numpy as jnp
from jax import lax
from jax.experimental import pallas as pl
from jax.experimental.pallas import tpu as pltpu
from jax.sharding import PartitionSpec as P

coeffs = (1225.0 / 1024.0, -245.0 / 3072.0, 49.0 / 5120.0, -5.0 / 7168.0)
UNIT = coeffs[0] / 105.0
wavelet = (20.0, -12.0)

BLOCK = 16
APER = 32
NZ = 128
ROWS = 8
EXTRA = 1
F32 = jnp.float32
small = pltpu.CompilerParams(vmem_limit_bytes=4 << 20)


def swap_pairs(odd):
    pairs = []
    for i in range(1 if odd else 0, 15, 2):
        pairs += [(i, i + 1), (i + 1, i)]
    return pairs


def swap(block, axis, odd):
    return lax.ppermute(block, axis, swap_pairs(odd))


def vmem(count):
    return [pl.BlockSpec(memory_space=pltpu.VMEM)] * count


def offset_in_frame(corner_ref, dim, axis):
    return corner_ref[dim, 0] - (lax.axis_index(axis) - 1) * BLOCK


def side(axis, odd):
    even = lax.rem(lax.axis_index(axis), 2) == 0
    return pl.multiple_of(jnp.where(even, 0, 2 * BLOCK) if odd else jnp.where(even, 2 * BLOCK, 0), BLOCK)


def stencil(window):
    rows = window.shape[0] - 7
    total = None
    for m in range(1, 5):
        part = coeffs[m - 1] * (window[3 + m : 3 + m + rows] - window[4 - m : 4 - m + rows])
        total = part if total is None else total + part
    return total


def band(size, run, first, source_dim):
    source = lax.broadcasted_iota(jnp.int32, (size, size), source_dim)
    target = lax.broadcasted_iota(jnp.int32, (size, size), 1 - source_dim)
    away = source - target + first
    total = jnp.zeros((size, size), F32)
    for m in range(1, 5):
        value = coeffs[m - 1] / UNIT
        total = jnp.where(away == m, value, total)
        total = jnp.where(away == 1 - m, -value, total)
    return jnp.where(source // run == target // run, total, 0.0)


def halves(values):
    flat = values.reshape(-1, NZ)
    upper = flat.astype(jnp.bfloat16)
    lower = (flat - upper.astype(F32)).astype(jnp.bfloat16)
    return jnp.concatenate([upper, lower], axis=1)


def along_depth(both, matrix):
    return jnp.dot(both, matrix, preferred_element_type=F32).reshape(ROWS, APER, NZ)


def along_width(both, matrix):
    out = jnp.dot(matrix, both, preferred_element_type=F32)
    return (out[:, :NZ] + out[:, NZ:]).reshape(ROWS, APER, NZ)


def chunks():
    return range(0, APER, ROWS)


def plus_all(field, i0, wide, deep):
    both = halves(field[4 + i0 : 4 + i0 + ROWS])
    return (
        stencil(field[1 + i0 : 8 + i0 + ROWS]),
        along_width(both, wide),
        along_depth(both, deep),
    )


def early_kernel(corner_ref, p0_ref, obs_ref, field, g1, wide, deep, obs_out, corner_out):
    obs_out[...] = obs_ref[...]
    row = lax.broadcasted_iota(jnp.int32, (8, NZ), 0)
    corner_out[...] = jnp.where(row == 0, corner_ref[0, 0, 0], corner_ref[0, 0, 1])
    for first in range(2):
        wide[first] = band(ROWS * APER, APER, first, 1).astype(jnp.bfloat16)
        half = band(NZ, NZ, first, 0).astype(jnp.bfloat16)
        deep[first] = jnp.concatenate([half, half], axis=0)
    field[0:4] = jnp.zeros((4, APER, NZ), F32)
    field[36:40] = jnp.zeros((4, APER, NZ), F32)
    field[4:36] = p0_ref[...]
    for i0 in chunks():
        for k, g in enumerate(plus_all(field, i0, wide[0], deep[0])):
            g1[k, i0 : i0 + ROWS] = g


def early(corners, p0, obs):
    return pl.pallas_call(
        early_kernel,
        out_shape=(
            jax.ShapeDtypeStruct((APER + 8, APER, NZ), F32),
            jax.ShapeDtypeStruct((3, APER, APER, NZ), F32),
            jax.ShapeDtypeStruct((2, ROWS * APER, ROWS * APER), jnp.bfloat16),
            jax.ShapeDtypeStruct((2, 2 * NZ, NZ), jnp.bfloat16),
            jax.ShapeDtypeStruct((APER, APER, NZ), F32),
            jax.ShapeDtypeStruct((8, NZ), jnp.int32),
        ),
        in_specs=[pl.BlockSpec(memory_space=pltpu.SMEM)] + vmem(2),
        out_specs=tuple(vmem(6)),
        compiler_params=pltpu.CompilerParams(vmem_limit_bytes=8 << 20),
        name="early",
    )(corners, p0, obs)


def wave_kernel(
    field0, g1, wide, deep, obs_ref, corner_vmem, own_ref, ye_ref, yo_ref, x_ref, c_ref, ye2_ref, yo2_ref, cye_ref, cyo_ref,
    c_out, xe_out, xo_out, xm_out, oe_out, oo_out, om_out,
    corner_ref, sem, model, terms, field, bx, by, bz, gs, a1, a2, lam, kap, buoy, quad,
):
    corner_copy = pltpu.make_async_copy(corner_vmem, corner_ref, sem)
    corner_copy.start()
    row_c, row_x = side("line", False), side("line", True)
    col_e, col_o = side("shot", False), side("shot", True)
    middle = slice(BLOCK, 2 * BLOCK)

    for f in range(2):
        rows = slice(f * BLOCK, (f + 1) * BLOCK)
        model[f, middle, middle] = own_ref[rows]
        model[f, middle, pl.ds(col_e, BLOCK)] = ye_ref[rows]
        model[f, middle, pl.ds(col_o, BLOCK)] = yo_ref[rows]
        model[f, pl.ds(row_c, BLOCK), middle] = c_ref[rows]
        model[f, pl.ds(row_c, BLOCK), pl.ds(col_e, BLOCK)] = cye_ref[rows]
        model[f, pl.ds(row_c, BLOCK), pl.ds(col_o, BLOCK)] = cyo_ref[rows]
        model[f, pl.ds(row_x, BLOCK), middle] = x_ref[rows]
        model[f, pl.ds(row_x, BLOCK), pl.ds(col_e, BLOCK)] = ye2_ref[rows]
        model[f, pl.ds(row_x, BLOCK), pl.ds(col_o, BLOCK)] = yo2_ref[rows]
        terms[f] = jnp.zeros((48, 48, NZ), F32)

    for padded in (field, bx):
        padded[0:4] = jnp.zeros((4, APER, NZ), F32)
        padded[36:40] = jnp.zeros((4, APER, NZ), F32)

    corner_copy.wait()
    ox = offset_in_frame(corner_ref, 0, "line")
    oy = offset_in_frame(corner_ref, 1, "shot")

    def scaled(i0, values):
        rows = slice(i0, i0 + ROWS)
        light = buoy[rows]
        bx[4 + i0 : 4 + i0 + ROWS] = light * values[0]
        light = light * (UNIT * UNIT)
        by[rows] = light * values[1]
        bz[rows] = light * values[2]

    def minus(i0):
        rows = slice(i0, i0 + ROWS)
        spread = along_width(halves(by[rows]), wide[1]) + along_depth(halves(bz[rows]), deep[1])
        return spread + stencil(bx[i0 : i0 + ROWS + 7])

    def dotted(h, g):
        return h[0] * g[0] + (UNIT * UNIT) * (h[1] * g[1] + h[2] * g[2])

    row = lax.broadcasted_iota(jnp.int32, (8, NZ), 0)
    lane = lax.broadcasted_iota(jnp.int32, (8, NZ), 1)
    centre = jnp.where((row == 0) & (lane == 64), 1.0, 0.0)

    for i0 in chunks():
        rows = slice(i0, i0 + ROWS)
        for i in range(i0, i0 + ROWS):
            slot = ox + i
            speed = model[0, slot, pl.ds(oy, APER)]
            dense = model[1, slot, pl.ds(oy, APER)]
            kap[i] = 0.1 * dense * speed * speed
            buoy[i] = 0.1 / dense
        scaled(i0, [g1[k, rows] for k in range(3)])

    for i0 in chunks():
        rows = slice(i0, i0 + ROWS)
        inner = slice(4 + i0, 4 + i0 + ROWS)
        spread = minus(i0)
        a1[rows] = spread
        field[inner] = field0[inner] + kap[rows] * spread
    field[20, 16:24] += wavelet[0] * centre

    for i0 in chunks():
        rows = slice(i0, i0 + ROWS)
        g = plus_all(field, i0, wide[0], deep[0])
        both = [g1[k, rows] + g[k] for k in range(3)]
        for k in range(3):
            gs[k, rows] = both[k]
        scaled(i0, both)
    field[20, 16:24] += wavelet[1] * centre

    for i0 in chunks():
        rows = slice(i0, i0 + ROWS)
        inner = slice(4 + i0, 4 + i0 + ROWS)
        spread = minus(i0)
        a2[rows] = spread
        stiff = kap[rows]
        value = field[inner] + stiff * spread - obs_ref[rows]
        lam[rows] = value
        field[inner] = stiff * value

    for i0 in chunks():
        rows = slice(i0, i0 + ROWS)
        h = plus_all(field, i0, wide[0], deep[0])
        quad[rows] = dotted(h, [gs[k, rows] for k in range(3)])
        scaled(i0, h)

    for i0 in chunks():
        rows = slice(i0, i0 + ROWS)
        inner = slice(4 + i0, 4 + i0 + ROWS)
        late = lam[rows]
        early = late + minus(i0)
        field[inner] = kap[rows] * early
        lam[rows] = late * a2[rows] + early * a1[rows]

    for i0 in chunks():
        rows = slice(i0, i0 + ROWS)
        h = plus_all(field, i0, wide[0], deep[0])
        quad[rows] += dotted(h, [g1[k, rows] for k in range(3)])
        for i in range(i0, i0 + ROWS):
            slot = ox + i
            speed = model[0, slot, pl.ds(oy, APER)]
            dense = model[1, slot, pl.ds(oy, APER)]
            light = buoy[i]
            stiff = lam[i]
            terms[0, slot, pl.ds(oy, APER)] = 0.2 * dense * speed * stiff
            terms[1, slot, pl.ds(oy, APER)] = 0.1 * speed * speed * stiff + 10.0 * light * light * quad[i]

    for f in range(2):
        rows = slice(f * BLOCK, (f + 1) * BLOCK)
        c_out[rows] = terms[f, pl.ds(row_c, BLOCK)]
        xe_out[rows] = terms[f, pl.ds(row_x, BLOCK), pl.ds(col_e, BLOCK)]
        xo_out[rows] = terms[f, pl.ds(row_x, BLOCK), pl.ds(col_o, BLOCK)]
        xm_out[rows] = terms[f, pl.ds(row_x, BLOCK), middle]
        oe_out[rows] = terms[f, middle, pl.ds(col_e, BLOCK)]
        oo_out[rows] = terms[f, middle, pl.ds(col_o, BLOCK)]
        om_out[rows] = terms[f, middle, middle]


part = jax.ShapeDtypeStruct((2 * BLOCK, BLOCK, NZ), F32)


def wave(begun, *blocks):
    cube = pltpu.VMEM((APER, APER, NZ), F32)
    padded = pltpu.VMEM((APER + 8, APER, NZ), F32)
    return pl.pallas_call(
        wave_kernel,
        out_shape=(jax.ShapeDtypeStruct((2 * BLOCK, 3 * BLOCK, NZ), F32),) + (part,) * 6,
        in_specs=vmem(15),
        out_specs=tuple(vmem(7)),
        scratch_shapes=[
            pltpu.SMEM((8, NZ), jnp.int32),
            pltpu.SemaphoreType.DMA,
            pltpu.VMEM((2, 48, 48, NZ), F32),
            pltpu.VMEM((2, 48, 48, NZ), F32),
            padded, padded, cube, cube,
            pltpu.VMEM((3, APER, APER, NZ), F32),
            cube, cube, cube, cube, cube, cube,
        ],
        compiler_params=pltpu.CompilerParams(vmem_limit_bytes=26 << 20),
        name="wave",
    )(*begun, *blocks)


def onward_kernel(x_ref, c_ref, out_ref):
    del c_ref
    out_ref[...] = x_ref[...]


def onward(x, c):
    return pl.pallas_call(
        onward_kernel,
        out_shape=part,
        in_specs=vmem(1) + [pl.BlockSpec(memory_space=pl.ANY)],
        out_specs=vmem(1)[0],
        compiler_params=small,
        name="onward",
    )(x, c)


def merge_kernel(first_ref, c_ref, oe_ref, oo_ref, om_ref, oe_out, oo_out, om_out):
    del first_ref
    oe_out[...] = oe_ref[...] + c_ref[:, pl.ds(side("shot", False), BLOCK)]
    oo_out[: 2 * BLOCK] = oo_ref[...] + c_ref[:, pl.ds(side("shot", True), BLOCK)]
    oo_out[2 * BLOCK :] = jnp.zeros((EXTRA, BLOCK, NZ), F32)
    om_out[...] = om_ref[...] + c_ref[:, BLOCK : 2 * BLOCK]


def merge(first, c, oe, oo, om):
    return pl.pallas_call(
        merge_kernel,
        out_shape=(part, jax.ShapeDtypeStruct((2 * BLOCK + EXTRA, BLOCK, NZ), F32), part),
        in_specs=[pl.BlockSpec(memory_space=pl.ANY)] + vmem(4),
        out_specs=tuple(vmem(3)),
        compiler_params=small,
        name="merge",
    )(first, c, oe, oo, om)


def combine_kernel(m_ref, e_ref, o_ref, oe_ref, out_ref, oe_out):
    del oe_ref, oe_out
    out_ref[...] = m_ref[...] + e_ref[...] + o_ref[...]


def combine(m, e, o, oe):
    place = pl.BlockSpec(memory_space=pl.ANY)
    return pl.pallas_call(
        combine_kernel,
        out_shape=(part, part),
        in_specs=vmem(3) + [place],
        out_specs=(vmem(1)[0], place),
        input_output_aliases={3: 1},
        compiler_params=small,
        name="combine",
    )(m, e, o, oe)


def total_kernel(own_ref, x_ref, e_ref, o_ref, vel_ref, rho_ref):
    for f, out_ref in ((0, vel_ref), (1, rho_ref)):
        rows = slice(f * BLOCK, (f + 1) * BLOCK)
        out_ref[...] = (own_ref[rows] + x_ref[rows]) + (e_ref[rows] + o_ref[rows])


def total(*parts):
    block = jax.ShapeDtypeStruct((BLOCK, BLOCK, NZ), F32)
    return pl.pallas_call(
        total_kernel,
        out_shape=(block, block),
        in_specs=vmem(4),
        out_specs=tuple(vmem(2)),
        compiler_params=small,
        name="total",
    )(*parts)


def body(velocity, density, start_pressure, observed, corners):
    own = jnp.stack([velocity, density]).reshape(2 * BLOCK, BLOCK, NZ)
    c = swap(own, "line", False)
    x = swap(own, "line", True)
    yo = swap(own, "shot", True)
    ye = swap(own, "shot", False)
    begun = early(corners, start_pressure, observed)
    passed = onward(x, c)
    yo2 = swap(passed, "shot", True)
    ye2 = swap(passed, "shot", False)
    cyo = swap(yo, "line", False)
    cye = swap(ye, "line", False)
    to_core, xe, xo, xm, oe, oo, om = wave(begun, own, ye, yo, x, c, ye2, yo2, cye, cyo)
    to_core = swap(to_core, "line", False)
    xo = swap(xo, "shot", True)
    xe = swap(xe, "shot", False)
    oe, oo, om = merge(xe, to_core, oe, oo, om)
    oo = swap(oo, "shot", True)
    xm, oe = combine(xm, xe, xo, oe)
    xm = swap(xm, "line", True)
    oe = swap(oe, "shot", False)
    return total(om, xm, oe, oo)


def solution(mesh):
    placed = (P("line", "shot", None),) * 5
    return jax.shard_map(
        body,
        mesh=mesh,
        in_specs=placed,
        out_specs=(P("line", "shot", None),) * 2,
        check_vma=False,
    )
```

time: 121 us -> 67.5 us (0.56)
  waiting for transfers between devices: 59.8 us -> 27.4 us
  other arithmetic: 21.8 us -> 1.07 us
  local copies, waits for them, and re-layouts: 9.91 us -> 0.66 us
  Pallas kernels: 0 us -> 6.47 us
  starting transfers between devices: 24.9 us -> 30 us
  between operations: 3.56 us -> 0.77 us
    ppermute x8 -> x14, waiting for transfers between devices: 59.8 us -> 27.4 us  [swap(): return lax.ppermute(block, axis, swap_pairs(odd))]
    sub x4 -> x0, other arithmetic: 7.81 us -> none  [the longest x2 5.7 us: shot_misfit(): vel_x = vel_x - time_ratio * deriv_plus(pressure, 0) / dense]
    pallas_call x0 -> x6, Pallas kernels: none -> 6.47 us  [the longest x1 4.23 us: wave(): pl.pallas_call(wave_kernel, out_shape=(jax.ShapeDtypeStruct((2 * BLOCK, 3...]
    ppermute x8 -> x14, starting transfers between devices: 24.9 us -> 30 us  [swap(): return lax.ppermute(block, axis, swap_pairs(odd))]
    neg x6 -> x0, other arithmetic: 4.05 us -> none  [the longest x4 3.07 us: deriv_plus(): total = total + coeffs[m - 1] * (upper - lower)]
    mul x2 -> x0, other arithmetic: 3.03 us -> none  [deriv_minus(): total = total + coeffs[m - 1] * (upper - lower)]
    broadcast_in_dim x2 -> x0, other arithmetic: 2.9 us -> none  [the longest x1 2.52 us: shot_misfit(): dense = model[1]]
    concatenate x2 -> x0, other arithmetic: 2.8 us -> none  [extended_2(): jnp.concatenate([lax.ppermute(tail, axis, [(i, (i + 1) % count) for i in...]
  transfers between devices with their start and end apart: 8 -> 14, of which waited for: 8 -> 6; matrix products, arithmetic and copies ran while one was open for 1% -> 0% of each run, Pallas kernels for 0% -> 2%
where the time goes in v2:
time: 67.5 us; the launch traced here: 66.4 us
  starting transfers between devices  30 us (44%)
  waiting for transfers between devices  27.4 us (41%)
  Pallas kernels  6.47 us (10%)
  other arithmetic  1.07 us (2%)
  between operations  0.77 us (1%)
    ppermute x14, starting transfers between devices, swap(): return lax.ppermute(block, axis, swap_pairs(odd))  30 us
    ppermute x14, waiting for transfers between devices, swap(): return lax.ppermute(block, axis, swap_pairs(odd))  27.4 us
    pallas_call x1, Pallas kernels, wave(): pl.pallas_call(wave_kernel, out_shape=(jax.ShapeDtypeStruct((2 * BLOCK, 3...  4.23 us
  transfers between devices with their start and end apart: 14, of which 6 were waited for; matrix products, arithmetic and copies ran while one was open for 0% of the time, Pallas kernels for 2%

profile of v2, /device:TPU:95, one launch (start us, length us, event | category | flops | bytes accessed | tf_op | source)
XLA Modules:
  0.0 66.4 jit_solution(17710706845951066030)
XLA Ops:
  0.6 0.0 copy-start.1
  0.6 0.0 copy-start
  0.7 1.1 %pad_maximum_fusion = f32[2,16,16,128]{3,2,1,0:T(8,128)S(1)} fusion(f32[1,16,16,128]{3,2,1,0:T(8,128)} %bitcast.8, f32[1,16,16,128]{3,2,1,0:T(8,128)} %bitcast.9), kind=kLoop, calls=%fused_computation | loop fusion | flops 65536 | bytes 524288 | tf_op jit(solution)/shard_map/stack | solution.py:353
  1.7 0.8 %collective-permute-start.3 = (f32[32,16,128]{2,1,0:T(8,128)S(1)}, f32[32,16,128]{2,1,0:T(8,128)S(1)}, u32[]{:S(2)}, u32[]{:S(2)}) collective-permute-start(f32[32,16,128]{2,1,0:T(8,128)S(1)} %bitcast.3), channel_id=1, source_target_pairs={{0,16},{16,0},{32,48},{48,32},{64,80},{80,64},{96,112},{112,96},{1... | collective-permute-start | bytes 786440 | tf_op jit(solution)/shard_map/ppermute | solution.py:29
  2.5 6.8 %collective-permute-start.2 = (f32[32,16,128]{2,1,0:T(8,128)S(1)}, f32[32,16,128]{2,1,0:T(8,128)S(1)}, u32[]{:S(2)}, u32[]{:S(2)}) collective-permute-start(f32[32,16,128]{2,1,0:T(8,128)S(1)} %bitcast.4), channel_id=1, source_target_pairs={{16,32},{32,16},{48,64},{64,48},{80,96},{96,80},{112,128},{128,112... | collective-permute-start | bytes 786440 | tf_op jit(solution)/shard_map/ppermute | solution.py:29
  9.3 2.3 %collective-permute-start.1 = (f32[32,16,128]{2,1,0:T(8,128)S(1)}, f32[32,16,128]{2,1,0:T(8,128)S(1)}, u32[]{:S(2)}, u32[]{:S(2)}) collective-permute-start(f32[32,16,128]{2,1,0:T(8,128)S(1)} %bitcast.5), channel_id=1, source_target_pairs={{1,2},{2,1},{3,4},{4,3},{5,6},{6,5},{7,8},{8,7},{9,10},{10,9},{11,... | collective-permute-start | bytes 786440 | tf_op jit(solution)/shard_map/ppermute | solution.py:29
  11.6 0.3 collective-permute-start
  12.0 0.0 collective-permute-done.3.c_ref
  12.0 8.9 %collective-permute-done.2.x_ref = f32[32,16,128]{2,1,0:T(8,128)S(1)} collective-permute-done((f32[32,16,128]{2,1,0:T(8,128)S(1)}, f32[32,16,128]{2,1,0:T(8,128)S(1)}, u32[]{:S(2)}, u32[]{:S(2)}) %collective-permute-start.2) | collective-permute-done | bytes 262176 | tf_op jit(solution)/shard_map/ppermute | solution.py:29
  20.9 1.9 %collective-permute-start.5 = (f32[32,16,128]{2,1,0:T(8,128)S(1)}, f32[32,16,128]{2,1,0:T(8,128)S(1)}, u32[]{:S(2)}, u32[]{:S(2)}) collective-permute-start(f32[32,16,128]{2,1,0:T(8,128)S(1)} %onward.1), channel_id=1, source_target_pairs={{1,2},{2,1},{3,4},{4,3},{5,6},{6,5},{7,8},{8,7},{9,10},{10,9},{11,... | collective-permute-start | bytes 786440 | tf_op jit(solution)/shard_map/ppermute | solution.py:29
  22.8 0.1 collective-permute-start.4
  22.9 0.6 collective-permute-done.1.yo_ref
  23.5 0.0 collective-permute-start.7
  23.5 0.0 collective-permute-done.ye_ref
  23.5 0.5 collective-permute-start.6
  24.1 0.0 copy-done.1
  24.1 0.0 copy-done
  24.1 0.0 copy-start.2
  24.1 0.7 copy-done.2
  24.7 1.3 %early.1 = (f32[40,32,128]{2,1,0:T(8,128)S(1)}, f32[3,32,32,128]{3,2,1,0:T(8,128)S(1)}, bf16[2,256,256]{2,1,0:T(8,128)(2,1)S(1)}, bf16[2,256,128]{2,1,0:T(8,128)...) custom-call(s32[1,1,2]{2,1,0:T(1,128)S(1)} %copy-done.2, f32[32,32,128]{2,1,0:T(8,128)S(1)} %copy-done, ...), custom_call_target="tpu_custom_call" | custom-call | tf_op jit(solution)/shard_map/early/pallas_call | solution.py:112
  26.0 4.1 %collective-permute-done.5.yo2_ref = f32[32,16,128]{2,1,0:T(8,128)S(1)} collective-permute-done((f32[32,16,128]{2,1,0:T(8,128)S(1)}, f32[32,16,128]{2,1,0:T(8,128)S(1)}, u32[]{:S(2)}, u32[]{:S(2)}) %collective-permute-start.5) | collective-permute-done | bytes 262176 | tf_op jit(solution)/shard_map/ppermute | solution.py:29
  30.1 0.0 collective-permute-done.4.ye2_ref
  30.1 0.0 collective-permute-done.7.cyo_ref
  30.1 0.0 collective-permute-done.6.cye_ref
  30.1 4.2 %wave.1 = (f32[32,48,128]{2,1,0:T(8,128)S(1)}, f32[32,16,128]{2,1,0:T(8,128)S(1)}, f32[32,16,128]{2,1,0:T(8,128)S(1)}, f32[32,16,128]{2,1,0:T(8,128)S(1)}, f32[3...) custom-call(f32[40,32,128]{2,1,0:T(8,128)S(1)} %get-tuple-element.20.field0, ...), custom_call_target="tpu_custom_call" | custom-call | tf_op jit(solution)/shard_map/wave/pallas_call | solution.py:262
  34.4 0.1 collective-permute-start.9
  34.5 0.1 collective-permute-start.8
  34.6 3.4 %collective-permute-start.10 = (f32[32,16,128]{2,1,0:T(8,128)S(1)}, f32[32,16,128]{2,1,0:T(8,128)S(1)}, u32[]{:S(2)}, u32[]{:S(2)}) collective-permute-start(f32[32,16,128]{2,1,0:T(8,128)S(1)} %get-tuple-element.33), channel_id=1, source_target_pairs={{1,2},{2,1},{3,4},{4,3},{5,6},{6,5},{7,8},{8,7},{9,10},{10,9},{11,... | collective-permute-start | bytes 786440 | tf_op jit(solution)/shard_map/ppermute | solution.py:29
  37.9 4.1 %collective-permute-done.8.first_ref.e_ref = f32[32,16,128]{2,1,0:T(8,128)S(1)} collective-permute-done((f32[32,16,128]{2,1,0:T(8,128)S(1)}, f32[32,16,128]{2,1,0:T(8,128)S(1)}, u32[]{:S(2)}, u32[]{:S(2)}) %collective-permute-start.8) | collective-permute-done | bytes 262176 | tf_op jit(solution)/shard_map/ppermute | solution.py:29
  42.0 0.0 collective-permute-done.9.c_ref
  42.0 0.1 merge.1
  42.1 3.4 %collective-permute-start.13 = (f32[33,16,128]{2,1,0:T(8,128)S(1)}, f32[33,16,128]{2,1,0:T(8,128)S(1)}, u32[]{:S(2)}, u32[]{:S(2)}) collective-permute-start(f32[33,16,128]{2,1,0:T(8,128)S(1)} %get-tuple-element.37), channel_id=1, source_target_pairs={{1,2},{2,1},{3,4},{4,3},{5,6},{6,5},{7,8},{8,7},{9,10},{10,9},{11,... | collective-permute-start | bytes 811016 | tf_op jit(solution)/shard_map/ppermute | solution.py:29
  45.5 0.6 collective-permute-done.10.o_ref
  46.1 0.1 combine.1
  46.1 10.2 %collective-permute-start.11 = (f32[32,16,128]{2,1,0:T(8,128)S(1)}, f32[32,16,128]{2,1,0:T(8,128)S(1)}, u32[]{:S(2)}, u32[]{:S(2)}) collective-permute-start(f32[32,16,128]{2,1,0:T(8,128)S(1)} %get-tuple-element.35), channel_id=1, source_target_pairs={{16,32},{32,16},{48,64},{64,48},{80,96},{96,80},{112,128},{128,112... | collective-permute-start | bytes 786440 | tf_op jit(solution)/shard_map/ppermute | solution.py:29
  56.3 0.1 collective-permute-start.12
  56.4 9.2 %collective-permute-done.11.x_ref = f32[32,16,128]{2,1,0:T(8,128)S(1)} collective-permute-done((f32[32,16,128]{2,1,0:T(8,128)S(1)}, f32[32,16,128]{2,1,0:T(8,128)S(1)}, u32[]{:S(2)}, u32[]{:S(2)}) %collective-permute-start.11) | collective-permute-done | bytes 262176 | tf_op jit(solution)/shard_map/ppermute | solution.py:29
  65.6 0.0 collective-permute-done.12.e_ref
  65.7 0.0 collective-permute-done.13.o_ref
  65.7 0.8 %total.1 = (f32[16,16,128]{2,1,0:T(8,128)}, f32[16,16,128]{2,1,0:T(8,128)}) custom-call(f32[32,16,128]{2,1,0:T(8,128)S(1)} %get-tuple-element.31.own_ref, f32[32,16,128]{2,1,0:T(8,128)S(1)} %collective-permute-done.11.x_ref, f32[32,16,128]{2,1,0:T(8,128)S(1)} %collective-permute-done.12.e_ref, f32[33,16,128]{2,1,0:T(8,128)S(1)} %collective-permute-done.13.o_ref), custom_call_target="tpu_custom_call" | custom-call | tf_op jit(solution)/shard_map/total/pallas_call | solution.py:342
  (1 shorter events, 0.0 us)
Async XLA Ops:
  0.6 23.4 %copy-start.1 = (f32[32,32,128]{2,1,0:T(8,128)S(1)}, f32[32,32,128]{2,1,0:T(8,128)}, u32[]{:S(2)}) copy-start(f32[32,32,128]{2,1,0:T(8,128)} %obs_ref.1) | copy-start | bytes 1572868
  0.6 23.4 %copy-start = (f32[32,32,128]{2,1,0:T(8,128)S(1)}, f32[32,32,128]{2,1,0:T(8,128)}, u32[]{:S(2)}) copy-start(f32[32,32,128]{2,1,0:T(8,128)} %p0_ref.1) | copy-start | bytes 1572868
  1.7 10.2 %collective-permute-start.3 = (f32[32,16,128]{2,1,0:T(8,128)S(1)}, f32[32,16,128]{2,1,0:T(8,128)S(1)}, u32[]{:S(2)}, u32[]{:S(2)}) collective-permute-start(f32[32,16,128]{2,1,0:T(8,128)S(1)} %bitcast.3), channel_id=1, source_target_pairs={{0,16},{16,0},{32,48},{48,32},{64,80},{80,64},{96,112},{112,96},{1... | collective-permute-start | bytes 786440 | tf_op jit(solution)/shard_map/ppermute | solution.py:29
  2.5 18.4 %collective-permute-start.2 = (f32[32,16,128]{2,1,0:T(8,128)S(1)}, f32[32,16,128]{2,1,0:T(8,128)S(1)}, u32[]{:S(2)}, u32[]{:S(2)}) collective-permute-start(f32[32,16,128]{2,1,0:T(8,128)S(1)} %bitcast.4), channel_id=1, source_target_pairs={{16,32},{32,16},{48,64},{64,48},{80,96},{96,80},{112,128},{128,112... | collective-permute-start | bytes 786440 | tf_op jit(solution)/shard_map/ppermute | solution.py:29
  9.3 14.2 %collective-permute-start.1 = (f32[32,16,128]{2,1,0:T(8,128)S(1)}, f32[32,16,128]{2,1,0:T(8,128)S(1)}, u32[]{:S(2)}, u32[]{:S(2)}) collective-permute-start(f32[32,16,128]{2,1,0:T(8,128)S(1)} %bitcast.5), channel_id=1, source_target_pairs={{1,2},{2,1},{3,4},{4,3},{5,6},{6,5},{7,8},{8,7},{9,10},{10,9},{11,... | collective-permute-start | bytes 786440 | tf_op jit(solution)/shard_map/ppermute | solution.py:29
  11.6 11.9 %collective-permute-start = (f32[32,16,128]{2,1,0:T(8,128)S(1)}, f32[32,16,128]{2,1,0:T(8,128)S(1)}, u32[]{:S(2)}, u32[]{:S(2)}) collective-permute-start(f32[32,16,128]{2,1,0:T(8,128)S(1)} %bitcast.6), channel_id=1, source_target_pairs={{0,1},{1,0},{2,3},{3,2},{4,5},{5,4},{6,7},{7,6},{8,9},{9,8},{10,11... | collective-permute-start | bytes 786440 | tf_op jit(solution)/shard_map/ppermute | solution.py:29
  20.9 9.2 %collective-permute-start.5 = (f32[32,16,128]{2,1,0:T(8,128)S(1)}, f32[32,16,128]{2,1,0:T(8,128)S(1)}, u32[]{:S(2)}, u32[]{:S(2)}) collective-permute-start(f32[32,16,128]{2,1,0:T(8,128)S(1)} %onward.1), channel_id=1, source_target_pairs={{1,2},{2,1},{3,4},{4,3},{5,6},{6,5},{7,8},{8,7},{9,10},{10,9},{11,... | collective-permute-start | bytes 786440 | tf_op jit(solution)/shard_map/ppermute | solution.py:29
  22.8 7.3 %collective-permute-start.4 = (f32[32,16,128]{2,1,0:T(8,128)S(1)}, f32[32,16,128]{2,1,0:T(8,128)S(1)}, u32[]{:S(2)}, u32[]{:S(2)}) collective-permute-start(f32[32,16,128]{2,1,0:T(8,128)S(1)} %onward.1), channel_id=1, source_target_pairs={{0,1},{1,0},{2,3},{3,2},{4,5},{5,4},{6,7},{7,6},{8,9},{9,8},{10,11... | collective-permute-start | bytes 786440 | tf_op jit(solution)/shard_map/ppermute | solution.py:29
  23.5 6.6 %collective-permute-start.7 = (f32[32,16,128]{2,1,0:T(8,128)S(1)}, f32[32,16,128]{2,1,0:T(8,128)S(1)}, u32[]{:S(2)}, u32[]{:S(2)}) collective-permute-start(f32[32,16,128]{2,1,0:T(8,128)S(1)} %collective-permute-done.1.yo_ref), channel_id=1, source_target_pairs={{0,16},{16,0},{32,48},{48,32},{64,80},{80,64},{96,112},{112,96},{1... | collective-permute-start | bytes 786440 | tf_op jit(solution)/shard_map/ppermute | solution.py:29
  23.5 6.6 %collective-permute-start.6 = (f32[32,16,128]{2,1,0:T(8,128)S(1)}, f32[32,16,128]{2,1,0:T(8,128)S(1)}, u32[]{:S(2)}, u32[]{:S(2)}) collective-permute-start(f32[32,16,128]{2,1,0:T(8,128)S(1)} %collective-permute-done.ye_ref), channel_id=1, source_target_pairs={{0,16},{16,0},{32,48},{48,32},{64,80},{80,64},{96,112},{112,96},{1... | collective-permute-start | bytes 786440 | tf_op jit(solution)/shard_map/ppermute | solution.py:29
  24.1 0.7 copy-start.2
  34.4 7.7 %collective-permute-start.9 = (f32[32,48,128]{2,1,0:T(8,128)S(1)}, f32[32,48,128]{2,1,0:T(8,128)S(1)}, u32[]{:S(2)}, u32[]{:S(2)}) collective-permute-start(f32[32,48,128]{2,1,0:T(8,128)S(1)} %get-tuple-element.27), channel_id=1, source_target_pairs={{0,16},{16,0},{32,48},{48,32},{64,80},{80,64},{96,112},{112,96},{1... | collective-permute-start | bytes 2359304 | tf_op jit(solution)/shard_map/ppermute | solution.py:29
  34.5 7.6 %collective-permute-start.8 = (f32[32,16,128]{2,1,0:T(8,128)S(1)}, f32[32,16,128]{2,1,0:T(8,128)S(1)}, u32[]{:S(2)}, u32[]{:S(2)}) collective-permute-start(f32[32,16,128]{2,1,0:T(8,128)S(1)} %get-tuple-element.26), channel_id=1, source_target_pairs={{0,1},{1,0},{2,3},{3,2},{4,5},{5,4},{6,7},{7,6},{8,9},{9,8},{10,11... | collective-permute-start | bytes 786440 | tf_op jit(solution)/shard_map/ppermute | solution.py:29
  34.6 11.5 %collective-permute-start.10 = (f32[32,16,128]{2,1,0:T(8,128)S(1)}, f32[32,16,128]{2,1,0:T(8,128)S(1)}, u32[]{:S(2)}, u32[]{:S(2)}) collective-permute-start(f32[32,16,128]{2,1,0:T(8,128)S(1)} %get-tuple-element.33), channel_id=1, source_target_pairs={{1,2},{2,1},{3,4},{4,3},{5,6},{6,5},{7,8},{8,7},{9,10},{10,9},{11,... | collective-permute-start | bytes 786440 | tf_op jit(solution)/shard_map/ppermute | solution.py:29
  42.1 23.5 %collective-permute-start.13 = (f32[33,16,128]{2,1,0:T(8,128)S(1)}, f32[33,16,128]{2,1,0:T(8,128)S(1)}, u32[]{:S(2)}, u32[]{:S(2)}) collective-permute-start(f32[33,16,128]{2,1,0:T(8,128)S(1)} %get-tuple-element.37), channel_id=1, source_target_pairs={{1,2},{2,1},{3,4},{4,3},{5,6},{6,5},{7,8},{8,7},{9,10},{10,9},{11,... | collective-permute-start | bytes 811016 | tf_op jit(solution)/shard_map/ppermute | solution.py:29
  46.1 19.5 %collective-permute-start.11 = (f32[32,16,128]{2,1,0:T(8,128)S(1)}, f32[32,16,128]{2,1,0:T(8,128)S(1)}, u32[]{:S(2)}, u32[]{:S(2)}) collective-permute-start(f32[32,16,128]{2,1,0:T(8,128)S(1)} %get-tuple-element.35), channel_id=1, source_target_pairs={{16,32},{32,16},{48,64},{64,48},{80,96},{96,80},{112,128},{128,112... | collective-permute-start | bytes 786440 | tf_op jit(solution)/shard_map/ppermute | solution.py:29
  56.3 9.3 %collective-permute-start.12 = (f32[32,16,128]{2,1,0:T(8,128)S(1)}, f32[32,16,128]{2,1,0:T(8,128)S(1)}, u32[]{:S(2)}, u32[]{:S(2)}) collective-permute-start(f32[32,16,128]{2,1,0:T(8,128)S(1)} %get-tuple-element.36), channel_id=1, source_target_pairs={{0,1},{1,0},{2,3},{3,2},{4,5},{5,4},{6,7},{7,6},{8,9},{9,8},{10,11... | collective-permute-start | bytes 786440 | tf_op jit(solution)/shard_map/ppermute | solution.py:29

commit v3 on v2

--- a/solution.py
+++ b/solution.py
@@ -128,7 +128,7 @@
 
 def wave_kernel(
     field0, g1, wide, deep, obs_ref, corner_vmem, own_ref, ye_ref, yo_ref, x_ref, c_ref, ye2_ref, yo2_ref, cye_ref, cyo_ref,
-    c_out, xe_out, xo_out, xm_out, oe_out, oo_out, om_out,
+    ce_out, co_out, cm_out, xe_out, xo_out, xm_out, oe_out, oo_out, om_out,
     corner_ref, sem, model, terms, field, bx, by, bz, gs, a1, a2, lam, kap, buoy, quad,
 ):
     corner_copy = pltpu.make_async_copy(corner_vmem, corner_ref, sem)
@@ -244,16 +244,21 @@
 
     for f in range(2):
         rows = slice(f * BLOCK, (f + 1) * BLOCK)
-        c_out[rows] = terms[f, pl.ds(row_c, BLOCK)]
+        ce_out[rows] = terms[f, pl.ds(row_c, BLOCK), pl.ds(col_e, BLOCK)]
+        co_out[rows] = terms[f, pl.ds(row_c, BLOCK), pl.ds(col_o, BLOCK)]
+        cm_out[rows] = terms[f, pl.ds(row_c, BLOCK), middle]
         xe_out[rows] = terms[f, pl.ds(row_x, BLOCK), pl.ds(col_e, BLOCK)]
         xo_out[rows] = terms[f, pl.ds(row_x, BLOCK), pl.ds(col_o, BLOCK)]
         xm_out[rows] = terms[f, pl.ds(row_x, BLOCK), middle]
         oe_out[rows] = terms[f, middle, pl.ds(col_e, BLOCK)]
         oo_out[rows] = terms[f, middle, pl.ds(col_o, BLOCK)]
         om_out[rows] = terms[f, middle, middle]
+    for out_ref in (xe_out, xo_out):
+        out_ref[2 * BLOCK :] = jnp.zeros((2 * EXTRA, BLOCK, NZ), F32)
 
 
 part = jax.ShapeDtypeStruct((2 * BLOCK, BLOCK, NZ), F32)
+early_part = jax.ShapeDtypeStruct((2 * BLOCK + 2 * EXTRA, BLOCK, NZ), F32)
 
 
 def wave(begun, *blocks):
@@ -261,9 +266,9 @@
     padded = pltpu.VMEM((APER + 8, APER, NZ), F32)
     return pl.pallas_call(
         wave_kernel,
-        out_shape=(jax.ShapeDtypeStruct((2 * BLOCK, 3 * BLOCK, NZ), F32),) + (part,) * 6,
+        out_shape=(part,) * 3 + (early_part,) * 2 + (part,) * 4,
         in_specs=vmem(15),
-        out_specs=tuple(vmem(7)),
+        out_specs=tuple(vmem(9)),
         scratch_shapes=[
             pltpu.SMEM((8, NZ), jnp.int32),
             pltpu.SemaphoreType.DMA,
@@ -294,47 +299,42 @@
     )(x, c)
 
 
-def merge_kernel(first_ref, c_ref, oe_ref, oo_ref, om_ref, oe_out, oo_out, om_out):
-    del first_ref
-    oe_out[...] = oe_ref[...] + c_ref[:, pl.ds(side("shot", False), BLOCK)]
-    oo_out[: 2 * BLOCK] = oo_ref[...] + c_ref[:, pl.ds(side("shot", True), BLOCK)]
-    oo_out[2 * BLOCK :] = jnp.zeros((EXTRA, BLOCK, NZ), F32)
-    om_out[...] = om_ref[...] + c_ref[:, BLOCK : 2 * BLOCK]
-
-
-def merge(first, c, oe, oo, om):
+def merge_kernel(c_ref, o_ref, out_ref):
+    out_ref[: 2 * BLOCK] = o_ref[...] + c_ref[...]
+    out_ref[2 * BLOCK :] = jnp.zeros((EXTRA, BLOCK, NZ), F32)
+
+
+def merge(c, o):
     return pl.pallas_call(
         merge_kernel,
-        out_shape=(part, jax.ShapeDtypeStruct((2 * BLOCK + EXTRA, BLOCK, NZ), F32), part),
-        in_specs=[pl.BlockSpec(memory_space=pl.ANY)] + vmem(4),
-        out_specs=tuple(vmem(3)),
+        out_shape=jax.ShapeDtypeStruct((2 * BLOCK + EXTRA, BLOCK, NZ), F32),
+        in_specs=vmem(2),
+        out_specs=vmem(1)[0],
         compiler_params=small,
         name="merge",
-    )(first, c, oe, oo, om)
-
-
-def combine_kernel(m_ref, e_ref, o_ref, oe_ref, out_ref, oe_out):
-    del oe_ref, oe_out
-    out_ref[...] = m_ref[...] + e_ref[...] + o_ref[...]
-
-
-def combine(m, e, o, oe):
-    place = pl.BlockSpec(memory_space=pl.ANY)
+    )(c, o)
+
+
+def combine_kernel(m_ref, e_ref, o_ref, c_ref, oe_ref, out_ref, oe_out):
+    out_ref[...] = m_ref[...] + e_ref[: 2 * BLOCK] + o_ref[: 2 * BLOCK]
+    oe_out[...] = oe_ref[...] + c_ref[...]
+
+
+def combine(m, e, o, c, oe):
     return pl.pallas_call(
         combine_kernel,
         out_shape=(part, part),
-        in_specs=vmem(3) + [place],
-        out_specs=(vmem(1)[0], place),
-        input_output_aliases={3: 1},
+        in_specs=vmem(5),
+        out_specs=tuple(vmem(2)),
         compiler_params=small,
         name="combine",
-    )(m, e, o, oe)
-
-
-def total_kernel(own_ref, x_ref, e_ref, o_ref, vel_ref, rho_ref):
+    )(m, e, o, c, oe)
+
+
+def total_kernel(own_ref, c_ref, x_ref, e_ref, o_ref, vel_ref, rho_ref):
     for f, out_ref in ((0, vel_ref), (1, rho_ref)):
         rows = slice(f * BLOCK, (f + 1) * BLOCK)
-        out_ref[...] = (own_ref[rows] + x_ref[rows]) + (e_ref[rows] + o_ref[rows])
+        out_ref[...] = ((own_ref[rows] + c_ref[rows]) + x_ref[rows]) + (e_ref[rows] + o_ref[rows])
 
 
 def total(*parts):
@@ -342,7 +342,7 @@
     return pl.pallas_call(
         total_kernel,
         out_shape=(block, block),
-        in_specs=vmem(4),
+        in_specs=vmem(5),
         out_specs=tuple(vmem(2)),
         compiler_params=small,
         name="total",
@@ -361,16 +361,15 @@
     ye2 = swap(passed, "shot", False)
     cyo = swap(yo, "line", False)
     cye = swap(ye, "line", False)
-    to_core, xe, xo, xm, oe, oo, om = wave(begun, own, ye, yo, x, c, ye2, yo2, cye, cyo)
-    to_core = swap(to_core, "line", False)
+    ce, co, cm, xe, xo, xm, oe, oo, om = wave(begun, own, ye, yo, x, c, ye2, yo2, cye, cyo)
     xo = swap(xo, "shot", True)
     xe = swap(xe, "shot", False)
-    oe, oo, om = merge(xe, to_core, oe, oo, om)
-    oo = swap(oo, "shot", True)
-    xm, oe = combine(xm, xe, xo, oe)
+    ce, co, cm = (swap(block, "line", False) for block in (ce, co, cm))
+    oo = swap(merge(co, oo), "shot", True)
+    xm, oe = combine(xm, xe, xo, ce, oe)
     xm = swap(xm, "line", True)
     oe = swap(oe, "shot", False)
-    return total(om, xm, oe, oo)
+    return total(om, cm, xm, oe, oo)
 
 
 def solution(mesh):

time: 67.5 us -> 64.8 us (0.960)
  waiting for transfers between devices: 27.4 us -> 23.8 us
  starting transfers between devices: 30 us -> 30.9 us
    ppermute x14 -> x16, waiting for transfers between devices: 27.4 us -> 23.8 us  [swap(): return lax.ppermute(block, axis, swap_pairs(odd))]
    ppermute x14 -> x16, starting transfers between devices: 30 us -> 30.9 us  [swap(): return lax.ppermute(block, axis, swap_pairs(odd))]
  transfers between devices with their start and end apart: 14 -> 16, of which waited for: 6 -> 6; matrix products, arithmetic and copies ran while one was open for 0% -> 0% of each run, Pallas kernels for 2% -> 2%
where the time goes in v3:
time: 64.8 us; the launch traced here: 63.7 us
  starting transfers between devices  30.9 us (48%)
  waiting for transfers between devices  23.8 us (37%)
  Pallas kernels  6.45 us (10%)
  other arithmetic  1.07 us (2%)
  between operations  0.79 us (1%)
  local copies, waits for them, and re-layouts  0.66 us (1%)
    ppermute x16, starting transfers between devices, swap(): return lax.ppermute(block, axis, swap_pairs(odd))  30.9 us
    ppermute x16, waiting for transfers between devices, swap(): return lax.ppermute(block, axis, swap_pairs(odd))  23.8 us
    pallas_call x1, Pallas kernels, wave(): pl.pallas_call(wave_kernel, out_shape=(part,) * 3 + (early_part,) * 2 + (...  4.23 us
    pallas_call x1, Pallas kernels, early(): pl.pallas_call(early_kernel, out_shape=(jax.ShapeDtypeStruct((APER + 8, A...  1.32 us
  transfers between devices with their start and end apart: 16, of which 6 were waited for; matrix products, arithmetic and copies ran while one was open for 0% of the time, Pallas kernels for 2%

profile of v3, /device:TPU:95, one launch (start us, length us, event | category | flops | bytes accessed | tf_op | source)
XLA Modules:
  0.0 63.7 jit_solution(15508181038727099125)
XLA Ops:
  0.6 0.0 copy-start.1
  0.6 0.0 copy-start
  0.7 1.1 %pad_maximum_fusion = f32[2,16,16,128]{3,2,1,0:T(8,128)S(1)} fusion(f32[1,16,16,128]{3,2,1,0:T(8,128)} %bitcast.8, f32[1,16,16,128]{3,2,1,0:T(8,128)} %bitcast.9), kind=kLoop, calls=%fused_computation | loop fusion | flops 65536 | bytes 524288 | tf_op jit(solution)/shard_map/stack | solution.py:353
  1.7 0.8 %collective-permute-start.3 = (f32[32,16,128]{2,1,0:T(8,128)S(1)}, f32[32,16,128]{2,1,0:T(8,128)S(1)}, u32[]{:S(2)}, u32[]{:S(2)}) collective-permute-start(f32[32,16,128]{2,1,0:T(8,128)S(1)} %bitcast.3), channel_id=1, source_target_pairs={{0,16},{16,0},{32,48},{48,32},{64,80},{80,64},{96,112},{112,96},{1... | collective-permute-start | bytes 786440 | tf_op jit(solution)/shard_map/ppermute | solution.py:29
  2.5 6.8 %collective-permute-start.2 = (f32[32,16,128]{2,1,0:T(8,128)S(1)}, f32[32,16,128]{2,1,0:T(8,128)S(1)}, u32[]{:S(2)}, u32[]{:S(2)}) collective-permute-start(f32[32,16,128]{2,1,0:T(8,128)S(1)} %bitcast.4), channel_id=1, source_target_pairs={{16,32},{32,16},{48,64},{64,48},{80,96},{96,80},{112,128},{128,112... | collective-permute-start | bytes 786440 | tf_op jit(solution)/shard_map/ppermute | solution.py:29
  9.3 2.3 %collective-permute-start.1 = (f32[32,16,128]{2,1,0:T(8,128)S(1)}, f32[32,16,128]{2,1,0:T(8,128)S(1)}, u32[]{:S(2)}, u32[]{:S(2)}) collective-permute-start(f32[32,16,128]{2,1,0:T(8,128)S(1)} %bitcast.5), channel_id=1, source_target_pairs={{1,2},{2,1},{3,4},{4,3},{5,6},{6,5},{7,8},{8,7},{9,10},{10,9},{11,... | collective-permute-start | bytes 786440 | tf_op jit(solution)/shard_map/ppermute | solution.py:29
  11.6 0.3 collective-permute-start
  12.0 0.0 collective-permute-done.3.c_ref
  12.0 8.9 %collective-permute-done.2.x_ref = f32[32,16,128]{2,1,0:T(8,128)S(1)} collective-permute-done((f32[32,16,128]{2,1,0:T(8,128)S(1)}, f32[32,16,128]{2,1,0:T(8,128)S(1)}, u32[]{:S(2)}, u32[]{:S(2)}) %collective-permute-start.2) | collective-permute-done | bytes 262176 | tf_op jit(solution)/shard_map/ppermute | solution.py:29
  20.9 1.9 %collective-permute-start.5 = (f32[32,16,128]{2,1,0:T(8,128)S(1)}, f32[32,16,128]{2,1,0:T(8,128)S(1)}, u32[]{:S(2)}, u32[]{:S(2)}) collective-permute-start(f32[32,16,128]{2,1,0:T(8,128)S(1)} %onward.1), channel_id=1, source_target_pairs={{1,2},{2,1},{3,4},{4,3},{5,6},{6,5},{7,8},{8,7},{9,10},{10,9},{11,... | collective-permute-start | bytes 786440 | tf_op jit(solution)/shard_map/ppermute | solution.py:29
  22.8 0.1 collective-permute-start.4
  22.9 0.6 collective-permute-done.1.yo_ref
  23.5 0.0 collective-permute-start.7
  23.5 0.0 collective-permute-done.ye_ref
  23.5 0.5 collective-permute-start.6
  24.1 0.0 copy-done.1
  24.1 0.0 copy-done
  24.1 0.0 copy-start.2
  24.1 0.7 %copy-done.2 = s32[1,1,2]{2,1,0:T(1,128)S(1)} copy-done((s32[1,1,2]{2,1,0:T(1,128)S(1)}, s32[1,1,2]{2,1,0:T(1,128)}, u32[]{:S(2)}) %copy-start.2) | copy-done | bytes 32
  24.7 1.3 %early.1 = (f32[40,32,128]{2,1,0:T(8,128)S(1)}, f32[3,32,32,128]{3,2,1,0:T(8,128)S(1)}, bf16[2,256,256]{2,1,0:T(8,128)(2,1)S(1)}, bf16[2,256,128]{2,1,0:T(8,128)...) custom-call(s32[1,1,2]{2,1,0:T(1,128)S(1)} %copy-done.2, f32[32,32,128]{2,1,0:T(8,128)S(1)} %copy-done, ...), custom_call_target="tpu_custom_call" | custom-call | tf_op jit(solution)/shard_map/early/pallas_call | solution.py:112
  26.0 4.1 %collective-permute-done.5.yo2_ref = f32[32,16,128]{2,1,0:T(8,128)S(1)} collective-permute-done((f32[32,16,128]{2,1,0:T(8,128)S(1)}, f32[32,16,128]{2,1,0:T(8,128)S(1)}, u32[]{:S(2)}, u32[]{:S(2)}) %collective-permute-start.5) | collective-permute-done | bytes 262176 | tf_op jit(solution)/shard_map/ppermute | solution.py:29
  30.1 0.0 collective-permute-done.4.ye2_ref
  30.1 0.0 collective-permute-done.7.cyo_ref
  30.1 0.0 collective-permute-done.6.cye_ref
  30.1 4.2 %wave.1 = (f32[32,16,128]{2,1,0:T(8,128)S(1)}, f32[32,16,128]{2,1,0:T(8,128)S(1)}, f32[32,16,128]{2,1,0:T(8,128)S(1)}, f32[34,16,128]{2,1,0:T(8,128)S(1)}, f32[3...) custom-call(f32[40,32,128]{2,1,0:T(8,128)S(1)} %get-tuple-element.19, ...), custom_call_target="tpu_custom_call" | custom-call | tf_op jit(solution)/shard_map/wave/pallas_call | solution.py:267
  34.4 0.1 collective-permute-start.9
  34.5 3.4 %collective-permute-start.10 = (f32[34,16,128]{2,1,0:T(8,128)S(1)}, f32[34,16,128]{2,1,0:T(8,128)S(1)}, u32[]{:S(2)}, u32[]{:S(2)}) collective-permute-start(f32[34,16,128]{2,1,0:T(8,128)S(1)} %get-tuple-element.29), channel_id=1, source_target_pairs={{1,2},{2,1},{3,4},{4,3},{5,6},{6,5},{7,8},{8,7},{9,10},{10,9},{11,... | collective-permute-start | bytes 835592 | tf_op jit(solution)/shard_map/ppermute | solution.py:29
  37.8 0.1 collective-permute-start.14
  37.9 0.5 collective-permute-start.11
  38.4 1.0 %collective-permute-done.14.c_ref = f32[32,16,128]{2,1,0:T(8,128)S(1)} collective-permute-done((f32[32,16,128]{2,1,0:T(8,128)S(1)}, f32[32,16,128]{2,1,0:T(8,128)S(1)}, u32[]{:S(2)}, u32[]{:S(2)}) %collective-permute-start.14) | collective-permute-done | bytes 262176 | tf_op jit(solution)/shard_map/ppermute | solution.py:29
  39.5 4.0 %collective-permute-start.15 = (f32[33,16,128]{2,1,0:T(8,128)S(1)}, f32[33,16,128]{2,1,0:T(8,128)S(1)}, u32[]{:S(2)}, u32[]{:S(2)}) collective-permute-start(f32[33,16,128]{2,1,0:T(8,128)S(1)} %merge.1), channel_id=1, source_target_pairs={{1,2},{2,1},{3,4},{4,3},{5,6},{6,5},{7,8},{8,7},{9,10},{10,9},{11,... | collective-permute-start | bytes 811016 | tf_op jit(solution)/shard_map/ppermute | solution.py:29
  43.5 0.5 collective-permute-start.8
  44.0 0.0 collective-permute-done.11.c_ref
  44.0 0.0 collective-permute-done.9.e_ref
  44.0 0.4 collective-permute-done.10.o_ref
  44.4 0.1 combine.1
  44.5 9.5 %collective-permute-start.12 = (f32[32,16,128]{2,1,0:T(8,128)S(1)}, f32[32,16,128]{2,1,0:T(8,128)S(1)}, u32[]{:S(2)}, u32[]{:S(2)}) collective-permute-start(f32[32,16,128]{2,1,0:T(8,128)S(1)} %get-tuple-element.32), channel_id=1, source_target_pairs={{16,32},{32,16},{48,64},{64,48},{80,96},{96,80},{112,128},{128,112... | collective-permute-start | bytes 786440 | tf_op jit(solution)/shard_map/ppermute | solution.py:29
  54.0 0.1 collective-permute-start.13
  54.1 0.0 collective-permute-done.8.c_ref
  54.1 0.0 collective-permute-done.15.o_ref
  54.1 8.8 %collective-permute-done.12.x_ref = f32[32,16,128]{2,1,0:T(8,128)S(1)} collective-permute-done((f32[32,16,128]{2,1,0:T(8,128)S(1)}, f32[32,16,128]{2,1,0:T(8,128)S(1)}, u32[]{:S(2)}, u32[]{:S(2)}) %collective-permute-start.12) | collective-permute-done | bytes 262176 | tf_op jit(solution)/shard_map/ppermute | solution.py:29
  62.9 0.0 collective-permute-done.13.e_ref
  62.9 0.8 %total.1 = (f32[16,16,128]{2,1,0:T(8,128)}, f32[16,16,128]{2,1,0:T(8,128)}) custom-call(f32[32,16,128]{2,1,0:T(8,128)S(1)} %get-tuple-element.25.own_ref, f32[32,16,128]{2,1,0:T(8,128)S(1)} %collective-permute-done.8.c_ref, f32[32,16,128]{2,1,0:T(8,128)S(1)} %collective-permute-done.12.x_ref, f32[32,16,128]{2,1,0:T(8,128)S(1)} %collective-permute-done.13.e_ref, ...), custom_call_target="tpu_custom_call" | custom-call | tf_op jit(solution)/shard_map/total/pallas_call | solution.py:342
  (2 shorter events, 0.0 us)
Async XLA Ops:
  0.6 23.4 %copy-start.1 = (f32[32,32,128]{2,1,0:T(8,128)S(1)}, f32[32,32,128]{2,1,0:T(8,128)}, u32[]{:S(2)}) copy-start(f32[32,32,128]{2,1,0:T(8,128)} %obs_ref.1) | copy-start | bytes 1572868
  0.6 23.4 %copy-start = (f32[32,32,128]{2,1,0:T(8,128)S(1)}, f32[32,32,128]{2,1,0:T(8,128)}, u32[]{:S(2)}) copy-start(f32[32,32,128]{2,1,0:T(8,128)} %p0_ref.1) | copy-start | bytes 1572868
  1.7 10.2 %collective-permute-start.3 = (f32[32,16,128]{2,1,0:T(8,128)S(1)}, f32[32,16,128]{2,1,0:T(8,128)S(1)}, u32[]{:S(2)}, u32[]{:S(2)}) collective-permute-start(f32[32,16,128]{2,1,0:T(8,128)S(1)} %bitcast.3), channel_id=1, source_target_pairs={{0,16},{16,0},{32,48},{48,32},{64,80},{80,64},{96,112},{112,96},{1... | collective-permute-start | bytes 786440 | tf_op jit(solution)/shard_map/ppermute | solution.py:29
  2.5 18.4 %collective-permute-start.2 = (f32[32,16,128]{2,1,0:T(8,128)S(1)}, f32[32,16,128]{2,1,0:T(8,128)S(1)}, u32[]{:S(2)}, u32[]{:S(2)}) collective-permute-start(f32[32,16,128]{2,1,0:T(8,128)S(1)} %bitcast.4), channel_id=1, source_target_pairs={{16,32},{32,16},{48,64},{64,48},{80,96},{96,80},{112,128},{128,112... | collective-permute-start | bytes 786440 | tf_op jit(solution)/shard_map/ppermute | solution.py:29
  9.3 14.2 %collective-permute-start.1 = (f32[32,16,128]{2,1,0:T(8,128)S(1)}, f32[32,16,128]{2,1,0:T(8,128)S(1)}, u32[]{:S(2)}, u32[]{:S(2)}) collective-permute-start(f32[32,16,128]{2,1,0:T(8,128)S(1)} %bitcast.5), channel_id=1, source_target_pairs={{1,2},{2,1},{3,4},{4,3},{5,6},{6,5},{7,8},{8,7},{9,10},{10,9},{11,... | collective-permute-start | bytes 786440 | tf_op jit(solution)/shard_map/ppermute | solution.py:29
  11.6 11.9 %collective-permute-start = (f32[32,16,128]{2,1,0:T(8,128)S(1)}, f32[32,16,128]{2,1,0:T(8,128)S(1)}, u32[]{:S(2)}, u32[]{:S(2)}) collective-permute-start(f32[32,16,128]{2,1,0:T(8,128)S(1)} %bitcast.6), channel_id=1, source_target_pairs={{0,1},{1,0},{2,3},{3,2},{4,5},{5,4},{6,7},{7,6},{8,9},{9,8},{10,11... | collective-permute-start | bytes 786440 | tf_op jit(solution)/shard_map/ppermute | solution.py:29
  20.9 9.2 %collective-permute-start.5 = (f32[32,16,128]{2,1,0:T(8,128)S(1)}, f32[32,16,128]{2,1,0:T(8,128)S(1)}, u32[]{:S(2)}, u32[]{:S(2)}) collective-permute-start(f32[32,16,128]{2,1,0:T(8,128)S(1)} %onward.1), channel_id=1, source_target_pairs={{1,2},{2,1},{3,4},{4,3},{5,6},{6,5},{7,8},{8,7},{9,10},{10,9},{11,... | collective-permute-start | bytes 786440 | tf_op jit(solution)/shard_map/ppermute | solution.py:29
  22.8 7.3 %collective-permute-start.4 = (f32[32,16,128]{2,1,0:T(8,128)S(1)}, f32[32,16,128]{2,1,0:T(8,128)S(1)}, u32[]{:S(2)}, u32[]{:S(2)}) collective-permute-start(f32[32,16,128]{2,1,0:T(8,128)S(1)} %onward.1), channel_id=1, source_target_pairs={{0,1},{1,0},{2,3},{3,2},{4,5},{5,4},{6,7},{7,6},{8,9},{9,8},{10,11... | collective-permute-start | bytes 786440 | tf_op jit(solution)/shard_map/ppermute | solution.py:29
  23.5 6.6 %collective-permute-start.7 = (f32[32,16,128]{2,1,0:T(8,128)S(1)}, f32[32,16,128]{2,1,0:T(8,128)S(1)}, u32[]{:S(2)}, u32[]{:S(2)}) collective-permute-start(f32[32,16,128]{2,1,0:T(8,128)S(1)} %collective-permute-done.1.yo_ref), channel_id=1, source_target_pairs={{0,16},{16,0},{32,48},{48,32},{64,80},{80,64},{96,112},{112,96},{1... | collective-permute-start | bytes 786440 | tf_op jit(solution)/shard_map/ppermute | solution.py:29
  23.5 6.6 %collective-permute-start.6 = (f32[32,16,128]{2,1,0:T(8,128)S(1)}, f32[32,16,128]{2,1,0:T(8,128)S(1)}, u32[]{:S(2)}, u32[]{:S(2)}) collective-permute-start(f32[32,16,128]{2,1,0:T(8,128)S(1)} %collective-permute-done.ye_ref), channel_id=1, source_target_pairs={{0,16},{16,0},{32,48},{48,32},{64,80},{80,64},{96,112},{112,96},{1... | collective-permute-start | bytes 786440 | tf_op jit(solution)/shard_map/ppermute | solution.py:29
  24.1 0.7 %copy-start.2 = (s32[1,1,2]{2,1,0:T(1,128)S(1)}, s32[1,1,2]{2,1,0:T(1,128)}, u32[]{:S(2)}) copy-start(s32[1,1,2]{2,1,0:T(1,128)} %corner_ref.1) | copy-start | bytes 28
  34.4 9.7 %collective-permute-start.9 = (f32[34,16,128]{2,1,0:T(8,128)S(1)}, f32[34,16,128]{2,1,0:T(8,128)S(1)}, u32[]{:S(2)}, u32[]{:S(2)}) collective-permute-start(f32[34,16,128]{2,1,0:T(8,128)S(1)} %get-tuple-element.28), channel_id=1, source_target_pairs={{0,1},{1,0},{2,3},{3,2},{4,5},{5,4},{6,7},{7,6},{8,9},{9,8},{10,11... | collective-permute-start | bytes 835592 | tf_op jit(solution)/shard_map/ppermute | solution.py:29
  34.5 10.0 %collective-permute-start.10 = (f32[34,16,128]{2,1,0:T(8,128)S(1)}, f32[34,16,128]{2,1,0:T(8,128)S(1)}, u32[]{:S(2)}, u32[]{:S(2)}) collective-permute-start(f32[34,16,128]{2,1,0:T(8,128)S(1)} %get-tuple-element.29), channel_id=1, source_target_pairs={{1,2},{2,1},{3,4},{4,3},{5,6},{6,5},{7,8},{8,7},{9,10},{10,9},{11,... | collective-permute-start | bytes 835592 | tf_op jit(solution)/shard_map/ppermute | solution.py:29
  37.8 1.6 %collective-permute-start.14 = (f32[32,16,128]{2,1,0:T(8,128)S(1)}, f32[32,16,128]{2,1,0:T(8,128)S(1)}, u32[]{:S(2)}, u32[]{:S(2)}) collective-permute-start(f32[32,16,128]{2,1,0:T(8,128)S(1)} %get-tuple-element.34), channel_id=1, source_target_pairs={{0,16},{16,0},{32,48},{48,32},{64,80},{80,64},{96,112},{112,96},{1... | collective-permute-start | bytes 786440 | tf_op jit(solution)/shard_map/ppermute | solution.py:29
  37.9 6.1 %collective-permute-start.11 = (f32[32,16,128]{2,1,0:T(8,128)S(1)}, f32[32,16,128]{2,1,0:T(8,128)S(1)}, u32[]{:S(2)}, u32[]{:S(2)}) collective-permute-start(f32[32,16,128]{2,1,0:T(8,128)S(1)} %get-tuple-element.30), channel_id=1, source_target_pairs={{0,16},{16,0},{32,48},{48,32},{64,80},{80,64},{96,112},{112,96},{1... | collective-permute-start | bytes 786440 | tf_op jit(solution)/shard_map/ppermute | solution.py:29
  39.5 14.6 %collective-permute-start.15 = (f32[33,16,128]{2,1,0:T(8,128)S(1)}, f32[33,16,128]{2,1,0:T(8,128)S(1)}, u32[]{:S(2)}, u32[]{:S(2)}) collective-permute-start(f32[33,16,128]{2,1,0:T(8,128)S(1)} %merge.1), channel_id=1, source_target_pairs={{1,2},{2,1},{3,4},{4,3},{5,6},{6,5},{7,8},{8,7},{9,10},{10,9},{11,... | collective-permute-start | bytes 811016 | tf_op jit(solution)/shard_map/ppermute | solution.py:29
  43.5 10.6 %collective-permute-start.8 = (f32[32,16,128]{2,1,0:T(8,128)S(1)}, f32[32,16,128]{2,1,0:T(8,128)S(1)}, u32[]{:S(2)}, u32[]{:S(2)}) collective-permute-start(f32[32,16,128]{2,1,0:T(8,128)S(1)} %get-tuple-element.26), channel_id=1, source_target_pairs={{0,16},{16,0},{32,48},{48,32},{64,80},{80,64},{96,112},{112,96},{1... | collective-permute-start | bytes 786440 | tf_op jit(solution)/shard_map/ppermute | solution.py:29
  44.5 18.4 %collective-permute-start.12 = (f32[32,16,128]{2,1,0:T(8,128)S(1)}, f32[32,16,128]{2,1,0:T(8,128)S(1)}, u32[]{:S(2)}, u32[]{:S(2)}) collective-permute-start(f32[32,16,128]{2,1,0:T(8,128)S(1)} %get-tuple-element.32), channel_id=1, source_target_pairs={{16,32},{32,16},{48,64},{64,48},{80,96},{96,80},{112,128},{128,112... | collective-permute-start | bytes 786440 | tf_op jit(solution)/shard_map/ppermute | solution.py:29
  54.0 8.9 %collective-permute-start.13 = (f32[32,16,128]{2,1,0:T(8,128)S(1)}, f32[32,16,128]{2,1,0:T(8,128)S(1)}, u32[]{:S(2)}, u32[]{:S(2)}) collective-permute-start(f32[32,16,128]{2,1,0:T(8,128)S(1)} %get-tuple-element.33), channel_id=1, source_target_pairs={{0,1},{1,0},{2,3},{3,2},{4,5},{5,4},{6,7},{7,6},{8,9},{9,8},{10,11... | collective-permute-start | bytes 786440 | tf_op jit(solution)/shard_map/ppermute | solution.py:29

commit v4 on v3

--- a/solution.py
+++ b/solution.py
@@ -127,7 +127,7 @@
 
 
 def wave_kernel(
-    field0, g1, wide, deep, obs_ref, corner_vmem, own_ref, ye_ref, yo_ref, x_ref, c_ref, ye2_ref, yo2_ref, cye_ref, cyo_ref,
+    field0, g1, wide, deep, obs_ref, corner_vmem, own_ref, ye_ref, yo_ref, c_ref, x_ref, ye2_ref, yo2_ref, cye_ref, cyo_ref,
     ce_out, co_out, cm_out, xe_out, xo_out, xm_out, oe_out, oo_out, om_out,
     corner_ref, sem, model, terms, field, bx, by, bz, gs, a1, a2, lam, kap, buoy, quad,
 ):
@@ -361,7 +361,7 @@
     ye2 = swap(passed, "shot", False)
     cyo = swap(yo, "line", False)
     cye = swap(ye, "line", False)
-    ce, co, cm, xe, xo, xm, oe, oo, om = wave(begun, own, ye, yo, x, c, ye2, yo2, cye, cyo)
+    ce, co, cm, xe, xo, xm, oe, oo, om = wave(begun, own, ye, yo, c, x, ye2, yo2, cye, cyo)
     xo = swap(xo, "shot", True)
     xe = swap(xe, "shot", False)
     ce, co, cm = (swap(block, "line", False) for block in (ce, co, cm))

time: 64.8 us -> 62.7 us (0.968); the launches traced: 63.7 us -> 62.4 us
  waiting for transfers between devices: 23.8 us -> 22.7 us
    ppermute x16, waiting for transfers between devices: 23.8 us -> 22.7 us  [swap(): return lax.ppermute(block, axis, swap_pairs(odd))]
where the time goes in v4:
time: 62.7 us; the launch traced here: 62.4 us
  starting transfers between devices  30.8 us (49%)
  waiting for transfers between devices  22.7 us (36%)
  Pallas kernels  6.45 us (10%)
  other arithmetic  1.07 us (2%)
  between operations  0.79 us (1%)
  local copies, waits for them, and re-layouts  0.66 us (1%)
    ppermute x16, starting transfers between devices, swap(): return lax.ppermute(block, axis, swap_pairs(odd))  30.8 us
    ppermute x16, waiting for transfers between devices, swap(): return lax.ppermute(block, axis, swap_pairs(odd))  22.7 us
    pallas_call x1, Pallas kernels, wave(): pl.pallas_call(wave_kernel, out_shape=(part,) * 3 + (early_part,) * 2 + (...  4.23 us
    pallas_call x1, Pallas kernels, early(): pl.pallas_call(early_kernel, out_shape=(jax.ShapeDtypeStruct((APER + 8, A...  1.32 us
  transfers between devices with their start and end apart: 16, of which 6 were waited for; matrix products, arithmetic and copies ran while one was open for 0% of the time, Pallas kernels for 2%

profile of v4, /device:TPU:95, one launch (start us, length us, event | category | flops | bytes accessed | tf_op | source)
XLA Modules:
  0.0 62.4 jit_solution(3696587976580733863)
XLA Ops:
  0.6 0.0 copy-start.1
  0.6 0.0 copy-start
  0.7 1.1 %pad_maximum_fusion = f32[2,16,16,128]{3,2,1,0:T(8,128)S(1)} fusion(f32[1,16,16,128]{3,2,1,0:T(8,128)} %bitcast.8, f32[1,16,16,128]{3,2,1,0:T(8,128)} %bitcast.9), kind=kLoop, calls=%fused_computation | loop fusion | flops 65536 | bytes 524288 | tf_op jit(solution)/shard_map/stack | solution.py:353
  1.7 7.5 %collective-permute-start.3 = (f32[32,16,128]{2,1,0:T(8,128)S(1)}, f32[32,16,128]{2,1,0:T(8,128)S(1)}, u32[]{:S(2)}, u32[]{:S(2)}) collective-permute-start(f32[32,16,128]{2,1,0:T(8,128)S(1)} %bitcast.3), channel_id=1, source_target_pairs={{16,32},{32,16},{48,64},{64,48},{80,96},{96,80},{112,128},{128,112... | collective-permute-start | bytes 786440 | tf_op jit(solution)/shard_map/ppermute | solution.py:29
  9.2 0.1 collective-permute-start.2
  9.3 2.3 %collective-permute-start.1 = (f32[32,16,128]{2,1,0:T(8,128)S(1)}, f32[32,16,128]{2,1,0:T(8,128)S(1)}, u32[]{:S(2)}, u32[]{:S(2)}) collective-permute-start(f32[32,16,128]{2,1,0:T(8,128)S(1)} %bitcast.5), channel_id=1, source_target_pairs={{1,2},{2,1},{3,4},{4,3},{5,6},{6,5},{7,8},{8,7},{9,10},{10,9},{11,... | collective-permute-start | bytes 786440 | tf_op jit(solution)/shard_map/ppermute | solution.py:29
  11.6 0.3 collective-permute-start
  12.0 6.9 %collective-permute-done.3.x_ref = f32[32,16,128]{2,1,0:T(8,128)S(1)} collective-permute-done((f32[32,16,128]{2,1,0:T(8,128)S(1)}, f32[32,16,128]{2,1,0:T(8,128)S(1)}, u32[]{:S(2)}, u32[]{:S(2)}) %collective-permute-start.3) | collective-permute-done | bytes 262176 | tf_op jit(solution)/shard_map/ppermute | solution.py:29
  18.9 0.0 collective-permute-done.2.c_ref
  18.9 1.9 %collective-permute-start.5 = (f32[32,16,128]{2,1,0:T(8,128)S(1)}, f32[32,16,128]{2,1,0:T(8,128)S(1)}, u32[]{:S(2)}, u32[]{:S(2)}) collective-permute-start(f32[32,16,128]{2,1,0:T(8,128)S(1)} %onward.1), channel_id=1, source_target_pairs={{1,2},{2,1},{3,4},{4,3},{5,6},{6,5},{7,8},{8,7},{9,10},{10,9},{11,... | collective-permute-start | bytes 786440 | tf_op jit(solution)/shard_map/ppermute | solution.py:29
  20.8 0.1 collective-permute-start.4
  20.9 1.8 %collective-permute-done.1.yo_ref = f32[32,16,128]{2,1,0:T(8,128)S(1)} collective-permute-done((f32[32,16,128]{2,1,0:T(8,128)S(1)}, f32[32,16,128]{2,1,0:T(8,128)S(1)}, u32[]{:S(2)}, u32[]{:S(2)}) %collective-permute-start.1) | collective-permute-done | bytes 262176 | tf_op jit(solution)/shard_map/ppermute | solution.py:29
  22.7 0.0 collective-permute-start.7
  22.7 0.0 collective-permute-done.ye_ref
  22.7 0.5 collective-permute-start.6
  23.2 0.0 copy-done.1
  23.2 0.0 copy-done
  23.2 0.0 copy-start.2
  23.2 0.7 %copy-done.2 = s32[1,1,2]{2,1,0:T(1,128)S(1)} copy-done((s32[1,1,2]{2,1,0:T(1,128)S(1)}, s32[1,1,2]{2,1,0:T(1,128)}, u32[]{:S(2)}) %copy-start.2) | copy-done | bytes 32
  23.9 1.3 %early.1 = (f32[40,32,128]{2,1,0:T(8,128)S(1)}, f32[3,32,32,128]{3,2,1,0:T(8,128)S(1)}, bf16[2,256,256]{2,1,0:T(8,128)(2,1)S(1)}, bf16[2,256,128]{2,1,0:T(8,128)...) custom-call(s32[1,1,2]{2,1,0:T(1,128)S(1)} %copy-done.2, f32[32,32,128]{2,1,0:T(8,128)S(1)} %copy-done, ...), custom_call_target="tpu_custom_call" | custom-call | tf_op jit(solution)/shard_map/early/pallas_call | solution.py:112
  25.2 2.9 %collective-permute-done.5.yo2_ref = f32[32,16,128]{2,1,0:T(8,128)S(1)} collective-permute-done((f32[32,16,128]{2,1,0:T(8,128)S(1)}, f32[32,16,128]{2,1,0:T(8,128)S(1)}, u32[]{:S(2)}, u32[]{:S(2)}) %collective-permute-start.5) | collective-permute-done | bytes 262176 | tf_op jit(solution)/shard_map/ppermute | solution.py:29
  28.1 0.0 collective-permute-done.4.ye2_ref
  28.1 0.0 collective-permute-done.7.cyo_ref
  28.1 0.0 collective-permute-done.6.cye_ref
  28.1 4.2 %wave.1 = (f32[32,16,128]{2,1,0:T(8,128)S(1)}, f32[32,16,128]{2,1,0:T(8,128)S(1)}, f32[32,16,128]{2,1,0:T(8,128)S(1)}, f32[34,16,128]{2,1,0:T(8,128)S(1)}, f32[3...) custom-call(f32[40,32,128]{2,1,0:T(8,128)S(1)} %get-tuple-element.19, ...), custom_call_target="tpu_custom_call" | custom-call | tf_op jit(solution)/shard_map/wave/pallas_call | solution.py:267
  32.4 0.1 collective-permute-start.9
  32.5 4.3 %collective-permute-start.10 = (f32[34,16,128]{2,1,0:T(8,128)S(1)}, f32[34,16,128]{2,1,0:T(8,128)S(1)}, u32[]{:S(2)}, u32[]{:S(2)}) collective-permute-start(f32[34,16,128]{2,1,0:T(8,128)S(1)} %get-tuple-element.29), channel_id=1, source_target_pairs={{1,2},{2,1},{3,4},{4,3},{5,6},{6,5},{7,8},{8,7},{9,10},{10,9},{11,... | collective-permute-start | bytes 835592 | tf_op jit(solution)/shard_map/ppermute | solution.py:29
  36.8 0.1 collective-permute-start.14
  36.9 0.5 collective-permute-start.11
  37.4 1.0 %collective-permute-done.14.c_ref = f32[32,16,128]{2,1,0:T(8,128)S(1)} collective-permute-done((f32[32,16,128]{2,1,0:T(8,128)S(1)}, f32[32,16,128]{2,1,0:T(8,128)S(1)}, u32[]{:S(2)}, u32[]{:S(2)}) %collective-permute-start.14) | collective-permute-done | bytes 262176 | tf_op jit(solution)/shard_map/ppermute | solution.py:29
  38.4 3.1 %collective-permute-start.15 = (f32[33,16,128]{2,1,0:T(8,128)S(1)}, f32[33,16,128]{2,1,0:T(8,128)S(1)}, u32[]{:S(2)}, u32[]{:S(2)}) collective-permute-start(f32[33,16,128]{2,1,0:T(8,128)S(1)} %merge.1), channel_id=1, source_target_pairs={{1,2},{2,1},{3,4},{4,3},{5,6},{6,5},{7,8},{8,7},{9,10},{10,9},{11,... | collective-permute-start | bytes 811016 | tf_op jit(solution)/shard_map/ppermute | solution.py:29
  41.5 0.5 collective-permute-start.8
  42.1 0.0 collective-permute-done.11.c_ref
  42.1 0.0 collective-permute-done.9.e_ref
  42.1 1.3 %collective-permute-done.10.o_ref = f32[34,16,128]{2,1,0:T(8,128)S(1)} collective-permute-done((f32[34,16,128]{2,1,0:T(8,128)S(1)}, f32[34,16,128]{2,1,0:T(8,128)S(1)}, u32[]{:S(2)}, u32[]{:S(2)}) %collective-permute-start.10) | collective-permute-done | bytes 278560 | tf_op jit(solution)/shard_map/ppermute | solution.py:29
  43.3 0.1 combine.1
  43.4 9.4 %collective-permute-start.12 = (f32[32,16,128]{2,1,0:T(8,128)S(1)}, f32[32,16,128]{2,1,0:T(8,128)S(1)}, u32[]{:S(2)}, u32[]{:S(2)}) collective-permute-start(f32[32,16,128]{2,1,0:T(8,128)S(1)} %get-tuple-element.32), channel_id=1, source_target_pairs={{16,32},{32,16},{48,64},{64,48},{80,96},{96,80},{112,128},{128,112... | collective-permute-start | bytes 786440 | tf_op jit(solution)/shard_map/ppermute | solution.py:29
  52.8 0.1 collective-permute-start.13
  52.9 0.0 collective-permute-done.8.c_ref
  52.9 0.0 collective-permute-done.15.o_ref
  52.9 8.8 %collective-permute-done.12.x_ref = f32[32,16,128]{2,1,0:T(8,128)S(1)} collective-permute-done((f32[32,16,128]{2,1,0:T(8,128)S(1)}, f32[32,16,128]{2,1,0:T(8,128)S(1)}, u32[]{:S(2)}, u32[]{:S(2)}) %collective-permute-start.12) | collective-permute-done | bytes 262176 | tf_op jit(solution)/shard_map/ppermute | solution.py:29
  61.7 0.0 collective-permute-done.13.e_ref
  61.7 0.8 %total.1 = (f32[16,16,128]{2,1,0:T(8,128)}, f32[16,16,128]{2,1,0:T(8,128)}) custom-call(f32[32,16,128]{2,1,0:T(8,128)S(1)} %get-tuple-element.25.own_ref, f32[32,16,128]{2,1,0:T(8,128)S(1)} %collective-permute-done.8.c_ref, f32[32,16,128]{2,1,0:T(8,128)S(1)} %collective-permute-done.12.x_ref, f32[32,16,128]{2,1,0:T(8,128)S(1)} %collective-permute-done.13.e_ref, ...), custom_call_target="tpu_custom_call" | custom-call | tf_op jit(solution)/shard_map/total/pallas_call | solution.py:342
  (2 shorter events, 0.0 us)
Async XLA Ops:
  0.6 22.6 %copy-start.1 = (f32[32,32,128]{2,1,0:T(8,128)S(1)}, f32[32,32,128]{2,1,0:T(8,128)}, u32[]{:S(2)}) copy-start(f32[32,32,128]{2,1,0:T(8,128)} %obs_ref.1) | copy-start | bytes 1572868
  0.6 22.6 %copy-start = (f32[32,32,128]{2,1,0:T(8,128)S(1)}, f32[32,32,128]{2,1,0:T(8,128)}, u32[]{:S(2)}) copy-start(f32[32,32,128]{2,1,0:T(8,128)} %p0_ref.1) | copy-start | bytes 1572868
  1.7 17.1 %collective-permute-start.3 = (f32[32,16,128]{2,1,0:T(8,128)S(1)}, f32[32,16,128]{2,1,0:T(8,128)S(1)}, u32[]{:S(2)}, u32[]{:S(2)}) collective-permute-start(f32[32,16,128]{2,1,0:T(8,128)S(1)} %bitcast.3), channel_id=1, source_target_pairs={{16,32},{32,16},{48,64},{64,48},{80,96},{96,80},{112,128},{128,112... | collective-permute-start | bytes 786440 | tf_op jit(solution)/shard_map/ppermute | solution.py:29
  9.2 9.6 %collective-permute-start.2 = (f32[32,16,128]{2,1,0:T(8,128)S(1)}, f32[32,16,128]{2,1,0:T(8,128)S(1)}, u32[]{:S(2)}, u32[]{:S(2)}) collective-permute-start(f32[32,16,128]{2,1,0:T(8,128)S(1)} %bitcast.4), channel_id=1, source_target_pairs={{0,16},{16,0},{32,48},{48,32},{64,80},{80,64},{96,112},{112,96},{1... | collective-permute-start | bytes 786440 | tf_op jit(solution)/shard_map/ppermute | solution.py:29
  9.3 13.4 %collective-permute-start.1 = (f32[32,16,128]{2,1,0:T(8,128)S(1)}, f32[32,16,128]{2,1,0:T(8,128)S(1)}, u32[]{:S(2)}, u32[]{:S(2)}) collective-permute-start(f32[32,16,128]{2,1,0:T(8,128)S(1)} %bitcast.5), channel_id=1, source_target_pairs={{1,2},{2,1},{3,4},{4,3},{5,6},{6,5},{7,8},{8,7},{9,10},{10,9},{11,... | collective-permute-start | bytes 786440 | tf_op jit(solution)/shard_map/ppermute | solution.py:29
  11.6 11.1 %collective-permute-start = (f32[32,16,128]{2,1,0:T(8,128)S(1)}, f32[32,16,128]{2,1,0:T(8,128)S(1)}, u32[]{:S(2)}, u32[]{:S(2)}) collective-permute-start(f32[32,16,128]{2,1,0:T(8,128)S(1)} %bitcast.6), channel_id=1, source_target_pairs={{0,1},{1,0},{2,3},{3,2},{4,5},{5,4},{6,7},{7,6},{8,9},{9,8},{10,11... | collective-permute-start | bytes 786440 | tf_op jit(solution)/shard_map/ppermute | solution.py:29
  18.9 9.2 %collective-permute-start.5 = (f32[32,16,128]{2,1,0:T(8,128)S(1)}, f32[32,16,128]{2,1,0:T(8,128)S(1)}, u32[]{:S(2)}, u32[]{:S(2)}) collective-permute-start(f32[32,16,128]{2,1,0:T(8,128)S(1)} %onward.1), channel_id=1, source_target_pairs={{1,2},{2,1},{3,4},{4,3},{5,6},{6,5},{7,8},{8,7},{9,10},{10,9},{11,... | collective-permute-start | bytes 786440 | tf_op jit(solution)/shard_map/ppermute | solution.py:29
  20.8 7.3 %collective-permute-start.4 = (f32[32,16,128]{2,1,0:T(8,128)S(1)}, f32[32,16,128]{2,1,0:T(8,128)S(1)}, u32[]{:S(2)}, u32[]{:S(2)}) collective-permute-start(f32[32,16,128]{2,1,0:T(8,128)S(1)} %onward.1), channel_id=1, source_target_pairs={{0,1},{1,0},{2,3},{3,2},{4,5},{5,4},{6,7},{7,6},{8,9},{9,8},{10,11... | collective-permute-start | bytes 786440 | tf_op jit(solution)/shard_map/ppermute | solution.py:29
  22.7 5.4 %collective-permute-start.7 = (f32[32,16,128]{2,1,0:T(8,128)S(1)}, f32[32,16,128]{2,1,0:T(8,128)S(1)}, u32[]{:S(2)}, u32[]{:S(2)}) collective-permute-start(f32[32,16,128]{2,1,0:T(8,128)S(1)} %collective-permute-done.1.yo_ref), channel_id=1, source_target_pairs={{0,16},{16,0},{32,48},{48,32},{64,80},{80,64},{96,112},{112,96},{1... | collective-permute-start | bytes 786440 | tf_op jit(solution)/shard_map/ppermute | solution.py:29
  22.7 5.4 %collective-permute-start.6 = (f32[32,16,128]{2,1,0:T(8,128)S(1)}, f32[32,16,128]{2,1,0:T(8,128)S(1)}, u32[]{:S(2)}, u32[]{:S(2)}) collective-permute-start(f32[32,16,128]{2,1,0:T(8,128)S(1)} %collective-permute-done.ye_ref), channel_id=1, source_target_pairs={{0,16},{16,0},{32,48},{48,32},{64,80},{80,64},{96,112},{112,96},{1... | collective-permute-start | bytes 786440 | tf_op jit(solution)/shard_map/ppermute | solution.py:29
  23.2 0.7 %copy-start.2 = (s32[1,1,2]{2,1,0:T(1,128)S(1)}, s32[1,1,2]{2,1,0:T(1,128)}, u32[]{:S(2)}) copy-start(s32[1,1,2]{2,1,0:T(1,128)} %corner_ref.1) | copy-start | bytes 28
  32.4 9.7 %collective-permute-start.9 = (f32[34,16,128]{2,1,0:T(8,128)S(1)}, f32[34,16,128]{2,1,0:T(8,128)S(1)}, u32[]{:S(2)}, u32[]{:S(2)}) collective-permute-start(f32[34,16,128]{2,1,0:T(8,128)S(1)} %get-tuple-element.28), channel_id=1, source_target_pairs={{0,1},{1,0},{2,3},{3,2},{4,5},{5,4},{6,7},{7,6},{8,9},{9,8},{10,11... | collective-permute-start | bytes 835592 | tf_op jit(solution)/shard_map/ppermute | solution.py:29
  32.5 10.9 %collective-permute-start.10 = (f32[34,16,128]{2,1,0:T(8,128)S(1)}, f32[34,16,128]{2,1,0:T(8,128)S(1)}, u32[]{:S(2)}, u32[]{:S(2)}) collective-permute-start(f32[34,16,128]{2,1,0:T(8,128)S(1)} %get-tuple-element.29), channel_id=1, source_target_pairs={{1,2},{2,1},{3,4},{4,3},{5,6},{6,5},{7,8},{8,7},{9,10},{10,9},{11,... | collective-permute-start | bytes 835592 | tf_op jit(solution)/shard_map/ppermute | solution.py:29
  36.8 1.6 %collective-permute-start.14 = (f32[32,16,128]{2,1,0:T(8,128)S(1)}, f32[32,16,128]{2,1,0:T(8,128)S(1)}, u32[]{:S(2)}, u32[]{:S(2)}) collective-permute-start(f32[32,16,128]{2,1,0:T(8,128)S(1)} %get-tuple-element.34), channel_id=1, source_target_pairs={{0,16},{16,0},{32,48},{48,32},{64,80},{80,64},{96,112},{112,96},{1... | collective-permute-start | bytes 786440 | tf_op jit(solution)/shard_map/ppermute | solution.py:29
  36.9 5.2 %collective-permute-start.11 = (f32[32,16,128]{2,1,0:T(8,128)S(1)}, f32[32,16,128]{2,1,0:T(8,128)S(1)}, u32[]{:S(2)}, u32[]{:S(2)}) collective-permute-start(f32[32,16,128]{2,1,0:T(8,128)S(1)} %get-tuple-element.30), channel_id=1, source_target_pairs={{0,16},{16,0},{32,48},{48,32},{64,80},{80,64},{96,112},{112,96},{1... | collective-permute-start | bytes 786440 | tf_op jit(solution)/shard_map/ppermute | solution.py:29
  38.4 14.5 %collective-permute-start.15 = (f32[33,16,128]{2,1,0:T(8,128)S(1)}, f32[33,16,128]{2,1,0:T(8,128)S(1)}, u32[]{:S(2)}, u32[]{:S(2)}) collective-permute-start(f32[33,16,128]{2,1,0:T(8,128)S(1)} %merge.1), channel_id=1, source_target_pairs={{1,2},{2,1},{3,4},{4,3},{5,6},{6,5},{7,8},{8,7},{9,10},{10,9},{11,... | collective-permute-start | bytes 811016 | tf_op jit(solution)/shard_map/ppermute | solution.py:29
  41.5 11.3 %collective-permute-start.8 = (f32[32,16,128]{2,1,0:T(8,128)S(1)}, f32[32,16,128]{2,1,0:T(8,128)S(1)}, u32[]{:S(2)}, u32[]{:S(2)}) collective-permute-start(f32[32,16,128]{2,1,0:T(8,128)S(1)} %get-tuple-element.26), channel_id=1, source_target_pairs={{0,16},{16,0},{32,48},{48,32},{64,80},{80,64},{96,112},{112,96},{1... | collective-permute-start | bytes 786440 | tf_op jit(solution)/shard_map/ppermute | solution.py:29
  43.4 18.3 %collective-permute-start.12 = (f32[32,16,128]{2,1,0:T(8,128)S(1)}, f32[32,16,128]{2,1,0:T(8,128)S(1)}, u32[]{:S(2)}, u32[]{:S(2)}) collective-permute-start(f32[32,16,128]{2,1,0:T(8,128)S(1)} %get-tuple-element.32), channel_id=1, source_target_pairs={{16,32},{32,16},{48,64},{64,48},{80,96},{96,80},{112,128},{128,112... | collective-permute-start | bytes 786440 | tf_op jit(solution)/shard_map/ppermute | solution.py:29
  52.8 8.9 %collective-permute-start.13 = (f32[32,16,128]{2,1,0:T(8,128)S(1)}, f32[32,16,128]{2,1,0:T(8,128)S(1)}, u32[]{:S(2)}, u32[]{:S(2)}) collective-permute-start(f32[32,16,128]{2,1,0:T(8,128)S(1)} %get-tuple-element.33), channel_id=1, source_target_pairs={{0,1},{1,0},{2,3},{3,2},{4,5},{5,4},{6,7},{7,6},{8,9},{9,8},{10,11... | collective-permute-start | bytes 786440 | tf_op jit(solution)/shard_map/ppermute | solution.py:29

commit v5 on v4

--- a/solution.py
+++ b/solution.py
@@ -127,7 +127,7 @@
 
 
 def wave_kernel(
-    field0, g1, wide, deep, obs_ref, corner_vmem, own_ref, ye_ref, yo_ref, c_ref, x_ref, ye2_ref, yo2_ref, cye_ref, cyo_ref,
+    field0, g1, wide, deep, obs_ref, corner_vmem, own_ref, yo_ref, ye_ref, c_ref, x_ref, ye2_ref, yo2_ref, cye_ref, cyo_ref,
     ce_out, co_out, cm_out, xe_out, xo_out, xm_out, oe_out, oo_out, om_out,
     corner_ref, sem, model, terms, field, bx, by, bz, gs, a1, a2, lam, kap, buoy, quad,
 ):
@@ -315,7 +315,7 @@
     )(c, o)
 
 
-def combine_kernel(m_ref, e_ref, o_ref, c_ref, oe_ref, out_ref, oe_out):
+def combine_kernel(m_ref, o_ref, e_ref, c_ref, oe_ref, out_ref, oe_out):
     out_ref[...] = m_ref[...] + e_ref[: 2 * BLOCK] + o_ref[: 2 * BLOCK]
     oe_out[...] = oe_ref[...] + c_ref[...]
 
@@ -328,7 +328,7 @@
         out_specs=tuple(vmem(2)),
         compiler_params=small,
         name="combine",
-    )(m, e, o, c, oe)
+    )(m, o, e, c, oe)
 
 
 def total_kernel(own_ref, c_ref, x_ref, e_ref, o_ref, vel_ref, rho_ref):
@@ -361,7 +361,7 @@
     ye2 = swap(passed, "shot", False)
     cyo = swap(yo, "line", False)
     cye = swap(ye, "line", False)
-    ce, co, cm, xe, xo, xm, oe, oo, om = wave(begun, own, ye, yo, c, x, ye2, yo2, cye, cyo)
+    ce, co, cm, xe, xo, xm, oe, oo, om = wave(begun, own, yo, ye, c, x, ye2, yo2, cye, cyo)
     xo = swap(xo, "shot", True)
     xe = swap(xe, "shot", False)
     ce, co, cm = (swap(block, "line", False) for block in (ce, co, cm))

time: 62.7 us -> 61.6 us (0.982)
  waiting for transfers between devices: 22.7 us -> 21.6 us
    ppermute x16, waiting for transfers between devices: 22.7 us -> 21.6 us  [swap(): return lax.ppermute(block, axis, swap_pairs(odd))]
where the time goes in v5:
time: 61.6 us; the launch traced here: 61.3 us
  starting transfers between devices  30.8 us (50%)
  waiting for transfers between devices  21.6 us (35%)
  Pallas kernels  6.45 us (10%)
  other arithmetic  1.07 us (2%)
  between operations  0.78 us (1%)
  local copies, waits for them, and re-layouts  0.66 us (1%)
    ppermute x16, starting transfers between devices, swap(): return lax.ppermute(block, axis, swap_pairs(odd))  30.8 us
    ppermute x16, waiting for transfers between devices, swap(): return lax.ppermute(block, axis, swap_pairs(odd))  21.6 us
    pallas_call x1, Pallas kernels, wave(): pl.pallas_call(wave_kernel, out_shape=(part,) * 3 + (early_part,) * 2 + (...  4.23 us
    pallas_call x1, Pallas kernels, early(): pl.pallas_call(early_kernel, out_shape=(jax.ShapeDtypeStruct((APER + 8, A...  1.32 us
  transfers between devices with their start and end apart: 16, of which 6 were waited for; matrix products, arithmetic and copies ran while one was open for 0% of the time, Pallas kernels for 2%

profile of v5, /device:TPU:95, one launch (start us, length us, event | category | flops | bytes accessed | tf_op | source)
XLA Modules:
  0.0 61.3 jit_solution(11184818812931401460)
XLA Ops:
  0.6 0.0 copy-start.1
  0.6 0.0 copy-start
  0.7 1.1 %pad_maximum_fusion = f32[2,16,16,128]{3,2,1,0:T(8,128)S(1)} fusion(f32[1,16,16,128]{3,2,1,0:T(8,128)} %bitcast.8, f32[1,16,16,128]{3,2,1,0:T(8,128)} %bitcast.9), kind=kLoop, calls=%fused_computation | loop fusion | flops 65536 | bytes 524288 | tf_op jit(solution)/shard_map/stack | solution.py:353
  1.7 7.5 %collective-permute-start.3 = (f32[32,16,128]{2,1,0:T(8,128)S(1)}, f32[32,16,128]{2,1,0:T(8,128)S(1)}, u32[]{:S(2)}, u32[]{:S(2)}) collective-permute-start(f32[32,16,128]{2,1,0:T(8,128)S(1)} %bitcast.3), channel_id=1, source_target_pairs={{16,32},{32,16},{48,64},{64,48},{80,96},{96,80},{112,128},{128,112... | collective-permute-start | bytes 786440 | tf_op jit(solution)/shard_map/ppermute | solution.py:29
  9.2 0.1 collective-permute-start.2
  9.3 0.6 collective-permute-start.1
  9.9 3.1 %collective-permute-start = (f32[32,16,128]{2,1,0:T(8,128)S(1)}, f32[32,16,128]{2,1,0:T(8,128)S(1)}, u32[]{:S(2)}, u32[]{:S(2)}) collective-permute-start(f32[32,16,128]{2,1,0:T(8,128)S(1)} %bitcast.6), channel_id=1, source_target_pairs={{1,2},{2,1},{3,4},{4,3},{5,6},{6,5},{7,8},{8,7},{9,10},{10,9},{11,... | collective-permute-start | bytes 786440 | tf_op jit(solution)/shard_map/ppermute | solution.py:29
  13.0 4.5 %collective-permute-done.3.x_ref = f32[32,16,128]{2,1,0:T(8,128)S(1)} collective-permute-done((f32[32,16,128]{2,1,0:T(8,128)S(1)}, f32[32,16,128]{2,1,0:T(8,128)S(1)}, u32[]{:S(2)}, u32[]{:S(2)}) %collective-permute-start.3) | collective-permute-done | bytes 262176 | tf_op jit(solution)/shard_map/ppermute | solution.py:29
  17.6 0.0 collective-permute-done.2.c_ref
  17.6 1.9 %collective-permute-start.5 = (f32[32,16,128]{2,1,0:T(8,128)S(1)}, f32[32,16,128]{2,1,0:T(8,128)S(1)}, u32[]{:S(2)}, u32[]{:S(2)}) collective-permute-start(f32[32,16,128]{2,1,0:T(8,128)S(1)} %onward.1), channel_id=1, source_target_pairs={{1,2},{2,1},{3,4},{4,3},{5,6},{6,5},{7,8},{8,7},{9,10},{10,9},{11,... | collective-permute-start | bytes 786440 | tf_op jit(solution)/shard_map/ppermute | solution.py:29
  19.5 0.5 collective-permute-start.4
  20.0 0.0 collective-permute-done.1.ye_ref
  20.0 0.0 collective-permute-start.6
  20.0 1.6 %collective-permute-done.yo_ref = f32[32,16,128]{2,1,0:T(8,128)S(1)} collective-permute-done((f32[32,16,128]{2,1,0:T(8,128)S(1)}, f32[32,16,128]{2,1,0:T(8,128)S(1)}, u32[]{:S(2)}, u32[]{:S(2)}) %collective-permute-start) | collective-permute-done | bytes 262176 | tf_op jit(solution)/shard_map/ppermute | solution.py:29
  21.6 1.0 %collective-permute-start.7 = (f32[32,16,128]{2,1,0:T(8,128)S(1)}, f32[32,16,128]{2,1,0:T(8,128)S(1)}, u32[]{:S(2)}, u32[]{:S(2)}) collective-permute-start(f32[32,16,128]{2,1,0:T(8,128)S(1)} %collective-permute-done.yo_ref), channel_id=1, source_target_pairs={{0,16},{16,0},{32,48},{48,32},{64,80},{80,64},{96,112},{112,96},{1... | collective-permute-start | bytes 786440 | tf_op jit(solution)/shard_map/ppermute | solution.py:29
  22.6 0.0 copy-done.1
  22.6 0.0 copy-done
  22.6 0.0 copy-start.2
  22.6 0.7 %copy-done.2 = s32[1,1,2]{2,1,0:T(1,128)S(1)} copy-done((s32[1,1,2]{2,1,0:T(1,128)S(1)}, s32[1,1,2]{2,1,0:T(1,128)}, u32[]{:S(2)}) %copy-start.2) | copy-done | bytes 32
  23.3 1.3 %early.1 = (f32[40,32,128]{2,1,0:T(8,128)S(1)}, f32[3,32,32,128]{3,2,1,0:T(8,128)S(1)}, bf16[2,256,256]{2,1,0:T(8,128)(2,1)S(1)}, bf16[2,256,128]{2,1,0:T(8,128)...) custom-call(s32[1,1,2]{2,1,0:T(1,128)S(1)} %copy-done.2, f32[32,32,128]{2,1,0:T(8,128)S(1)} %copy-done, ...), custom_call_target="tpu_custom_call" | custom-call | tf_op jit(solution)/shard_map/early/pallas_call | solution.py:112
  24.6 2.9 %collective-permute-done.5.yo2_ref = f32[32,16,128]{2,1,0:T(8,128)S(1)} collective-permute-done((f32[32,16,128]{2,1,0:T(8,128)S(1)}, f32[32,16,128]{2,1,0:T(8,128)S(1)}, u32[]{:S(2)}, u32[]{:S(2)}) %collective-permute-start.5) | collective-permute-done | bytes 262176 | tf_op jit(solution)/shard_map/ppermute | solution.py:29
  27.5 0.0 collective-permute-done.4.ye2_ref
  27.5 0.0 collective-permute-done.6.cye_ref
  27.5 0.0 collective-permute-done.7.cyo_ref
  27.5 4.2 %wave.1 = (f32[32,16,128]{2,1,0:T(8,128)S(1)}, f32[32,16,128]{2,1,0:T(8,128)S(1)}, f32[32,16,128]{2,1,0:T(8,128)S(1)}, f32[34,16,128]{2,1,0:T(8,128)S(1)}, f32[3...) custom-call(f32[40,32,128]{2,1,0:T(8,128)S(1)} %get-tuple-element.19, ...), custom_call_target="tpu_custom_call" | custom-call | tf_op jit(solution)/shard_map/wave/pallas_call | solution.py:267
  31.8 4.7 %collective-permute-start.9 = (f32[34,16,128]{2,1,0:T(8,128)S(1)}, f32[34,16,128]{2,1,0:T(8,128)S(1)}, u32[]{:S(2)}, u32[]{:S(2)}) collective-permute-start(f32[34,16,128]{2,1,0:T(8,128)S(1)} %get-tuple-element.28), channel_id=1, source_target_pairs={{1,2},{2,1},{3,4},{4,3},{5,6},{6,5},{7,8},{8,7},{9,10},{10,9},{11,... | collective-permute-start | bytes 835592 | tf_op jit(solution)/shard_map/ppermute | solution.py:29
  36.5 0.1 collective-permute-start.10
  36.6 0.7 %collective-permute-start.14 = (f32[32,16,128]{2,1,0:T(8,128)S(1)}, f32[32,16,128]{2,1,0:T(8,128)S(1)}, u32[]{:S(2)}, u32[]{:S(2)}) collective-permute-start(f32[32,16,128]{2,1,0:T(8,128)S(1)} %get-tuple-element.34), channel_id=1, source_target_pairs={{0,16},{16,0},{32,48},{48,32},{64,80},{80,64},{96,112},{112,96},{1... | collective-permute-start | bytes 786440 | tf_op jit(solution)/shard_map/ppermute | solution.py:29
  37.3 0.1 collective-permute-start.11
  37.4 1.1 %collective-permute-done.14.c_ref = f32[32,16,128]{2,1,0:T(8,128)S(1)} collective-permute-done((f32[32,16,128]{2,1,0:T(8,128)S(1)}, f32[32,16,128]{2,1,0:T(8,128)S(1)}, u32[]{:S(2)}, u32[]{:S(2)}) %collective-permute-start.14) | collective-permute-done | bytes 262176 | tf_op jit(solution)/shard_map/ppermute | solution.py:29
  38.5 2.5 %collective-permute-start.15 = (f32[33,16,128]{2,1,0:T(8,128)S(1)}, f32[33,16,128]{2,1,0:T(8,128)S(1)}, u32[]{:S(2)}, u32[]{:S(2)}) collective-permute-start(f32[33,16,128]{2,1,0:T(8,128)S(1)} %merge.1), channel_id=1, source_target_pairs={{1,2},{2,1},{3,4},{4,3},{5,6},{6,5},{7,8},{8,7},{9,10},{10,9},{11,... | collective-permute-start | bytes 811016 | tf_op jit(solution)/shard_map/ppermute | solution.py:29
  40.9 0.6 collective-permute-start.8
  41.5 0.0 collective-permute-done.11.c_ref
  41.5 2.7 %collective-permute-done.9.o_ref = f32[34,16,128]{2,1,0:T(8,128)S(1)} collective-permute-done((f32[34,16,128]{2,1,0:T(8,128)S(1)}, f32[34,16,128]{2,1,0:T(8,128)S(1)}, u32[]{:S(2)}, u32[]{:S(2)}) %collective-permute-start.9) | collective-permute-done | bytes 278560 | tf_op jit(solution)/shard_map/ppermute | solution.py:29
  44.2 0.0 collective-permute-done.10.e_ref
  44.2 0.1 combine.1
  44.3 7.4 %collective-permute-start.12 = (f32[32,16,128]{2,1,0:T(8,128)S(1)}, f32[32,16,128]{2,1,0:T(8,128)S(1)}, u32[]{:S(2)}, u32[]{:S(2)}) collective-permute-start(f32[32,16,128]{2,1,0:T(8,128)S(1)} %get-tuple-element.32), channel_id=1, source_target_pairs={{16,32},{32,16},{48,64},{64,48},{80,96},{96,80},{112,128},{128,112... | collective-permute-start | bytes 786440 | tf_op jit(solution)/shard_map/ppermute | solution.py:29
  51.7 0.1 collective-permute-start.13
  51.8 0.0 collective-permute-done.8.c_ref
  51.8 0.0 collective-permute-done.15.o_ref
  51.8 8.8 %collective-permute-done.12.x_ref = f32[32,16,128]{2,1,0:T(8,128)S(1)} collective-permute-done((f32[32,16,128]{2,1,0:T(8,128)S(1)}, f32[32,16,128]{2,1,0:T(8,128)S(1)}, u32[]{:S(2)}, u32[]{:S(2)}) %collective-permute-start.12) | collective-permute-done | bytes 262176 | tf_op jit(solution)/shard_map/ppermute | solution.py:29
  60.5 0.0 collective-permute-done.13.e_ref
  60.5 0.8 %total.1 = (f32[16,16,128]{2,1,0:T(8,128)}, f32[16,16,128]{2,1,0:T(8,128)}) custom-call(f32[32,16,128]{2,1,0:T(8,128)S(1)} %get-tuple-element.25.own_ref, f32[32,16,128]{2,1,0:T(8,128)S(1)} %collective-permute-done.8.c_ref, f32[32,16,128]{2,1,0:T(8,128)S(1)} %collective-permute-done.12.x_ref, f32[32,16,128]{2,1,0:T(8,128)S(1)} %collective-permute-done.13.e_ref, ...), custom_call_target="tpu_custom_call" | custom-call | tf_op jit(solution)/shard_map/total/pallas_call | solution.py:342
  (2 shorter events, 0.0 us)
Async XLA Ops:
  0.6 22.0 %copy-start.1 = (f32[32,32,128]{2,1,0:T(8,128)S(1)}, f32[32,32,128]{2,1,0:T(8,128)}, u32[]{:S(2)}) copy-start(f32[32,32,128]{2,1,0:T(8,128)} %obs_ref.1) | copy-start | bytes 1572868
  0.6 22.0 %copy-start = (f32[32,32,128]{2,1,0:T(8,128)S(1)}, f32[32,32,128]{2,1,0:T(8,128)}, u32[]{:S(2)}) copy-start(f32[32,32,128]{2,1,0:T(8,128)} %p0_ref.1) | copy-start | bytes 1572868
  1.7 15.8 %collective-permute-start.3 = (f32[32,16,128]{2,1,0:T(8,128)S(1)}, f32[32,16,128]{2,1,0:T(8,128)S(1)}, u32[]{:S(2)}, u32[]{:S(2)}) collective-permute-start(f32[32,16,128]{2,1,0:T(8,128)S(1)} %bitcast.3), channel_id=1, source_target_pairs={{16,32},{32,16},{48,64},{64,48},{80,96},{96,80},{112,128},{128,112... | collective-permute-start | bytes 786440 | tf_op jit(solution)/shard_map/ppermute | solution.py:29
  9.2 8.3 %collective-permute-start.2 = (f32[32,16,128]{2,1,0:T(8,128)S(1)}, f32[32,16,128]{2,1,0:T(8,128)S(1)}, u32[]{:S(2)}, u32[]{:S(2)}) collective-permute-start(f32[32,16,128]{2,1,0:T(8,128)S(1)} %bitcast.4), channel_id=1, source_target_pairs={{0,16},{16,0},{32,48},{48,32},{64,80},{80,64},{96,112},{112,96},{1... | collective-permute-start | bytes 786440 | tf_op jit(solution)/shard_map/ppermute | solution.py:29
  9.3 10.7 %collective-permute-start.1 = (f32[32,16,128]{2,1,0:T(8,128)S(1)}, f32[32,16,128]{2,1,0:T(8,128)S(1)}, u32[]{:S(2)}, u32[]{:S(2)}) collective-permute-start(f32[32,16,128]{2,1,0:T(8,128)S(1)} %bitcast.5), channel_id=1, source_target_pairs={{0,1},{1,0},{2,3},{3,2},{4,5},{5,4},{6,7},{7,6},{8,9},{9,8},{10,11... | collective-permute-start | bytes 786440 | tf_op jit(solution)/shard_map/ppermute | solution.py:29
  9.9 11.7 %collective-permute-start = (f32[32,16,128]{2,1,0:T(8,128)S(1)}, f32[32,16,128]{2,1,0:T(8,128)S(1)}, u32[]{:S(2)}, u32[]{:S(2)}) collective-permute-start(f32[32,16,128]{2,1,0:T(8,128)S(1)} %bitcast.6), channel_id=1, source_target_pairs={{1,2},{2,1},{3,4},{4,3},{5,6},{6,5},{7,8},{8,7},{9,10},{10,9},{11,... | collective-permute-start | bytes 786440 | tf_op jit(solution)/shard_map/ppermute | solution.py:29
  17.6 9.9 %collective-permute-start.5 = (f32[32,16,128]{2,1,0:T(8,128)S(1)}, f32[32,16,128]{2,1,0:T(8,128)S(1)}, u32[]{:S(2)}, u32[]{:S(2)}) collective-permute-start(f32[32,16,128]{2,1,0:T(8,128)S(1)} %onward.1), channel_id=1, source_target_pairs={{1,2},{2,1},{3,4},{4,3},{5,6},{6,5},{7,8},{8,7},{9,10},{10,9},{11,... | collective-permute-start | bytes 786440 | tf_op jit(solution)/shard_map/ppermute | solution.py:29
  19.5 8.0 %collective-permute-start.4 = (f32[32,16,128]{2,1,0:T(8,128)S(1)}, f32[32,16,128]{2,1,0:T(8,128)S(1)}, u32[]{:S(2)}, u32[]{:S(2)}) collective-permute-start(f32[32,16,128]{2,1,0:T(8,128)S(1)} %onward.1), channel_id=1, source_target_pairs={{0,1},{1,0},{2,3},{3,2},{4,5},{5,4},{6,7},{7,6},{8,9},{9,8},{10,11... | collective-permute-start | bytes 786440 | tf_op jit(solution)/shard_map/ppermute | solution.py:29
  20.0 7.5 %collective-permute-start.6 = (f32[32,16,128]{2,1,0:T(8,128)S(1)}, f32[32,16,128]{2,1,0:T(8,128)S(1)}, u32[]{:S(2)}, u32[]{:S(2)}) collective-permute-start(f32[32,16,128]{2,1,0:T(8,128)S(1)} %collective-permute-done.1.ye_ref), channel_id=1, source_target_pairs={{0,16},{16,0},{32,48},{48,32},{64,80},{80,64},{96,112},{112,96},{1... | collective-permute-start | bytes 786440 | tf_op jit(solution)/shard_map/ppermute | solution.py:29
  21.6 6.0 %collective-permute-start.7 = (f32[32,16,128]{2,1,0:T(8,128)S(1)}, f32[32,16,128]{2,1,0:T(8,128)S(1)}, u32[]{:S(2)}, u32[]{:S(2)}) collective-permute-start(f32[32,16,128]{2,1,0:T(8,128)S(1)} %collective-permute-done.yo_ref), channel_id=1, source_target_pairs={{0,16},{16,0},{32,48},{48,32},{64,80},{80,64},{96,112},{112,96},{1... | collective-permute-start | bytes 786440 | tf_op jit(solution)/shard_map/ppermute | solution.py:29
  22.6 0.7 %copy-start.2 = (s32[1,1,2]{2,1,0:T(1,128)S(1)}, s32[1,1,2]{2,1,0:T(1,128)}, u32[]{:S(2)}) copy-start(s32[1,1,2]{2,1,0:T(1,128)} %corner_ref.1) | copy-start | bytes 28
  31.8 12.4 %collective-permute-start.9 = (f32[34,16,128]{2,1,0:T(8,128)S(1)}, f32[34,16,128]{2,1,0:T(8,128)S(1)}, u32[]{:S(2)}, u32[]{:S(2)}) collective-permute-start(f32[34,16,128]{2,1,0:T(8,128)S(1)} %get-tuple-element.28), channel_id=1, source_target_pairs={{1,2},{2,1},{3,4},{4,3},{5,6},{6,5},{7,8},{8,7},{9,10},{10,9},{11,... | collective-permute-start | bytes 835592 | tf_op jit(solution)/shard_map/ppermute | solution.py:29
  36.5 7.7 %collective-permute-start.10 = (f32[34,16,128]{2,1,0:T(8,128)S(1)}, f32[34,16,128]{2,1,0:T(8,128)S(1)}, u32[]{:S(2)}, u32[]{:S(2)}) collective-permute-start(f32[34,16,128]{2,1,0:T(8,128)S(1)} %get-tuple-element.29), channel_id=1, source_target_pairs={{0,1},{1,0},{2,3},{3,2},{4,5},{5,4},{6,7},{7,6},{8,9},{9,8},{10,11... | collective-permute-start | bytes 835592 | tf_op jit(solution)/shard_map/ppermute | solution.py:29
  36.6 1.8 %collective-permute-start.14 = (f32[32,16,128]{2,1,0:T(8,128)S(1)}, f32[32,16,128]{2,1,0:T(8,128)S(1)}, u32[]{:S(2)}, u32[]{:S(2)}) collective-permute-start(f32[32,16,128]{2,1,0:T(8,128)S(1)} %get-tuple-element.34), channel_id=1, source_target_pairs={{0,16},{16,0},{32,48},{48,32},{64,80},{80,64},{96,112},{112,96},{1... | collective-permute-start | bytes 786440 | tf_op jit(solution)/shard_map/ppermute | solution.py:29
  37.3 4.2 %collective-permute-start.11 = (f32[32,16,128]{2,1,0:T(8,128)S(1)}, f32[32,16,128]{2,1,0:T(8,128)S(1)}, u32[]{:S(2)}, u32[]{:S(2)}) collective-permute-start(f32[32,16,128]{2,1,0:T(8,128)S(1)} %get-tuple-element.30), channel_id=1, source_target_pairs={{0,16},{16,0},{32,48},{48,32},{64,80},{80,64},{96,112},{112,96},{1... | collective-permute-start | bytes 786440 | tf_op jit(solution)/shard_map/ppermute | solution.py:29
  38.5 13.3 %collective-permute-start.15 = (f32[33,16,128]{2,1,0:T(8,128)S(1)}, f32[33,16,128]{2,1,0:T(8,128)S(1)}, u32[]{:S(2)}, u32[]{:S(2)}) collective-permute-start(f32[33,16,128]{2,1,0:T(8,128)S(1)} %merge.1), channel_id=1, source_target_pairs={{1,2},{2,1},{3,4},{4,3},{5,6},{6,5},{7,8},{8,7},{9,10},{10,9},{11,... | collective-permute-start | bytes 811016 | tf_op jit(solution)/shard_map/ppermute | solution.py:29
  40.9 10.8 %collective-permute-start.8 = (f32[32,16,128]{2,1,0:T(8,128)S(1)}, f32[32,16,128]{2,1,0:T(8,128)S(1)}, u32[]{:S(2)}, u32[]{:S(2)}) collective-permute-start(f32[32,16,128]{2,1,0:T(8,128)S(1)} %get-tuple-element.26), channel_id=1, source_target_pairs={{0,16},{16,0},{32,48},{48,32},{64,80},{80,64},{96,112},{112,96},{1... | collective-permute-start | bytes 786440 | tf_op jit(solution)/shard_map/ppermute | solution.py:29
  44.3 16.3 %collective-permute-start.12 = (f32[32,16,128]{2,1,0:T(8,128)S(1)}, f32[32,16,128]{2,1,0:T(8,128)S(1)}, u32[]{:S(2)}, u32[]{:S(2)}) collective-permute-start(f32[32,16,128]{2,1,0:T(8,128)S(1)} %get-tuple-element.32), channel_id=1, source_target_pairs={{16,32},{32,16},{48,64},{64,48},{80,96},{96,80},{112,128},{128,112... | collective-permute-start | bytes 786440 | tf_op jit(solution)/shard_map/ppermute | solution.py:29
  51.7 8.9 %collective-permute-start.13 = (f32[32,16,128]{2,1,0:T(8,128)S(1)}, f32[32,16,128]{2,1,0:T(8,128)S(1)}, u32[]{:S(2)}, u32[]{:S(2)}) collective-permute-start(f32[32,16,128]{2,1,0:T(8,128)S(1)} %get-tuple-element.33), channel_id=1, source_target_pairs={{0,1},{1,0},{2,3},{3,2},{4,5},{5,4},{6,7},{7,6},{8,9},{9,8},{10,11... | collective-permute-start | bytes 786440 | tf_op jit(solution)/shard_map/ppermute | solution.py:29

commit v6 on v5

--- a/solution.py
+++ b/solution.py
@@ -331,10 +331,15 @@
     )(m, o, e, c, oe)
 
 
-def total_kernel(own_ref, c_ref, x_ref, e_ref, o_ref, vel_ref, rho_ref):
-    for f, out_ref in ((0, vel_ref), (1, rho_ref)):
+def total_kernel(own_ref, c_ref, x_ref, e_ref, o_ref, vel_hbm, rho_hbm, held, sems):
+    copies = []
+    for f, out_hbm in ((0, vel_hbm), (1, rho_hbm)):
         rows = slice(f * BLOCK, (f + 1) * BLOCK)
-        out_ref[...] = ((own_ref[rows] + c_ref[rows]) + x_ref[rows]) + (e_ref[rows] + o_ref[rows])
+        held[f] = ((own_ref[rows] + c_ref[rows]) + x_ref[rows]) + (e_ref[rows] + o_ref[rows])
+        copies.append(pltpu.make_async_copy(held.at[f], out_hbm, sems.at[f]))
+        copies[f].start()
+    for copy in copies:
+        copy.wait()
 
 
 def total(*parts):
@@ -343,7 +348,8 @@
         total_kernel,
         out_shape=(block, block),
         in_specs=vmem(5),
-        out_specs=tuple(vmem(2)),
+        out_specs=(pl.BlockSpec(memory_space=pltpu.HBM),) * 2,
+        scratch_shapes=[pltpu.VMEM((2, BLOCK, BLOCK, NZ), F32), pltpu.SemaphoreType.DMA((2,))],
         compiler_params=small,
         name="total",
     )(*parts)

time: 61.6 us -> 61.5 us (level)
  transfers between devices with their start and end apart: 16 -> 16, of which waited for: 6 -> 7; matrix products, arithmetic and copies ran while one was open for 0% -> 0% of each run, Pallas kernels for 2% -> 2%
where the time goes in v6:
time: 61.5 us; the launch traced here: 61.1 us
  starting transfers between devices  30.4 us (49%)
  waiting for transfers between devices  21.9 us (36%)
  Pallas kernels  6.32 us (10%)
  other arithmetic  1.07 us (2%)
  between operations  0.78 us (1%)
  local copies, waits for them, and re-layouts  0.66 us (1%)
    ppermute x16, starting transfers between devices, swap(): return lax.ppermute(block, axis, swap_pairs(odd))  30.4 us
    ppermute x16, waiting for transfers between devices, swap(): return lax.ppermute(block, axis, swap_pairs(odd))  21.9 us
    pallas_call x1, Pallas kernels, wave(): pl.pallas_call(wave_kernel, out_shape=(part,) * 3 + (early_part,) * 2 + (...  4.13 us
    pallas_call x1, Pallas kernels, early(): pl.pallas_call(early_kernel, out_shape=(jax.ShapeDtypeStruct((APER + 8, A...  1.32 us
  transfers between devices with their start and end apart: 16, of which 7 were waited for; matrix products, arithmetic and copies ran while one was open for 0% of the time, Pallas kernels for 2%

profile of v6, /device:TPU:95, one launch (start us, length us, event | category | flops | bytes accessed | tf_op | source)
XLA Modules:
  0.0 61.1 jit_solution(10461537369159955898)
XLA Ops:
  0.6 0.0 copy-start.1
  0.6 0.0 copy-start
  0.7 1.1 %pad_maximum_fusion = f32[2,16,16,128]{3,2,1,0:T(8,128)S(1)} fusion(f32[1,16,16,128]{3,2,1,0:T(8,128)} %bitcast.8, f32[1,16,16,128]{3,2,1,0:T(8,128)} %bitcast.9), kind=kLoop, calls=%fused_computation | loop fusion | flops 65536 | bytes 524288 | tf_op jit(solution)/shard_map/stack | solution.py:359
  1.7 7.5 %collective-permute-start.3 = (f32[32,16,128]{2,1,0:T(8,128)S(1)}, f32[32,16,128]{2,1,0:T(8,128)S(1)}, u32[]{:S(2)}, u32[]{:S(2)}) collective-permute-start(f32[32,16,128]{2,1,0:T(8,128)S(1)} %bitcast.3), channel_id=1, source_target_pairs={{16,32},{32,16},{48,64},{64,48},{80,96},{96,80},{112,128},{128,112... | collective-permute-start | bytes 786440 | tf_op jit(solution)/shard_map/ppermute | solution.py:29
  9.2 0.1 collective-permute-start.2
  9.3 0.6 collective-permute-start.1
  9.9 3.1 %collective-permute-start = (f32[32,16,128]{2,1,0:T(8,128)S(1)}, f32[32,16,128]{2,1,0:T(8,128)S(1)}, u32[]{:S(2)}, u32[]{:S(2)}) collective-permute-start(f32[32,16,128]{2,1,0:T(8,128)S(1)} %bitcast.6), channel_id=1, source_target_pairs={{1,2},{2,1},{3,4},{4,3},{5,6},{6,5},{7,8},{8,7},{9,10},{10,9},{11,... | collective-permute-start | bytes 786440 | tf_op jit(solution)/shard_map/ppermute | solution.py:29
  13.0 4.5 %collective-permute-done.3.x_ref = f32[32,16,128]{2,1,0:T(8,128)S(1)} collective-permute-done((f32[32,16,128]{2,1,0:T(8,128)S(1)}, f32[32,16,128]{2,1,0:T(8,128)S(1)}, u32[]{:S(2)}, u32[]{:S(2)}) %collective-permute-start.3) | collective-permute-done | bytes 262176 | tf_op jit(solution)/shard_map/ppermute | solution.py:29
  17.6 0.0 collective-permute-done.2.c_ref
  17.6 1.9 %collective-permute-start.5 = (f32[32,16,128]{2,1,0:T(8,128)S(1)}, f32[32,16,128]{2,1,0:T(8,128)S(1)}, u32[]{:S(2)}, u32[]{:S(2)}) collective-permute-start(f32[32,16,128]{2,1,0:T(8,128)S(1)} %onward.1), channel_id=1, source_target_pairs={{1,2},{2,1},{3,4},{4,3},{5,6},{6,5},{7,8},{8,7},{9,10},{10,9},{11,... | collective-permute-start | bytes 786440 | tf_op jit(solution)/shard_map/ppermute | solution.py:29
  19.5 0.5 collective-permute-start.4
  20.0 0.0 collective-permute-done.1.ye_ref
  20.0 0.0 collective-permute-start.6
  20.0 1.6 %collective-permute-done.yo_ref = f32[32,16,128]{2,1,0:T(8,128)S(1)} collective-permute-done((f32[32,16,128]{2,1,0:T(8,128)S(1)}, f32[32,16,128]{2,1,0:T(8,128)S(1)}, u32[]{:S(2)}, u32[]{:S(2)}) %collective-permute-start) | collective-permute-done | bytes 262176 | tf_op jit(solution)/shard_map/ppermute | solution.py:29
  21.6 1.0 %collective-permute-start.7 = (f32[32,16,128]{2,1,0:T(8,128)S(1)}, f32[32,16,128]{2,1,0:T(8,128)S(1)}, u32[]{:S(2)}, u32[]{:S(2)}) collective-permute-start(f32[32,16,128]{2,1,0:T(8,128)S(1)} %collective-permute-done.yo_ref), channel_id=1, source_target_pairs={{0,16},{16,0},{32,48},{48,32},{64,80},{80,64},{96,112},{112,96},{1... | collective-permute-start | bytes 786440 | tf_op jit(solution)/shard_map/ppermute | solution.py:29
  22.6 0.0 copy-done.1
  22.6 0.0 copy-done
  22.6 0.0 copy-start.2
  22.6 0.7 %copy-done.2 = s32[1,1,2]{2,1,0:T(1,128)S(1)} copy-done((s32[1,1,2]{2,1,0:T(1,128)S(1)}, s32[1,1,2]{2,1,0:T(1,128)}, u32[]{:S(2)}) %copy-start.2) | copy-done | bytes 32
  23.3 1.3 %early.1 = (f32[40,32,128]{2,1,0:T(8,128)S(1)}, f32[3,32,32,128]{3,2,1,0:T(8,128)S(1)}, bf16[2,256,256]{2,1,0:T(8,128)(2,1)S(1)}, bf16[2,256,128]{2,1,0:T(8,128)...) custom-call(s32[1,1,2]{2,1,0:T(1,128)S(1)} %copy-done.2, f32[32,32,128]{2,1,0:T(8,128)S(1)} %copy-done, ...), custom_call_target="tpu_custom_call" | custom-call | tf_op jit(solution)/shard_map/early/pallas_call | solution.py:112
  24.6 2.9 %collective-permute-done.5.yo2_ref = f32[32,16,128]{2,1,0:T(8,128)S(1)} collective-permute-done((f32[32,16,128]{2,1,0:T(8,128)S(1)}, f32[32,16,128]{2,1,0:T(8,128)S(1)}, u32[]{:S(2)}, u32[]{:S(2)}) %collective-permute-start.5) | collective-permute-done | bytes 262176 | tf_op jit(solution)/shard_map/ppermute | solution.py:29
  27.5 0.0 collective-permute-done.4.ye2_ref
  27.5 0.0 collective-permute-done.6.cye_ref
  27.5 0.0 collective-permute-done.7.cyo_ref
  27.5 4.1 %wave.1 = (f32[32,16,128]{2,1,0:T(8,128)S(1)}, f32[32,16,128]{2,1,0:T(8,128)S(1)}, f32[32,16,128]{2,1,0:T(8,128)S(1)}, f32[34,16,128]{2,1,0:T(8,128)S(1)}, f32[3...) custom-call(f32[40,32,128]{2,1,0:T(8,128)S(1)} %get-tuple-element.19, ...), custom_call_target="tpu_custom_call" | custom-call | tf_op jit(solution)/shard_map/wave/pallas_call | solution.py:267
  31.7 5.0 %collective-permute-start.9 = (f32[34,16,128]{2,1,0:T(8,128)S(1)}, f32[34,16,128]{2,1,0:T(8,128)S(1)}, u32[]{:S(2)}, u32[]{:S(2)}) collective-permute-start(f32[34,16,128]{2,1,0:T(8,128)S(1)} %get-tuple-element.28), channel_id=1, source_target_pairs={{1,2},{2,1},{3,4},{4,3},{5,6},{6,5},{7,8},{8,7},{9,10},{10,9},{11,... | collective-permute-start | bytes 835592 | tf_op jit(solution)/shard_map/ppermute | solution.py:29
  36.6 0.1 collective-permute-start.10
  36.7 0.4 collective-permute-start.14
  37.2 0.2 collective-permute-start.11
  37.3 1.0 %collective-permute-done.14.c_ref = f32[32,16,128]{2,1,0:T(8,128)S(1)} collective-permute-done((f32[32,16,128]{2,1,0:T(8,128)S(1)}, f32[32,16,128]{2,1,0:T(8,128)S(1)}, u32[]{:S(2)}, u32[]{:S(2)}) %collective-permute-start.14) | collective-permute-done | bytes 262176 | tf_op jit(solution)/shard_map/ppermute | solution.py:29
  38.4 2.4 %collective-permute-start.15 = (f32[33,16,128]{2,1,0:T(8,128)S(1)}, f32[33,16,128]{2,1,0:T(8,128)S(1)}, u32[]{:S(2)}, u32[]{:S(2)}) collective-permute-start(f32[33,16,128]{2,1,0:T(8,128)S(1)} %merge.1), channel_id=1, source_target_pairs={{1,2},{2,1},{3,4},{4,3},{5,6},{6,5},{7,8},{8,7},{9,10},{10,9},{11,... | collective-permute-start | bytes 811016 | tf_op jit(solution)/shard_map/ppermute | solution.py:29
  40.8 0.6 collective-permute-start.8
  41.4 0.0 collective-permute-done.11.c_ref
  41.4 2.7 %collective-permute-done.9.o_ref = f32[34,16,128]{2,1,0:T(8,128)S(1)} collective-permute-done((f32[34,16,128]{2,1,0:T(8,128)S(1)}, f32[34,16,128]{2,1,0:T(8,128)S(1)}, u32[]{:S(2)}, u32[]{:S(2)}) %collective-permute-start.9) | collective-permute-done | bytes 278560 | tf_op jit(solution)/shard_map/ppermute | solution.py:29
  44.1 0.5 collective-permute-done.10.e_ref
  44.6 0.1 combine.1
  44.7 7.0 %collective-permute-start.12 = (f32[32,16,128]{2,1,0:T(8,128)S(1)}, f32[32,16,128]{2,1,0:T(8,128)S(1)}, u32[]{:S(2)}, u32[]{:S(2)}) collective-permute-start(f32[32,16,128]{2,1,0:T(8,128)S(1)} %get-tuple-element.32), channel_id=1, source_target_pairs={{16,32},{32,16},{48,64},{64,48},{80,96},{96,80},{112,128},{128,112... | collective-permute-start | bytes 786440 | tf_op jit(solution)/shard_map/ppermute | solution.py:29
  51.7 0.1 collective-permute-start.13
  51.8 0.0 collective-permute-done.8.c_ref
  51.8 0.0 collective-permute-done.15.o_ref
  51.8 8.6 %collective-permute-done.12.x_ref = f32[32,16,128]{2,1,0:T(8,128)S(1)} collective-permute-done((f32[32,16,128]{2,1,0:T(8,128)S(1)}, f32[32,16,128]{2,1,0:T(8,128)S(1)}, u32[]{:S(2)}, u32[]{:S(2)}) %collective-permute-start.12) | collective-permute-done | bytes 262176 | tf_op jit(solution)/shard_map/ppermute | solution.py:29
  60.4 0.0 collective-permute-done.13.e_ref
  60.4 0.8 %total.1 = (f32[16,16,128]{2,1,0:T(8,128)}, f32[16,16,128]{2,1,0:T(8,128)}) custom-call(f32[32,16,128]{2,1,0:T(8,128)S(1)} %get-tuple-element.25.own_ref, f32[32,16,128]{2,1,0:T(8,128)S(1)} %collective-permute-done.8.c_ref, f32[32,16,128]{2,1,0:T(8,128)S(1)} %collective-permute-done.12.x_ref, f32[32,16,128]{2,1,0:T(8,128)S(1)} %collective-permute-done.13.e_ref, ...), custom_call_target="tpu_custom_call" | custom-call | tf_op jit(solution)/shard_map/total/pallas_call | solution.py:347
  (2 shorter events, 0.0 us)
Async XLA Ops:
  0.6 22.0 %copy-start.1 = (f32[32,32,128]{2,1,0:T(8,128)S(1)}, f32[32,32,128]{2,1,0:T(8,128)}, u32[]{:S(2)}) copy-start(f32[32,32,128]{2,1,0:T(8,128)} %obs_ref.1) | copy-start | bytes 1572868
  0.6 22.0 %copy-start = (f32[32,32,128]{2,1,0:T(8,128)S(1)}, f32[32,32,128]{2,1,0:T(8,128)}, u32[]{:S(2)}) copy-start(f32[32,32,128]{2,1,0:T(8,128)} %p0_ref.1) | copy-start | bytes 1572868
  1.7 15.8 %collective-permute-start.3 = (f32[32,16,128]{2,1,0:T(8,128)S(1)}, f32[32,16,128]{2,1,0:T(8,128)S(1)}, u32[]{:S(2)}, u32[]{:S(2)}) collective-permute-start(f32[32,16,128]{2,1,0:T(8,128)S(1)} %bitcast.3), channel_id=1, source_target_pairs={{16,32},{32,16},{48,64},{64,48},{80,96},{96,80},{112,128},{128,112... | collective-permute-start | bytes 786440 | tf_op jit(solution)/shard_map/ppermute | solution.py:29
  9.2 8.3 %collective-permute-start.2 = (f32[32,16,128]{2,1,0:T(8,128)S(1)}, f32[32,16,128]{2,1,0:T(8,128)S(1)}, u32[]{:S(2)}, u32[]{:S(2)}) collective-permute-start(f32[32,16,128]{2,1,0:T(8,128)S(1)} %bitcast.4), channel_id=1, source_target_pairs={{0,16},{16,0},{32,48},{48,32},{64,80},{80,64},{96,112},{112,96},{1... | collective-permute-start | bytes 786440 | tf_op jit(solution)/shard_map/ppermute | solution.py:29
  9.3 10.7 %collective-permute-start.1 = (f32[32,16,128]{2,1,0:T(8,128)S(1)}, f32[32,16,128]{2,1,0:T(8,128)S(1)}, u32[]{:S(2)}, u32[]{:S(2)}) collective-permute-start(f32[32,16,128]{2,1,0:T(8,128)S(1)} %bitcast.5), channel_id=1, source_target_pairs={{0,1},{1,0},{2,3},{3,2},{4,5},{5,4},{6,7},{7,6},{8,9},{9,8},{10,11... | collective-permute-start | bytes 786440 | tf_op jit(solution)/shard_map/ppermute | solution.py:29
  9.9 11.7 %collective-permute-start = (f32[32,16,128]{2,1,0:T(8,128)S(1)}, f32[32,16,128]{2,1,0:T(8,128)S(1)}, u32[]{:S(2)}, u32[]{:S(2)}) collective-permute-start(f32[32,16,128]{2,1,0:T(8,128)S(1)} %bitcast.6), channel_id=1, source_target_pairs={{1,2},{2,1},{3,4},{4,3},{5,6},{6,5},{7,8},{8,7},{9,10},{10,9},{11,... | collective-permute-start | bytes 786440 | tf_op jit(solution)/shard_map/ppermute | solution.py:29
  17.6 9.9 %collective-permute-start.5 = (f32[32,16,128]{2,1,0:T(8,128)S(1)}, f32[32,16,128]{2,1,0:T(8,128)S(1)}, u32[]{:S(2)}, u32[]{:S(2)}) collective-permute-start(f32[32,16,128]{2,1,0:T(8,128)S(1)} %onward.1), channel_id=1, source_target_pairs={{1,2},{2,1},{3,4},{4,3},{5,6},{6,5},{7,8},{8,7},{9,10},{10,9},{11,... | collective-permute-start | bytes 786440 | tf_op jit(solution)/shard_map/ppermute | solution.py:29
  19.5 8.0 %collective-permute-start.4 = (f32[32,16,128]{2,1,0:T(8,128)S(1)}, f32[32,16,128]{2,1,0:T(8,128)S(1)}, u32[]{:S(2)}, u32[]{:S(2)}) collective-permute-start(f32[32,16,128]{2,1,0:T(8,128)S(1)} %onward.1), channel_id=1, source_target_pairs={{0,1},{1,0},{2,3},{3,2},{4,5},{5,4},{6,7},{7,6},{8,9},{9,8},{10,11... | collective-permute-start | bytes 786440 | tf_op jit(solution)/shard_map/ppermute | solution.py:29
  20.0 7.5 %collective-permute-start.6 = (f32[32,16,128]{2,1,0:T(8,128)S(1)}, f32[32,16,128]{2,1,0:T(8,128)S(1)}, u32[]{:S(2)}, u32[]{:S(2)}) collective-permute-start(f32[32,16,128]{2,1,0:T(8,128)S(1)} %collective-permute-done.1.ye_ref), channel_id=1, source_target_pairs={{0,16},{16,0},{32,48},{48,32},{64,80},{80,64},{96,112},{112,96},{1... | collective-permute-start | bytes 786440 | tf_op jit(solution)/shard_map/ppermute | solution.py:29
  21.6 6.0 %collective-permute-start.7 = (f32[32,16,128]{2,1,0:T(8,128)S(1)}, f32[32,16,128]{2,1,0:T(8,128)S(1)}, u32[]{:S(2)}, u32[]{:S(2)}) collective-permute-start(f32[32,16,128]{2,1,0:T(8,128)S(1)} %collective-permute-done.yo_ref), channel_id=1, source_target_pairs={{0,16},{16,0},{32,48},{48,32},{64,80},{80,64},{96,112},{112,96},{1... | collective-permute-start | bytes 786440 | tf_op jit(solution)/shard_map/ppermute | solution.py:29
  22.6 0.7 %copy-start.2 = (s32[1,1,2]{2,1,0:T(1,128)S(1)}, s32[1,1,2]{2,1,0:T(1,128)}, u32[]{:S(2)}) copy-start(s32[1,1,2]{2,1,0:T(1,128)} %corner_ref.1) | copy-start | bytes 28
  31.7 12.4 %collective-permute-start.9 = (f32[34,16,128]{2,1,0:T(8,128)S(1)}, f32[34,16,128]{2,1,0:T(8,128)S(1)}, u32[]{:S(2)}, u32[]{:S(2)}) collective-permute-start(f32[34,16,128]{2,1,0:T(8,128)S(1)} %get-tuple-element.28), channel_id=1, source_target_pairs={{1,2},{2,1},{3,4},{4,3},{5,6},{6,5},{7,8},{8,7},{9,10},{10,9},{11,... | collective-permute-start | bytes 835592 | tf_op jit(solution)/shard_map/ppermute | solution.py:29
  36.6 8.0 %collective-permute-start.10 = (f32[34,16,128]{2,1,0:T(8,128)S(1)}, f32[34,16,128]{2,1,0:T(8,128)S(1)}, u32[]{:S(2)}, u32[]{:S(2)}) collective-permute-start(f32[34,16,128]{2,1,0:T(8,128)S(1)} %get-tuple-element.29), channel_id=1, source_target_pairs={{0,1},{1,0},{2,3},{3,2},{4,5},{5,4},{6,7},{7,6},{8,9},{9,8},{10,11... | collective-permute-start | bytes 835592 | tf_op jit(solution)/shard_map/ppermute | solution.py:29
  36.7 1.6 %collective-permute-start.14 = (f32[32,16,128]{2,1,0:T(8,128)S(1)}, f32[32,16,128]{2,1,0:T(8,128)S(1)}, u32[]{:S(2)}, u32[]{:S(2)}) collective-permute-start(f32[32,16,128]{2,1,0:T(8,128)S(1)} %get-tuple-element.34), channel_id=1, source_target_pairs={{0,16},{16,0},{32,48},{48,32},{64,80},{80,64},{96,112},{112,96},{1... | collective-permute-start | bytes 786440 | tf_op jit(solution)/shard_map/ppermute | solution.py:29
  37.2 4.2 %collective-permute-start.11 = (f32[32,16,128]{2,1,0:T(8,128)S(1)}, f32[32,16,128]{2,1,0:T(8,128)S(1)}, u32[]{:S(2)}, u32[]{:S(2)}) collective-permute-start(f32[32,16,128]{2,1,0:T(8,128)S(1)} %get-tuple-element.30), channel_id=1, source_target_pairs={{0,16},{16,0},{32,48},{48,32},{64,80},{80,64},{96,112},{112,96},{1... | collective-permute-start | bytes 786440 | tf_op jit(solution)/shard_map/ppermute | solution.py:29
  38.4 13.4 %collective-permute-start.15 = (f32[33,16,128]{2,1,0:T(8,128)S(1)}, f32[33,16,128]{2,1,0:T(8,128)S(1)}, u32[]{:S(2)}, u32[]{:S(2)}) collective-permute-start(f32[33,16,128]{2,1,0:T(8,128)S(1)} %merge.1), channel_id=1, source_target_pairs={{1,2},{2,1},{3,4},{4,3},{5,6},{6,5},{7,8},{8,7},{9,10},{10,9},{11,... | collective-permute-start | bytes 811016 | tf_op jit(solution)/shard_map/ppermute | solution.py:29
  40.8 10.9 %collective-permute-start.8 = (f32[32,16,128]{2,1,0:T(8,128)S(1)}, f32[32,16,128]{2,1,0:T(8,128)S(1)}, u32[]{:S(2)}, u32[]{:S(2)}) collective-permute-start(f32[32,16,128]{2,1,0:T(8,128)S(1)} %get-tuple-element.26), channel_id=1, source_target_pairs={{0,16},{16,0},{32,48},{48,32},{64,80},{80,64},{96,112},{112,96},{1... | collective-permute-start | bytes 786440 | tf_op jit(solution)/shard_map/ppermute | solution.py:29
  44.7 15.7 %collective-permute-start.12 = (f32[32,16,128]{2,1,0:T(8,128)S(1)}, f32[32,16,128]{2,1,0:T(8,128)S(1)}, u32[]{:S(2)}, u32[]{:S(2)}) collective-permute-start(f32[32,16,128]{2,1,0:T(8,128)S(1)} %get-tuple-element.32), channel_id=1, source_target_pairs={{16,32},{32,16},{48,64},{64,48},{80,96},{96,80},{112,128},{128,112... | collective-permute-start | bytes 786440 | tf_op jit(solution)/shard_map/ppermute | solution.py:29
  51.7 8.7 %collective-permute-start.13 = (f32[32,16,128]{2,1,0:T(8,128)S(1)}, f32[32,16,128]{2,1,0:T(8,128)S(1)}, u32[]{:S(2)}, u32[]{:S(2)}) collective-permute-start(f32[32,16,128]{2,1,0:T(8,128)S(1)} %get-tuple-element.33), channel_id=1, source_target_pairs={{0,1},{1,0},{2,3},{3,2},{4,5},{5,4},{6,7},{7,6},{8,9},{9,8},{10,11... | collective-permute-start | bytes 786440 | tf_op jit(solution)/shard_map/ppermute | solution.py:29

commit v7 on v6

--- a/solution.py
+++ b/solution.py
@@ -12,7 +12,7 @@
 BLOCK = 16
 APER = 32
 NZ = 128
-ROWS = 8
+ROWS = 4
 EXTRA = 1
 F32 = jnp.float32
 small = pltpu.CompilerParams(vmem_limit_bytes=4 << 20)

time: 61.5 us -> 61.6 us (level)
  no operation moved by 1% of the time
where the time goes in v7:
time: 61.6 us; the launch traced here: 61.4 us
  starting transfers between devices  30.5 us (50%)
  waiting for transfers between devices  22.3 us (36%)
  Pallas kernels  6.06 us (10%)
  other arithmetic  1.07 us (2%)
  between operations  0.78 us (1%)
  local copies, waits for them, and re-layouts  0.66 us (1%)
    ppermute x16, starting transfers between devices, swap(): return lax.ppermute(block, axis, swap_pairs(odd))  30.5 us
    ppermute x16, waiting for transfers between devices, swap(): return lax.ppermute(block, axis, swap_pairs(odd))  22.3 us
    pallas_call x1, Pallas kernels, wave(): pl.pallas_call(wave_kernel, out_shape=(part,) * 3 + (early_part,) * 2 + (...  3.99 us
  transfers between devices with their start and end apart: 16, of which 7 were waited for; matrix products, arithmetic and copies ran while one was open for 0% of the time, Pallas kernels for 2%

profile of v7, /device:TPU:95, one launch (start us, length us, event | category | flops | bytes accessed | tf_op | source)
XLA Modules:
  0.0 61.4 jit_solution(4963571742215362109)
XLA Ops:
  0.6 0.0 copy-start.1
  0.6 0.0 copy-start
  0.7 1.1 %pad_maximum_fusion = f32[2,16,16,128]{3,2,1,0:T(8,128)S(1)} fusion(f32[1,16,16,128]{3,2,1,0:T(8,128)} %bitcast.8, f32[1,16,16,128]{3,2,1,0:T(8,128)} %bitcast.9), kind=kLoop, calls=%fused_computation | loop fusion | flops 65536 | bytes 524288 | tf_op jit(solution)/shard_map/stack | solution.py:359
  1.7 7.5 %collective-permute-start.3 = (f32[32,16,128]{2,1,0:T(8,128)S(1)}, f32[32,16,128]{2,1,0:T(8,128)S(1)}, u32[]{:S(2)}, u32[]{:S(2)}) collective-permute-start(f32[32,16,128]{2,1,0:T(8,128)S(1)} %bitcast.3), channel_id=1, source_target_pairs={{16,32},{32,16},{48,64},{64,48},{80,96},{96,80},{112,128},{128,112... | collective-permute-start | bytes 786440 | tf_op jit(solution)/shard_map/ppermute | solution.py:29
  9.2 0.1 collective-permute-start.2
  9.3 0.6 collective-permute-start.1
  9.9 3.1 %collective-permute-start = (f32[32,16,128]{2,1,0:T(8,128)S(1)}, f32[32,16,128]{2,1,0:T(8,128)S(1)}, u32[]{:S(2)}, u32[]{:S(2)}) collective-permute-start(f32[32,16,128]{2,1,0:T(8,128)S(1)} %bitcast.6), channel_id=1, source_target_pairs={{1,2},{2,1},{3,4},{4,3},{5,6},{6,5},{7,8},{8,7},{9,10},{10,9},{11,... | collective-permute-start | bytes 786440 | tf_op jit(solution)/shard_map/ppermute | solution.py:29
  13.0 4.5 %collective-permute-done.3.x_ref = f32[32,16,128]{2,1,0:T(8,128)S(1)} collective-permute-done((f32[32,16,128]{2,1,0:T(8,128)S(1)}, f32[32,16,128]{2,1,0:T(8,128)S(1)}, u32[]{:S(2)}, u32[]{:S(2)}) %collective-permute-start.3) | collective-permute-done | bytes 262176 | tf_op jit(solution)/shard_map/ppermute | solution.py:29
  17.6 0.0 collective-permute-done.2.c_ref
  17.6 1.9 %collective-permute-start.5 = (f32[32,16,128]{2,1,0:T(8,128)S(1)}, f32[32,16,128]{2,1,0:T(8,128)S(1)}, u32[]{:S(2)}, u32[]{:S(2)}) collective-permute-start(f32[32,16,128]{2,1,0:T(8,128)S(1)} %onward.1), channel_id=1, source_target_pairs={{1,2},{2,1},{3,4},{4,3},{5,6},{6,5},{7,8},{8,7},{9,10},{10,9},{11,... | collective-permute-start | bytes 786440 | tf_op jit(solution)/shard_map/ppermute | solution.py:29
  19.5 0.5 collective-permute-start.4
  20.0 0.0 collective-permute-done.1.ye_ref
  20.0 0.0 collective-permute-start.6
  20.0 1.6 %collective-permute-done.yo_ref = f32[32,16,128]{2,1,0:T(8,128)S(1)} collective-permute-done((f32[32,16,128]{2,1,0:T(8,128)S(1)}, f32[32,16,128]{2,1,0:T(8,128)S(1)}, u32[]{:S(2)}, u32[]{:S(2)}) %collective-permute-start) | collective-permute-done | bytes 262176 | tf_op jit(solution)/shard_map/ppermute | solution.py:29
  21.6 1.0 %collective-permute-start.7 = (f32[32,16,128]{2,1,0:T(8,128)S(1)}, f32[32,16,128]{2,1,0:T(8,128)S(1)}, u32[]{:S(2)}, u32[]{:S(2)}) collective-permute-start(f32[32,16,128]{2,1,0:T(8,128)S(1)} %collective-permute-done.yo_ref), channel_id=1, source_target_pairs={{0,16},{16,0},{32,48},{48,32},{64,80},{80,64},{96,112},{112,96},{1... | collective-permute-start | bytes 786440 | tf_op jit(solution)/shard_map/ppermute | solution.py:29
  22.6 0.0 copy-done.1
  22.6 0.0 copy-done
  22.6 0.0 copy-start.2
  22.6 0.7 %copy-done.2 = s32[1,1,2]{2,1,0:T(1,128)S(1)} copy-done((s32[1,1,2]{2,1,0:T(1,128)S(1)}, s32[1,1,2]{2,1,0:T(1,128)}, u32[]{:S(2)}) %copy-start.2) | copy-done | bytes 32
  23.3 1.2 %early.1 = (f32[40,32,128]{2,1,0:T(8,128)S(1)}, f32[3,32,32,128]{3,2,1,0:T(8,128)S(1)}, bf16[2,128,128]{2,1,0:T(8,128)(2,1)S(1)}, bf16[2,256,128]{2,1,0:T(8,128)...) custom-call(s32[1,1,2]{2,1,0:T(1,128)S(1)} %copy-done.2, f32[32,32,128]{2,1,0:T(8,128)S(1)} %copy-done, ...), custom_call_target="tpu_custom_call" | custom-call | tf_op jit(solution)/shard_map/early/pallas_call | solution.py:112
  24.5 3.1 %collective-permute-done.5.yo2_ref = f32[32,16,128]{2,1,0:T(8,128)S(1)} collective-permute-done((f32[32,16,128]{2,1,0:T(8,128)S(1)}, f32[32,16,128]{2,1,0:T(8,128)S(1)}, u32[]{:S(2)}, u32[]{:S(2)}) %collective-permute-start.5) | collective-permute-done | bytes 262176 | tf_op jit(solution)/shard_map/ppermute | solution.py:29
  27.5 0.0 collective-permute-done.4.ye2_ref
  27.5 0.0 collective-permute-done.6.cye_ref
  27.5 0.0 collective-permute-done.7.cyo_ref
  27.5 4.0 %wave.1 = (f32[32,16,128]{2,1,0:T(8,128)S(1)}, f32[32,16,128]{2,1,0:T(8,128)S(1)}, f32[32,16,128]{2,1,0:T(8,128)S(1)}, f32[34,16,128]{2,1,0:T(8,128)S(1)}, f32[3...) custom-call(f32[40,32,128]{2,1,0:T(8,128)S(1)} %get-tuple-element.19, ...), custom_call_target="tpu_custom_call" | custom-call | tf_op jit(solution)/shard_map/wave/pallas_call | solution.py:267
  31.5 5.2 %collective-permute-start.9 = (f32[34,16,128]{2,1,0:T(8,128)S(1)}, f32[34,16,128]{2,1,0:T(8,128)S(1)}, u32[]{:S(2)}, u32[]{:S(2)}) collective-permute-start(f32[34,16,128]{2,1,0:T(8,128)S(1)} %get-tuple-element.28), channel_id=1, source_target_pairs={{1,2},{2,1},{3,4},{4,3},{5,6},{6,5},{7,8},{8,7},{9,10},{10,9},{11,... | collective-permute-start | bytes 835592 | tf_op jit(solution)/shard_map/ppermute | solution.py:29
  36.7 0.1 collective-permute-start.10
  36.8 0.4 collective-permute-start.14
  37.3 0.2 collective-permute-start.11
  37.4 1.0 %collective-permute-done.14.c_ref = f32[32,16,128]{2,1,0:T(8,128)S(1)} collective-permute-done((f32[32,16,128]{2,1,0:T(8,128)S(1)}, f32[32,16,128]{2,1,0:T(8,128)S(1)}, u32[]{:S(2)}, u32[]{:S(2)}) %collective-permute-start.14) | collective-permute-done | bytes 262176 | tf_op jit(solution)/shard_map/ppermute | solution.py:29
  38.5 2.2 %collective-permute-start.15 = (f32[33,16,128]{2,1,0:T(8,128)S(1)}, f32[33,16,128]{2,1,0:T(8,128)S(1)}, u32[]{:S(2)}, u32[]{:S(2)}) collective-permute-start(f32[33,16,128]{2,1,0:T(8,128)S(1)} %merge.1), channel_id=1, source_target_pairs={{1,2},{2,1},{3,4},{4,3},{5,6},{6,5},{7,8},{8,7},{9,10},{10,9},{11,... | collective-permute-start | bytes 811016 | tf_op jit(solution)/shard_map/ppermute | solution.py:29
  40.8 0.7 %collective-permute-start.8 = (f32[32,16,128]{2,1,0:T(8,128)S(1)}, f32[32,16,128]{2,1,0:T(8,128)S(1)}, u32[]{:S(2)}, u32[]{:S(2)}) collective-permute-start(f32[32,16,128]{2,1,0:T(8,128)S(1)} %get-tuple-element.26), channel_id=1, source_target_pairs={{0,16},{16,0},{32,48},{48,32},{64,80},{80,64},{96,112},{112,96},{1... | collective-permute-start | bytes 786440 | tf_op jit(solution)/shard_map/ppermute | solution.py:29
  41.5 0.0 collective-permute-done.11.c_ref
  41.5 2.2 %collective-permute-done.9.o_ref = f32[34,16,128]{2,1,0:T(8,128)S(1)} collective-permute-done((f32[34,16,128]{2,1,0:T(8,128)S(1)}, f32[34,16,128]{2,1,0:T(8,128)S(1)}, u32[]{:S(2)}, u32[]{:S(2)}) %collective-permute-start.9) | collective-permute-done | bytes 278560 | tf_op jit(solution)/shard_map/ppermute | solution.py:29
  43.7 1.1 %collective-permute-done.10.e_ref = f32[34,16,128]{2,1,0:T(8,128)S(1)} collective-permute-done((f32[34,16,128]{2,1,0:T(8,128)S(1)}, f32[34,16,128]{2,1,0:T(8,128)S(1)}, u32[]{:S(2)}, u32[]{:S(2)}) %collective-permute-start.10) | collective-permute-done | bytes 278560 | tf_op jit(solution)/shard_map/ppermute | solution.py:29
  44.7 0.1 combine.1
  44.8 6.8 %collective-permute-start.12 = (f32[32,16,128]{2,1,0:T(8,128)S(1)}, f32[32,16,128]{2,1,0:T(8,128)S(1)}, u32[]{:S(2)}, u32[]{:S(2)}) collective-permute-start(f32[32,16,128]{2,1,0:T(8,128)S(1)} %get-tuple-element.32), channel_id=1, source_target_pairs={{16,32},{32,16},{48,64},{64,48},{80,96},{96,80},{112,128},{128,112... | collective-permute-start | bytes 786440 | tf_op jit(solution)/shard_map/ppermute | solution.py:29
  51.6 0.1 collective-permute-start.13
  51.7 0.0 collective-permute-done.8.c_ref
  51.7 0.0 collective-permute-done.15.o_ref
  51.7 8.9 %collective-permute-done.12.x_ref = f32[32,16,128]{2,1,0:T(8,128)S(1)} collective-permute-done((f32[32,16,128]{2,1,0:T(8,128)S(1)}, f32[32,16,128]{2,1,0:T(8,128)S(1)}, u32[]{:S(2)}, u32[]{:S(2)}) %collective-permute-start.12) | collective-permute-done | bytes 262176 | tf_op jit(solution)/shard_map/ppermute | solution.py:29
  60.6 0.0 collective-permute-done.13.e_ref
  60.6 0.8 %total.1 = (f32[16,16,128]{2,1,0:T(8,128)}, f32[16,16,128]{2,1,0:T(8,128)}) custom-call(f32[32,16,128]{2,1,0:T(8,128)S(1)} %get-tuple-element.25.own_ref, f32[32,16,128]{2,1,0:T(8,128)S(1)} %collective-permute-done.8.c_ref, f32[32,16,128]{2,1,0:T(8,128)S(1)} %collective-permute-done.12.x_ref, f32[32,16,128]{2,1,0:T(8,128)S(1)} %collective-permute-done.13.e_ref, ...), custom_call_target="tpu_custom_call" | custom-call | tf_op jit(solution)/shard_map/total/pallas_call | solution.py:347
  (2 shorter events, 0.0 us)
Async XLA Ops:
  0.6 22.0 %copy-start.1 = (f32[32,32,128]{2,1,0:T(8,128)S(1)}, f32[32,32,128]{2,1,0:T(8,128)}, u32[]{:S(2)}) copy-start(f32[32,32,128]{2,1,0:T(8,128)} %obs_ref.1) | copy-start | bytes 1572868
  0.6 22.0 %copy-start = (f32[32,32,128]{2,1,0:T(8,128)S(1)}, f32[32,32,128]{2,1,0:T(8,128)}, u32[]{:S(2)}) copy-start(f32[32,32,128]{2,1,0:T(8,128)} %p0_ref.1) | copy-start | bytes 1572868
  1.7 15.8 %collective-permute-start.3 = (f32[32,16,128]{2,1,0:T(8,128)S(1)}, f32[32,16,128]{2,1,0:T(8,128)S(1)}, u32[]{:S(2)}, u32[]{:S(2)}) collective-permute-start(f32[32,16,128]{2,1,0:T(8,128)S(1)} %bitcast.3), channel_id=1, source_target_pairs={{16,32},{32,16},{48,64},{64,48},{80,96},{96,80},{112,128},{128,112... | collective-permute-start | bytes 786440 | tf_op jit(solution)/shard_map/ppermute | solution.py:29
  9.2 8.3 %collective-permute-start.2 = (f32[32,16,128]{2,1,0:T(8,128)S(1)}, f32[32,16,128]{2,1,0:T(8,128)S(1)}, u32[]{:S(2)}, u32[]{:S(2)}) collective-permute-start(f32[32,16,128]{2,1,0:T(8,128)S(1)} %bitcast.4), channel_id=1, source_target_pairs={{0,16},{16,0},{32,48},{48,32},{64,80},{80,64},{96,112},{112,96},{1... | collective-permute-start | bytes 786440 | tf_op jit(solution)/shard_map/ppermute | solution.py:29
  9.3 10.7 %collective-permute-start.1 = (f32[32,16,128]{2,1,0:T(8,128)S(1)}, f32[32,16,128]{2,1,0:T(8,128)S(1)}, u32[]{:S(2)}, u32[]{:S(2)}) collective-permute-start(f32[32,16,128]{2,1,0:T(8,128)S(1)} %bitcast.5), channel_id=1, source_target_pairs={{0,1},{1,0},{2,3},{3,2},{4,5},{5,4},{6,7},{7,6},{8,9},{9,8},{10,11... | collective-permute-start | bytes 786440 | tf_op jit(solution)/shard_map/ppermute | solution.py:29
  9.9 11.7 %collective-permute-start = (f32[32,16,128]{2,1,0:T(8,128)S(1)}, f32[32,16,128]{2,1,0:T(8,128)S(1)}, u32[]{:S(2)}, u32[]{:S(2)}) collective-permute-start(f32[32,16,128]{2,1,0:T(8,128)S(1)} %bitcast.6), channel_id=1, source_target_pairs={{1,2},{2,1},{3,4},{4,3},{5,6},{6,5},{7,8},{8,7},{9,10},{10,9},{11,... | collective-permute-start | bytes 786440 | tf_op jit(solution)/shard_map/ppermute | solution.py:29
  17.6 9.9 %collective-permute-start.5 = (f32[32,16,128]{2,1,0:T(8,128)S(1)}, f32[32,16,128]{2,1,0:T(8,128)S(1)}, u32[]{:S(2)}, u32[]{:S(2)}) collective-permute-start(f32[32,16,128]{2,1,0:T(8,128)S(1)} %onward.1), channel_id=1, source_target_pairs={{1,2},{2,1},{3,4},{4,3},{5,6},{6,5},{7,8},{8,7},{9,10},{10,9},{11,... | collective-permute-start | bytes 786440 | tf_op jit(solution)/shard_map/ppermute | solution.py:29
  19.5 8.0 %collective-permute-start.4 = (f32[32,16,128]{2,1,0:T(8,128)S(1)}, f32[32,16,128]{2,1,0:T(8,128)S(1)}, u32[]{:S(2)}, u32[]{:S(2)}) collective-permute-start(f32[32,16,128]{2,1,0:T(8,128)S(1)} %onward.1), channel_id=1, source_target_pairs={{0,1},{1,0},{2,3},{3,2},{4,5},{5,4},{6,7},{7,6},{8,9},{9,8},{10,11... | collective-permute-start | bytes 786440 | tf_op jit(solution)/shard_map/ppermute | solution.py:29
  20.0 7.5 %collective-permute-start.6 = (f32[32,16,128]{2,1,0:T(8,128)S(1)}, f32[32,16,128]{2,1,0:T(8,128)S(1)}, u32[]{:S(2)}, u32[]{:S(2)}) collective-permute-start(f32[32,16,128]{2,1,0:T(8,128)S(1)} %collective-permute-done.1.ye_ref), channel_id=1, source_target_pairs={{0,16},{16,0},{32,48},{48,32},{64,80},{80,64},{96,112},{112,96},{1... | collective-permute-start | bytes 786440 | tf_op jit(solution)/shard_map/ppermute | solution.py:29
  21.6 6.0 %collective-permute-start.7 = (f32[32,16,128]{2,1,0:T(8,128)S(1)}, f32[32,16,128]{2,1,0:T(8,128)S(1)}, u32[]{:S(2)}, u32[]{:S(2)}) collective-permute-start(f32[32,16,128]{2,1,0:T(8,128)S(1)} %collective-permute-done.yo_ref), channel_id=1, source_target_pairs={{0,16},{16,0},{32,48},{48,32},{64,80},{80,64},{96,112},{112,96},{1... | collective-permute-start | bytes 786440 | tf_op jit(solution)/shard_map/ppermute | solution.py:29
  22.6 0.7 %copy-start.2 = (s32[1,1,2]{2,1,0:T(1,128)S(1)}, s32[1,1,2]{2,1,0:T(1,128)}, u32[]{:S(2)}) copy-start(s32[1,1,2]{2,1,0:T(1,128)} %corner_ref.1) | copy-start | bytes 28
  31.5 12.1 %collective-permute-start.9 = (f32[34,16,128]{2,1,0:T(8,128)S(1)}, f32[34,16,128]{2,1,0:T(8,128)S(1)}, u32[]{:S(2)}, u32[]{:S(2)}) collective-permute-start(f32[34,16,128]{2,1,0:T(8,128)S(1)} %get-tuple-element.28), channel_id=1, source_target_pairs={{1,2},{2,1},{3,4},{4,3},{5,6},{6,5},{7,8},{8,7},{9,10},{10,9},{11,... | collective-permute-start | bytes 835592 | tf_op jit(solution)/shard_map/ppermute | solution.py:29
  36.7 8.0 %collective-permute-start.10 = (f32[34,16,128]{2,1,0:T(8,128)S(1)}, f32[34,16,128]{2,1,0:T(8,128)S(1)}, u32[]{:S(2)}, u32[]{:S(2)}) collective-permute-start(f32[34,16,128]{2,1,0:T(8,128)S(1)} %get-tuple-element.29), channel_id=1, source_target_pairs={{0,1},{1,0},{2,3},{3,2},{4,5},{5,4},{6,7},{7,6},{8,9},{9,8},{10,11... | collective-permute-start | bytes 835592 | tf_op jit(solution)/shard_map/ppermute | solution.py:29
  36.8 1.6 %collective-permute-start.14 = (f32[32,16,128]{2,1,0:T(8,128)S(1)}, f32[32,16,128]{2,1,0:T(8,128)S(1)}, u32[]{:S(2)}, u32[]{:S(2)}) collective-permute-start(f32[32,16,128]{2,1,0:T(8,128)S(1)} %get-tuple-element.34), channel_id=1, source_target_pairs={{0,16},{16,0},{32,48},{48,32},{64,80},{80,64},{96,112},{112,96},{1... | collective-permute-start | bytes 786440 | tf_op jit(solution)/shard_map/ppermute | solution.py:29
  37.3 4.2 %collective-permute-start.11 = (f32[32,16,128]{2,1,0:T(8,128)S(1)}, f32[32,16,128]{2,1,0:T(8,128)S(1)}, u32[]{:S(2)}, u32[]{:S(2)}) collective-permute-start(f32[32,16,128]{2,1,0:T(8,128)S(1)} %get-tuple-element.30), channel_id=1, source_target_pairs={{0,16},{16,0},{32,48},{48,32},{64,80},{80,64},{96,112},{112,96},{1... | collective-permute-start | bytes 786440 | tf_op jit(solution)/shard_map/ppermute | solution.py:29
  38.5 13.2 %collective-permute-start.15 = (f32[33,16,128]{2,1,0:T(8,128)S(1)}, f32[33,16,128]{2,1,0:T(8,128)S(1)}, u32[]{:S(2)}, u32[]{:S(2)}) collective-permute-start(f32[33,16,128]{2,1,0:T(8,128)S(1)} %merge.1), channel_id=1, source_target_pairs={{1,2},{2,1},{3,4},{4,3},{5,6},{6,5},{7,8},{8,7},{9,10},{10,9},{11,... | collective-permute-start | bytes 811016 | tf_op jit(solution)/shard_map/ppermute | solution.py:29
  40.8 11.0 %collective-permute-start.8 = (f32[32,16,128]{2,1,0:T(8,128)S(1)}, f32[32,16,128]{2,1,0:T(8,128)S(1)}, u32[]{:S(2)}, u32[]{:S(2)}) collective-permute-start(f32[32,16,128]{2,1,0:T(8,128)S(1)} %get-tuple-element.26), channel_id=1, source_target_pairs={{0,16},{16,0},{32,48},{48,32},{64,80},{80,64},{96,112},{112,96},{1... | collective-permute-start | bytes 786440 | tf_op jit(solution)/shard_map/ppermute | solution.py:29
  44.8 15.8 %collective-permute-start.12 = (f32[32,16,128]{2,1,0:T(8,128)S(1)}, f32[32,16,128]{2,1,0:T(8,128)S(1)}, u32[]{:S(2)}, u32[]{:S(2)}) collective-permute-start(f32[32,16,128]{2,1,0:T(8,128)S(1)} %get-tuple-element.32), channel_id=1, source_target_pairs={{16,32},{32,16},{48,64},{64,48},{80,96},{96,80},{112,128},{128,112... | collective-permute-start | bytes 786440 | tf_op jit(solution)/shard_map/ppermute | solution.py:29
  51.6 9.0 %collective-permute-start.13 = (f32[32,16,128]{2,1,0:T(8,128)S(1)}, f32[32,16,128]{2,1,0:T(8,128)S(1)}, u32[]{:S(2)}, u32[]{:S(2)}) collective-permute-start(f32[32,16,128]{2,1,0:T(8,128)S(1)} %get-tuple-element.33), channel_id=1, source_target_pairs={{0,1},{1,0},{2,3},{3,2},{4,5},{5,4},{6,7},{7,6},{8,9},{9,8},{10,11... | collective-permute-start | bytes 786440 | tf_op jit(solution)/shard_map/ppermute | solution.py:29
